TPU v7x, 128 devices: a whole 4x4x4 slice. The times are simulated.
128 devices in a mesh: dom: 64 (over z_lo, x, y, core), head: 2 (over z_hi).
Axes of the slice: x: 4, y: 4, z: 4 (z_hi: 2, z_lo: 2; z = z_hi * 2 + z_lo), core: 2. Of those that a mesh axis runs over, the one named last changes fastest.
Arguments:
- node_feats: bfloat16 [131072, 512], P(('dom', 'head')), may hold values from -16 to 16
- w_qkv: bfloat16 [512, 1536], replicated, may hold values from -1 to 1
- w_out: bfloat16 [512, 512], replicated, may hold values from -2 to 2
- neighbours: int32 [1024, 4], P('dom'), may hold values from 0 to 15
- tiles: int32 [1024, 4, 128, 128], P('dom'), may hold values 0 or 1
- partner: int32 [1024], P('dom'), may hold values from 0 to 1023, as said below
- layer_cot: bfloat16 [131072, 512], P(('dom', 'head')), may hold values from -6 to 6
Outputs:
- layer_out: bfloat16 [131072, 512], P(('dom', 'head'))
- feat_grad: bfloat16 [131072, 512], P(('dom', 'head'))
- dw_qkv: float32 [512, 1536], P('dom', 'head')
- dw_out: float32 [512, 512], P('head', 'dom')
Inputs may be any that keep to these rules, and one draw needn't show every extreme that they name: partner is a perfect matching of the 1024 node blocks: partner[partner[b]] = b, and the partner of a block lies in another part (part = block // 16). For every two parts, at most 1 block of one are matched to blocks of the other, and some two parts have exactly 1 such pairs.
All inputs are finite; a program needn't handle non-finite values. No bound on the sum of `tiles` on one device may be relied on, other than what follows from the above.
Results may differ from a plain program's by a relative error of at most 0.019.
The roundings to bfloat16 on the way count: a program that leaves them out, or rounds other values in their place, can miss the bound.
Values may be sent and summed in bfloat16 or wider, within the bound.
No kernel may reach another device: no remote copies, remote signals or barrier semaphores. Data moves between devices by JAX's collectives and lax.ppermute only.
A program may use at most 192 MiB of HBM per device.

v0:
```python
import jax
import jax.numpy as jnp
from jax import lax
from jax.sharding import PartitionSpec as P

H = 8
NBR = 4
GB = 4


def body(node_feats, w_qkv, w_out, neighbours, tiles, partner, layer_cot):
    rows, width = node_feats.shape
    groups = lax.axis_size("head")
    parts = lax.axis_size("dom")
    blocks = partner.shape[0]
    block_size = tiles.shape[2]
    head_dim = width // H
    group_heads = H // groups
    span = group_heads * head_dim
    slots = (blocks + parts - 2) // (parts - 1)
    scale = head_dim ** (-0.5)
    part_rows = blocks * block_size
    qkv_node = jnp.dot(node_feats, w_qkv, preferred_element_type=jnp.float32).astype(jnp.bfloat16)
    qkv_part = lax.all_to_all(
        qkv_node.reshape(rows, groups, 3 * span), "head", split_axis=1, concat_axis=0, tiled=True
    )
    qkv_part = qkv_part.reshape(part_rows, 3 * span)
    query_all = qkv_part[:, :span].reshape(blocks, block_size, span)
    kv_all = qkv_part[:, span:].reshape(blocks, block_size, 2 * span)
    target = partner // blocks
    block_iota = jnp.arange(blocks, dtype=jnp.int32)
    same_target = target[:, None] == target[None, :]
    earlier = block_iota[None, :] < block_iota[:, None]
    lower = partner[None, :] < partner[:, None]
    send_slot = target * slots + jnp.sum((same_target & earlier).astype(jnp.int32), axis=1)
    recv_slot = target * slots + jnp.sum((same_target & lower).astype(jnp.int32), axis=1)
    outgoing = (
        jnp.zeros((parts * slots, block_size, 2 * span), jnp.bfloat16).at[send_slot].set(kv_all)
    )
    incoming = lax.all_to_all(outgoing, "dom", split_axis=0, concat_axis=0, tiled=True)
    kv_partner = incoming[recv_slot]

    def key_sets(start):
        ids = lax.dynamic_slice_in_dim(neighbours, start, GB, 0)
        near_kv = kv_all[ids].reshape(GB, NBR * block_size, 2 * span)
        far_kv = lax.dynamic_slice_in_dim(kv_partner, start, GB, 0)
        joined = jnp.concatenate([near_kv, far_kv], axis=1)
        key_four = joined[..., :span].reshape(GB, (NBR + 1) * block_size, group_heads, head_dim)
        value_four = joined[..., span:].reshape(GB, (NBR + 1) * block_size, group_heads, head_dim)
        tile_block = lax.dynamic_slice_in_dim(tiles, start, GB, 0)
        visible = jnp.concatenate(
            [
                tile_block.transpose(0, 2, 1, 3).reshape(GB, block_size, NBR * block_size) != 0,
                jnp.ones((GB, block_size, block_size), dtype=jnp.bool_),
            ],
            axis=2,
        )
        query_four = lax.dynamic_slice_in_dim(query_all, start, GB, 0).reshape(
            GB, block_size, group_heads, head_dim
        )
        scores = (
            jnp.einsum("bqhd,bkhd->bhqk", query_four, key_four, preferred_element_type=jnp.float32)
            * scale
        )
        scores = jnp.where(visible[:, None], scores, -1e30)
        return (ids, query_four, key_four, value_four, scores)

    def forward_step(start):
        ids, query_four, key_four, value_four, scores = key_sets(start)
        peak = jnp.max(scores, axis=-1)
        total = jnp.sum(jnp.exp(scores - peak[..., None]), axis=-1)
        probs_low = (jnp.exp(scores - peak[..., None]) / total[..., None]).astype(jnp.bfloat16)
        attended = jnp.einsum(
            "bhqk,bkhd->bqhd", probs_low, value_four, preferred_element_type=jnp.float32
        )
        return (attended.astype(jnp.bfloat16).reshape(GB, block_size, span), peak, total)

    starts = jnp.arange(0, blocks, GB, dtype=jnp.int32)
    attended_all, peak_all, total_all = lax.map(forward_step, starts)
    attended_all = attended_all.reshape(blocks, block_size, span)
    peak_all = peak_all.reshape(blocks, group_heads, block_size)
    total_all = total_all.reshape(blocks, group_heads, block_size)
    attended_part = attended_all.reshape(part_rows, span)
    attended_node = lax.all_to_all(attended_part, "head", split_axis=0, concat_axis=1, tiled=True)
    layer_out = jnp.dot(attended_node, w_out, preferred_element_type=jnp.float32).astype(
        jnp.bfloat16
    )
    cot_node = jnp.dot(layer_cot, w_out.T, preferred_element_type=jnp.float32).astype(jnp.bfloat16)
    cot_part = lax.all_to_all(cot_node, "head", split_axis=1, concat_axis=0, tiled=True)
    cot_all = cot_part.reshape(blocks, block_size, span)
    delta_all = jnp.sum(
        (cot_all.astype(jnp.float32) * attended_all.astype(jnp.float32)).reshape(
            blocks, block_size, group_heads, head_dim
        ),
        axis=-1,
    ).transpose(0, 2, 1)
    reach = (NBR + 1) * block_size

    def backward_step(accum, start):
        ids, query_four, key_four, value_four, scores = key_sets(start)
        peak = lax.dynamic_slice_in_dim(peak_all, start, GB, 0)
        total = lax.dynamic_slice_in_dim(total_all, start, GB, 0)
        delta = lax.dynamic_slice_in_dim(delta_all, start, GB, 0)
        probs = jnp.exp(scores - peak[..., None]) / total[..., None]
        probs_low = probs.astype(jnp.bfloat16)
        grad_four = lax.dynamic_slice_in_dim(cot_all, start, GB, 0).reshape(
            GB, block_size, group_heads, head_dim
        )
        grad_probs = jnp.einsum(
            "bqhd,bkhd->bhqk", grad_four, value_four, preferred_element_type=jnp.float32
        )
        grad_scores = (probs * (grad_probs - delta[..., None]) * scale).astype(jnp.bfloat16)
        grad_query = jnp.einsum(
            "bhqk,bkhd->bqhd", grad_scores, key_four, preferred_element_type=jnp.float32
        )
        grad_keys = jnp.einsum(
            "bhqk,bqhd->bkhd", grad_scores, query_four, preferred_element_type=jnp.float32
        )
        grad_values = jnp.einsum(
            "bhqk,bqhd->bkhd", probs_low, grad_four, preferred_element_type=jnp.float32
        )
        joined_grad = jnp.concatenate(
            [grad_keys.reshape(GB, reach, span), grad_values.reshape(GB, reach, span)], axis=-1
        )
        near_grad = joined_grad[:, : NBR * block_size].reshape(GB * NBR, block_size, 2 * span)
        one_hot = (ids.reshape(-1)[:, None] == block_iota[None, :]).astype(jnp.float32)
        accum = accum + jnp.einsum(
            "jb,jrc->brc", one_hot, near_grad, precision=lax.Precision.HIGHEST
        )
        query_flat = grad_query.reshape(GB, block_size, span)
        outputs = (query_flat, joined_grad[:, NBR * block_size :].astype(jnp.bfloat16))
        return (accum, outputs)

    zero_accum = jnp.zeros((blocks, block_size, 2 * span), jnp.float32)
    accum, outputs = lax.scan(backward_step, zero_accum, starts)
    grad_query_all = outputs[0].reshape(blocks, block_size, span)
    far_all = outputs[1].reshape(blocks, block_size, 2 * span)
    buffer = (
        jnp.zeros((parts * slots, block_size, 2 * span), jnp.bfloat16).at[recv_slot].set(far_all)
    )
    returned = lax.all_to_all(buffer, "dom", split_axis=0, concat_axis=0, tiled=True)
    accum = accum + returned[send_slot].astype(jnp.float32)
    dqkv_part = (
        jnp.concatenate([grad_query_all, accum], axis=-1)
        .reshape(part_rows, 3 * span)
        .astype(jnp.bfloat16)
    )
    dqkv_node = lax.all_to_all(dqkv_part, "head", split_axis=0, concat_axis=1, tiled=True)
    feat_grad = jnp.dot(dqkv_node, w_qkv.T, preferred_element_type=jnp.float32).astype(jnp.bfloat16)
    full_qkv = jnp.einsum("rd,rc->dc", node_feats, dqkv_node, preferred_element_type=jnp.float32)
    full_out = jnp.einsum("rd,rc->dc", attended_node, layer_cot, preferred_element_type=jnp.float32)
    grad_qkv, grad_out = (
        lax.psum_scatter(
            full_qkv.astype(jnp.bfloat16), "head", scatter_dimension=1, tiled=True
        ).astype(jnp.float32),
        lax.psum_scatter(
            full_out.astype(jnp.bfloat16), "head", scatter_dimension=0, tiled=True
        ).astype(jnp.float32),
    )
    dw_qkv, dw_out = (
        lax.psum_scatter(grad_qkv, "dom", scatter_dimension=0, tiled=True),
        lax.psum_scatter(grad_out, "dom", scatter_dimension=1, tiled=True),
    )
    return (layer_out, feat_grad, dw_qkv, dw_out)


def solution(mesh):
    placed = (
        P(("dom", "head"), None),
        P(),
        P(),
        P("dom", None),
        P("dom", None, None, None),
        P("dom"),
        P(("dom", "head"), None),
    )
    return jax.shard_map(
        body,
        mesh=mesh,
        in_specs=placed,
        out_specs=(
            P(("dom", "head"), None),
            P(("dom", "head"), None),
            P("dom", "head"),
            P("head", "dom"),
        ),
        check_vma=False,
    )
```

profile of v0, /device:TPU:0, one launch (start us, length us, event | category | flops | bytes accessed | tf_op | source)
XLA Modules:
  0.0 1383.8 jit_solution(1048007028215436780)
XLA Ops:
  13.4 5.4 all-to-all-start
  22.1 35.3 %all-to-all-done = bf16[1024,2,768]{2,0,1:T(8,128)(2,1)} async-done(((bf16[1024,2,768]{2,0,1:T(8,128)(2,1)}), bf16[1024,2,768]{2,0,1:T(8,128)(2,1)}, u32[]{:S(2)}, u32[]{:S(2)}) %all-to-all-start) | async-done | bytes 3145760 | tf_op jit(solution)/shard_map/all_to_all | solution.py:24
  64.4 4.2 broadcast.76.clone
  68.7 6.0 scatter_fusion
  75.8 8.8 all-to-all-start.1
  84.7 6.9 copy.78
  104.0 86.9 %all-to-all-done.1 = bf16[64,128,512]{2,1,0:T(8,128)(2,1)} async-done(((bf16[64,128,512]{2,1,0:T(8,128)(2,1)}), bf16[64,128,512]{2,1,0:T(8,128)(2,1)}, u32[]{:S(2)}, u32[]{:S(2)}) %all-to-all-start.1) | async-done | bytes 8388640 | tf_op jit(solution)/shard_map/all_to_all | solution.py:40
  190.9 5.5 gather_fusion.2
  200.3 89.3 %while.29 = (s32[]{:T(128)}, bf16[4,4,128,256]{2,3,1,0:T(8,128)(2,1)}, f32[4,4,4,128]{3,2,1,0:T(4,128)S(1)}, f32[4,4,4,128]{3,2,1,0:T(4,128)S(1)}, s32[4]{0:T(12...) while((s32[]{:T(128)}, ...), condition=%wide.region_6.7_spmd, body=%wide.region_3.6_spmd.sunk | while | flops 356906048 | bytes 43332708 | solution.py:79
  292.1 239.7 %while.30 = (s32[]{:T(128)}, f32[16,128,512]{2,0,1:T(8,128)}, bf16[4,4,128,256]{3,2,1,0:T(8,128)(2,1)}, bf16[4,4,128,512]{3,2,1,0:T(8,128)(2,1)}, s32[4]{0:T(128...) while((s32[]{:T(128)}, f32[16,128,512]{2,0,1:T(8,128)}, ...), condition=%wide.region_9.10_spmd.clone, body=%wide.region_8.9_spmd.clone.sunk | while | flops 1061684544 | bytes 134445024 | solution.py:135
  327.0 4.6 fusion.99
  340.5 8.8 select_add_fusion.2
  385.9 4.6 fusion.99
  399.4 10.0 select_add_fusion.2
  446.1 4.6 fusion.99
  459.5 10.0 select_add_fusion.2
  506.3 4.6 fusion.99
  519.7 10.0 select_add_fusion.2
  531.8 4.2 broadcast.76
  536.0 6.0 scatter_fusion.1
  542.0 30.9 %all-to-all-start.4 = ((bf16[64,128,512]{2,1,0:T(8,128)(2,1)}), bf16[64,128,512]{2,1,0:T(8,128)(2,1)}, u32[]{:S(2)}, u32[]{:S(2)}) async-start(bf16[64,128,512]{2,1,0:T(8,128)(2,1)} %scatter_fusion.1), calls=%async_computation.4 | async-start | bytes 16777216 | tf_op jit(solution)/shard_map/all_to_all | solution.py:141
  574.3 105.1 %all-to-all-done.4 = bf16[64,128,512]{2,1,0:T(8,128)(2,1)} async-done(((bf16[64,128,512]{2,1,0:T(8,128)(2,1)}), bf16[64,128,512]{2,1,0:T(8,128)(2,1)}, u32[]{:S(2)}, u32[]{:S(2)}) %all-to-all-start.4) | async-done | bytes 8388640 | tf_op jit(solution)/shard_map/all_to_all | solution.py:141
  679.4 4.5 all-to-all-start.2
  683.9 5.5 gather_fusion.3
  689.4 5.3 fusion.25
  698.8 5.2 all-to-all-start.5
  708.5 32.1 %all-to-all-done.5 = bf16[2,1024,768]{2,1,0:T(8,128)(2,1)} async-done(((bf16[2,1024,768]{2,1,0:T(8,128)(2,1)}), bf16[2,1024,768]{2,1,0:T(8,128)(2,1)}, u32[]{:S(2)}, u32[]{:S(2)}) %all-to-all-start.5) | async-done | bytes 3145760 | tf_op jit(solution)/shard_map/all_to_all | solution.py:148
  740.6 4.7 copy.93
  745.4 4.9 fusion.26
  754.4 49.7 %reduce-scatter.9.cloned.1.call-done = bf16[512,768]{0,1:T(8,128)(2,1)} async-done(((bf16[512,1536]{0,1:T(8,128)(2,1)}), bf16[512,768]{0,1:T(8,128)(2,1)}) %reduce-scatter.9.cloned.1.call-update) | async-done | bytes 786448 | tf_op jit(solution)/shard_map/reduce_scatter | solution.py:153
  811.8 279.3 %reduce-scatter.15.cloned.1.call-done = f32[8,256]{1,0:T(8,128)} async-done(((f32[512,256]{1,0:T(8,128)}), f32[8,256]{1,0:T(8,128)}) %reduce-scatter.15.cloned.1.call-update) | async-done | bytes 8208
  1091.1 285.7 %reduce-scatter.13.cloned.1.call-done = f32[8,768]{1,0:T(8,128)} async-done(((f32[512,768]{1,0:T(8,128)}), f32[8,768]{1,0:T(8,128)}) %reduce-scatter.13.cloned.1.call-update) | async-done | bytes 24592
  (298 shorter events, 314.3 us)
Async XLA Ops:
  13.4 5.4 copy-start.19
  13.4 44.0 %all-to-all-start = ((bf16[1024,2,768]{2,0,1:T(8,128)(2,1)}), bf16[1024,2,768]{2,0,1:T(8,128)(2,1)}, u32[]{:S(2)}, u32[]{:S(2)}) async-start(bf16[1024,2,768]{2,0,1:T(8,128)(2,1)} %bitcast.182), calls=%async_computation | async-start | bytes 6291456 | tf_op jit(solution)/shard_map/all_to_all | solution.py:24
  20.8 40.2 %copy-start.16 = (s32[16]{0:T(128)S(1)}, s32[16]{0:T(128)}, u32[]{:S(2)}) copy-start(s32[16]{0:T(128)} %param.16) | copy-start | bytes 196
  57.4 18.4 %all-to-all-start.3 = ((bf16[1024,2,256]{2,0,1:T(8,128)(2,1)}), bf16[1024,2,256]{2,0,1:T(8,128)(2,1)S(1)}, u32[]{:S(2)}, u32[]{:S(2)}) async-start(bf16[1024,2,256]{2,0,1:T(8,128)(2,1)} %copy.82), calls=%async_computation.3 | async-start | bytes 2097152 | tf_op jit(solution)/shard_map/all_to_all | solution.py:89
  61.2 7.4 copy-start.12
  61.3 30.5 %copy-start.14 = (s32[16]{0:T(128)}, s32[16]{0:T(128)S(1)}, u32[]{:S(2)}) copy-start(s32[16]{0:T(128)S(1)} %get-tuple-element.364) | copy-start | bytes 196
  75.8 15.9 %copy-start.6 = (bf16[1024,2,256]{2,0,1:T(8,128)(2,1)}, bf16[1024,2,256]{2,0,1:T(8,128)(2,1)S(1)}, u32[]{:S(2)}) copy-start(bf16[1024,2,256]{2,0,1:T(8,128)(2,1)S(1)} %all-to-all-done.3) | copy-start | bytes 3145732
  75.8 115.1 %all-to-all-start.1 = ((bf16[64,128,512]{2,1,0:T(8,128)(2,1)}), bf16[64,128,512]{2,1,0:T(8,128)(2,1)}, u32[]{:S(2)}, u32[]{:S(2)}) async-start(bf16[64,128,512]{2,1,0:T(8,128)(2,1)} %scatter_fusion), calls=%async_computation.1 | async-start | bytes 16777216 | tf_op jit(solution)/shard_map/all_to_all | solution.py:40
  84.7 6.9 copy-start.17
  334.9 3.0 copy-start.4
  340.5 8.8 copy-start.2
  393.8 3.0 copy-start.4
  399.4 10.0 copy-start.2
  440.3 2.4 copy-start.1
  453.9 3.0 copy-start.4
  459.5 10.0 copy-start.2
  514.1 3.0 copy-start.4
  519.7 10.0 copy-start.2
  531.8 4.2 copy-start.15
  542.0 30.9 %copy-start.13 = (s32[16]{0:T(128)S(1)}, s32[16]{0:T(128)}, u32[]{:S(2)}) copy-start(s32[16]{0:T(128)} %copy-done.12) | copy-start | bytes 196
  542.0 31.0 %copy-start.8 = (bf16[4,4,128,256]{2,3,1,0:T(8,128)(2,1)S(1)}, bf16[4,4,128,256]{2,3,1,0:T(8,128)(2,1)}, u32[]{:S(2)}) copy-start(bf16[4,4,128,256]{2,3,1,0:T(8,128)(2,1)} %get-tuple-element.137) | copy-start | bytes 3145732
  542.0 137.4 %all-to-all-start.4 = ((bf16[64,128,512]{2,1,0:T(8,128)(2,1)}), bf16[64,128,512]{2,1,0:T(8,128)(2,1)}, u32[]{:S(2)}, u32[]{:S(2)}) async-start(bf16[64,128,512]{2,1,0:T(8,128)(2,1)} %scatter_fusion.1), calls=%async_computation.4 | async-start | bytes 16777216 | tf_op jit(solution)/shard_map/all_to_all | solution.py:141
  679.4 19.5 %all-to-all-start.2 = ((bf16[2,1024,256]{2,1,0:T(8,128)(2,1)}), bf16[2,1024,256]{2,1,0:T(8,128)(2,1)S(1)}, u32[]{:S(2)}, u32[]{:S(2)}) async-start(bf16[2,1024,256]{2,1,0:T(8,128)(2,1)} %bitcast.188), calls=%async_computation.2 | async-start | bytes 2097152 | tf_op jit(solution)/shard_map/all_to_all | solution.py:84
  689.4 5.3 copy-start.11
  698.8 41.8 %all-to-all-start.5 = ((bf16[2,1024,768]{2,1,0:T(8,128)(2,1)}), bf16[2,1024,768]{2,1,0:T(8,128)(2,1)}, u32[]{:S(2)}, u32[]{:S(2)}) async-start(bf16[2,1024,768]{2,1,0:T(8,128)(2,1)} %pad_maximum_fusion.3), calls=%async_computation.5 | async-start | bytes 6291456 | tf_op jit(solution)/shard_map/all_to_all | solution.py:148
  704.1 48.4 %reduce-scatter.11.cloned.1.call-start = ((), (), s32[]{:S(2)}) async-start(), calls=%async_computation.11 | async-start | bytes 786432 | tf_op jit(solution)/shard_map/reduce_scatter | solution.py:156
  708.5 95.6 %reduce-scatter.9.cloned.1.call-start = ((), (), s32[]{:S(2)}) async-start(), calls=%async_computation.10 | async-start | bytes 2359296 | tf_op jit(solution)/shard_map/reduce_scatter | solution.py:153
  740.6 4.7 copy-start.18
  750.3 56.4 %copy-start.10 = (bf16[1024,2,256]{0,2,1:T(8,128)(2,1)S(1)}, bf16[1024,2,256]{0,2,1:T(8,128)(2,1)}, u32[]{:S(2)}) copy-start(bf16[1024,2,256]{0,2,1:T(8,128)(2,1)} %copy.81) | copy-start | bytes 3145732
  750.3 56.4 %copy-start.20 = (bf16[512,512]{1,0:T(8,128)(2,1)S(1)}, bf16[512,512]{1,0:T(8,128)(2,1)}, u32[]{:S(2)}) copy-start(bf16[512,512]{1,0:T(8,128)(2,1)} %param.13) | copy-start | bytes 1572868
  750.3 340.8 %reduce-scatter.15.cloned.1.call-start = ((), (), s32[]{:S(2)}) async-start(), calls=%async_computation.13 | async-start | bytes 532480
  754.3 622.4 %reduce-scatter.13.cloned.1.call-start = ((), (), s32[]{:S(2)}) async-start(), calls=%async_computation.12 | async-start | bytes 1597440
  (14 other events, 28.1 us)
Sparse Core Ops, SparseCore 0:
  708.6 43.7 reduce-scatter.10
  754.9 49.1 reduce-scatter.8
  807.0 284.0 reduce-scatter.14
  1094.0 282.7 reduce-scatter.12
where the time goes:
time: 1390 us; the launch traced here: 1380 us
  waiting for transfers between devices  880 us (63%)
  local copies, waits for them, and re-layouts  215 us (15%)
  matrix products  131 us (9%)
  other arithmetic  69.3 us (5%)
  starting transfers between devices  58.6 us (4%)
  loops' own time  15.4 us (1%)
  between operations  14.5 us (1%)
    unnamed x6, waiting for transfers between devices  565 us
    all_to_all x1, waiting for transfers between devices, body(): lax.all_to_all(buffer, 'dom', split_axis=0, concat_axis=0, tiled=True)  105 us
    all_to_all x1, waiting for transfers between devices, body(): lax.all_to_all(outgoing, 'dom', split_axis=0, concat_axis=0, tiled=True)  86.9 us
    reduce_scatter x1, waiting for transfers between devices, body(): lax.psum_scatter(full_qkv.astype(jnp.bfloat16), 'head', scatter_dimension...  49.7 us
    dot_general x4, matrix products, backward_step(): jnp.einsum('jb,jrc->brc', one_hot, near_grad, precision=lax.Precision.HIG...  38.9 us
    all_to_all x1, waiting for transfers between devices, body(): lax.all_to_all(qkv_node.reshape(rows, groups, 3 * span), 'head', split_ax...  35.3 us
    reshape x8, local copies, waits for them, and re-layouts, key_sets(): near_kv = kv_all[ids].reshape(GB, NBR * block_size, 2 * span)  33.3 us
    all_to_all x1, waiting for transfers between devices, body(): lax.all_to_all(dqkv_part, 'head', split_axis=0, concat_axis=1, tiled=True)  32.1 us
  transfers between devices with their start and end apart: 10, of which 10 were waited for; matrix products, arithmetic and copies ran while one was open for 5% of the time, Pallas kernels for 0%

commit v1 on v0

v1 whole, which is shorter than its diff:
```python
import jax
import jax.numpy as jnp
from jax import lax
from jax.experimental import pallas as pl
from jax.experimental.pallas import tpu as pltpu
from jax.sharding import PartitionSpec as P

H = 8
NBR = 4
DEVICES = ("dom", "head")
F32, BF16 = jnp.float32, jnp.bfloat16
NEG = -1e30
LANES = 128
STATS = 3 * H
VMEM_LIMIT = 58 * 1024 * 1024


def nn(a, b):
    return jnp.dot(a, b, preferred_element_type=F32)


def nt(a, b):
    return lax.dot_general(a, b, (((1,), (1,)), ((), ())), preferred_element_type=F32)


def two_heads(pair):
    lane = lax.broadcasted_iota(jnp.int32, pair.shape, 1)
    zero = jnp.zeros_like(pair)
    return jnp.concatenate(
        [jnp.where(lane < LANES // 2, pair, zero), jnp.where(lane >= LANES // 2, pair, zero)], axis=0
    )


def own_heads(both):
    half, rows = both.shape[0] // 2, both.shape[1] // 2
    return jnp.concatenate([both[:half, :rows], both[half:, rows:]], axis=0)


def bias_of(tile):
    bias = jnp.where(tile != 0, 0.0, NEG).astype(F32).T
    return jnp.concatenate([bias, bias], axis=1)


def split_stat(row):
    return row[:, : row.shape[1] // 2], row[:, row.shape[1] // 2 :]


def query_kernel(near_ids, meta, q_ref, cot_ref, tile_ref, k_ref, v_ref, kt_ref, vt_ref, fk_ref,
                 fv_ref, fkt_ref, fvt_ref, att_ref, dq_ref, acc_ref, stats_ref, slot_ref, p_scr, ds_scr,
                 qz_scr, cz_scr, bias_scr):
    i = pl.program_id(0)
    pairs = q_ref.shape[1] // LANES
    bs = q_ref.shape[0]
    width = q_ref.shape[1]
    own = acc_ref.shape[0]

    @pl.when(i == 0)
    def _():
        acc_ref[...] = jnp.zeros_like(acc_ref)

    for j in range(NBR):
        bias_scr[j] = bias_of(tile_ref[0, j])
    ids = [near_ids[i, j] for j in range(NBR)]
    for c in range(pairs):
        cols = slice(c * LANES, (c + 1) * LANES)
        cot = cot_ref[:, cols]
        qz = two_heads(q_ref[:, cols])
        cz = two_heads(cot)
        qz_scr[c] = qz
        cz_scr[c] = cz
        scores = [nt(k_ref[ids[j], :, cols], qz) + bias_scr[j] for j in range(NBR)]
        scores.append(nt(fk_ref[0, :, cols], qz))
        scores = jnp.concatenate(scores, axis=0)
        peak = jnp.max(scores, axis=0, keepdims=True)
        probs = jnp.exp(scores - peak)
        inv = 1.0 / jnp.sum(probs, axis=0, keepdims=True)
        probs = probs * inv
        low = probs.astype(BF16)
        vt = jnp.concatenate([vt_ref[ids[j], cols, :] for j in range(NBR)] + [fvt_ref[0, cols, :]], axis=1)
        att = own_heads(nn(vt, low)).astype(BF16).astype(F32)
        att_ref[:, cols] = att.T.astype(BF16)
        prod = cot.astype(F32).T * att
        delta = jnp.concatenate(
            [jnp.sum(prod[: LANES // 2], axis=0, keepdims=True), jnp.sum(prod[LANES // 2 :], axis=0, keepdims=True)],
            axis=1,
        )
        grad_probs = jnp.concatenate(
            [nt(v_ref[ids[j], :, cols], cz) for j in range(NBR)] + [nt(fv_ref[0, :, cols], cz)], axis=0
        )
        ds = (probs * (grad_probs - delta)).astype(BF16)
        kt = jnp.concatenate([kt_ref[ids[j], cols, :] for j in range(NBR)] + [fkt_ref[0, cols, :]], axis=1)
        dq = own_heads(nn(kt, ds)) * 0.125
        dq_ref[:, cols] = dq.T.astype(BF16)
        p_scr[c] = low[: NBR * bs]
        ds_scr[c] = ds[: NBR * bs]
        for s, row in enumerate((peak, inv, delta)):
            first, second = split_stat(row)
            for e, part in enumerate((first, second)):
                at = s * H + 2 * c + e
                stats_ref[0, at : at + 1, :] = part
                slot_ref[0, at : at + 1, :] = part

    for j in range(NBR):

        @pl.when(ids[j] < own)
        def _(j=j):
            n = ids[j]
            for c in range(pairs):
                cols = slice(c * LANES, (c + 1) * LANES)
                vcols = slice(width + c * LANES, width + (c + 1) * LANES)
                rows = slice(j * bs, (j + 1) * bs)
                acc_ref[n, :, cols] += nn(ds_scr[c, rows, :], qz_scr[c])
                acc_ref[n, :, vcols] += nn(p_scr[c, rows, :], cz_scr[c])


def load_stats(ref, c):
    return [
        jnp.concatenate(
            [ref[0, s * H + 2 * c : s * H + 2 * c + 1, :], ref[0, s * H + 2 * c + 1 : s * H + 2 * c + 2, :]], axis=1
        )
        for s in range(3)
    ]


def key_terms(k, v, qz, cz, bias, stats):
    peak, inv, delta = stats
    scores = nt(k, qz)
    if bias is not None:
        scores = scores + bias
    probs = jnp.exp(scores - peak) * inv
    ds = (probs * (nt(v, cz) - delta)).astype(BF16)
    return nn(ds, qz), nn(probs.astype(BF16), cz)


def peer_kernel(near_ids, meta, q_ref, cot_ref, stats_ref, tile_ref, k_ref, v_ref, acc_in, acc_ref, qz_scr, cz_scr):
    i = pl.program_id(0)
    pairs = q_ref.shape[1] // LANES
    width = q_ref.shape[1]
    own = acc_ref.shape[0]

    @pl.when(i == 0)
    def _():
        acc_ref[...] = acc_in[...]

    for c in range(pairs):
        cols = slice(c * LANES, (c + 1) * LANES)
        qz_scr[c] = two_heads(q_ref[:, cols])
        cz_scr[c] = two_heads(cot_ref[:, cols])
    for j in range(NBR):
        n = near_ids[own + i, j]

        @pl.when(n < own)
        def _(j=j, n=n):
            bias = bias_of(tile_ref[0, j])
            for c in range(pairs):
                cols = slice(c * LANES, (c + 1) * LANES)
                vcols = slice(width + c * LANES, width + (c + 1) * LANES)
                dk, dv = key_terms(
                    k_ref[n, :, cols], v_ref[n, :, cols], qz_scr[c], cz_scr[c], bias, load_stats(stats_ref, c)
                )
                acc_ref[n, :, cols] += dk
                acc_ref[n, :, vcols] += dv


def far_kernel(meta, q_ref, cot_ref, stats_ref, k_ref, v_ref, acc_ref, dkv_ref):
    pairs = q_ref.shape[1] // LANES
    width = q_ref.shape[1]
    for c in range(pairs):
        cols = slice(c * LANES, (c + 1) * LANES)
        vcols = slice(width + c * LANES, width + (c + 1) * LANES)
        dk, dv = key_terms(
            k_ref[0, :, cols], v_ref[0, :, cols], two_heads(q_ref[:, cols]), two_heads(cot_ref[:, cols]), None,
            load_stats(stats_ref, c),
        )
        dkv_ref[:, cols] = (acc_ref[0, :, cols] + dk.astype(BF16).astype(F32)).astype(BF16)
        dkv_ref[:, vcols] = (acc_ref[0, :, vcols] + dv.astype(BF16).astype(F32)).astype(BF16)


def call(kernel, scalars, steps, in_specs, out_specs, out_shape, scratch, flops, touched, name):
    return pl.pallas_call(
        kernel,
        grid_spec=pltpu.PrefetchScalarGridSpec(
            num_scalar_prefetch=scalars, grid=(steps,), in_specs=in_specs, out_specs=out_specs, scratch_shapes=scratch
        ),
        out_shape=out_shape,
        compiler_params=pltpu.CompilerParams(dimension_semantics=("arbitrary",), vmem_limit_bytes=VMEM_LIMIT),
        cost_estimate=pl.CostEstimate(flops=flops, bytes_accessed=touched, transcendentals=0),
        name=name,
    )


def once(shape, at=0):
    return pl.BlockSpec(shape, lambda i, *s: (at,) + (0,) * (len(shape) - 1), pipeline_mode=pl.Buffered(1))


def body(node_feats, w_qkv, w_out, neighbours, tiles, partner, layer_cot):
    rows, width = node_feats.shape
    doms, groups = lax.axis_size("dom"), lax.axis_size("head")
    devices = doms * groups
    blocks = partner.shape[0]
    own = blocks // groups
    bs = tiles.shape[2]
    span = width // groups
    half = lax.axis_index("head")
    base = half * own

    near_ids = jnp.roll((neighbours - base) % blocks, -base, axis=0)
    mine = lax.dynamic_slice_in_dim(partner, base, own, 0)
    meta = jnp.concatenate([base[None].astype(jnp.int32), mine // own])
    table = lax.all_gather(partner, "dom", axis=0, tiled=True)
    one_hot = (table[:, None] == jnp.arange(table.shape[0], dtype=jnp.int32)[None, :]).astype(BF16)

    w_by = w_qkv.reshape(width, groups, 3, span).transpose(2, 0, 1, 3).reshape(3, width, width)
    w_all = jnp.concatenate([w_by[0] * jnp.asarray(0.125, BF16), w_by[1], w_by[2]], axis=1)

    def swap(x):
        return lax.ppermute(x, "head", [(0, 1), (1, 0)])

    def exchange(x):
        return lax.all_to_all(x, DEVICES, split_axis=0, concat_axis=0, tiled=True)

    def far(x):
        spread = exchange(x.reshape(own, bs, width).transpose(1, 0, 2))
        picked = jnp.dot(one_hot, spread.reshape(-1, width), preferred_element_type=F32).astype(BF16)
        back = exchange(picked.reshape(devices, own, width))
        return back.transpose(1, 0, 2).reshape(rows, width)

    cot = jnp.dot(layer_cot, w_out.T, preferred_element_type=F32).astype(BF16)
    far_feats = far(node_feats)
    peer_feats = swap(node_feats)
    far_cot = far(cot)
    peer_cot = swap(cot)

    part_feats = jnp.concatenate([node_feats, peer_feats], axis=0)
    part_qkv = jnp.dot(part_feats, w_all, preferred_element_type=F32).astype(BF16)
    far_qkv = jnp.dot(far_feats, w_all, preferred_element_type=F32).astype(BF16)

    def turned(feats):
        flat = jnp.einsum("dc,brd->bcr", w_all[:, width:], feats.reshape(-1, bs, width), preferred_element_type=F32)
        return flat.astype(BF16)

    part_t, far_t = turned(part_feats), turned(far_feats)
    part_blk = part_qkv.reshape(blocks, bs, 3 * width)
    far_blk = far_qkv.reshape(own, bs, 3 * width)

    step = lambda i, *s: (i, 0)
    pair_flops = 2 * bs * bs * width * 2
    att, dq, acc, stats, slots = call(
        query_kernel, 2, own,
        [
            pl.BlockSpec((bs, width), step),
            pl.BlockSpec((bs, width), step),
            pl.BlockSpec((1, NBR, bs, bs), lambda i, ids, meta: (meta[0] + i, 0, 0, 0)),
            pl.BlockSpec((blocks, bs, width), lambda i, *s: (0, 0, 1), pipeline_mode=pl.Buffered(1)),
            pl.BlockSpec((blocks, bs, width), lambda i, *s: (0, 0, 2), pipeline_mode=pl.Buffered(1)),
            pl.BlockSpec((blocks, width, bs), lambda i, *s: (0, 0, 0), pipeline_mode=pl.Buffered(1)),
            pl.BlockSpec((blocks, width, bs), lambda i, *s: (0, 1, 0), pipeline_mode=pl.Buffered(1)),
            pl.BlockSpec((1, bs, width), lambda i, *s: (i, 0, 1)),
            pl.BlockSpec((1, bs, width), lambda i, *s: (i, 0, 2)),
            pl.BlockSpec((1, width, bs), lambda i, *s: (i, 0, 0)),
            pl.BlockSpec((1, width, bs), lambda i, *s: (i, 1, 0)),
        ],
        [
            pl.BlockSpec((bs, width), step),
            pl.BlockSpec((bs, width), step),
            pl.BlockSpec((own, bs, 2 * width), lambda i, *s: (0, 0, 0)),
            pl.BlockSpec((1, STATS, bs), lambda i, *s: (i, 0, 0)),
            pl.BlockSpec((1, STATS, bs), lambda i, ids, meta: (meta[1 + i], 0, 0)),
        ],
        [
            jax.ShapeDtypeStruct((rows, width), BF16),
            jax.ShapeDtypeStruct((rows, width), BF16),
            jax.ShapeDtypeStruct((own, bs, 2 * width), F32),
            jax.ShapeDtypeStruct((own, STATS, bs), F32),
            jax.ShapeDtypeStruct((devices, STATS, bs), F32),
        ],
        [
            pltpu.VMEM((width // LANES, NBR * bs, 2 * bs), BF16),
            pltpu.VMEM((width // LANES, NBR * bs, 2 * bs), BF16),
            pltpu.VMEM((width // LANES, 2 * bs, LANES), BF16),
            pltpu.VMEM((width // LANES, 2 * bs, LANES), BF16),
            pltpu.VMEM((NBR, bs, 2 * bs), F32),
        ],
        own * 40 * pair_flops, 30 << 20, "own_queries",
    )(near_ids, meta, part_qkv, cot, tiles, part_blk, part_blk, part_t, part_t, far_blk, far_blk, far_t, far_t)

    peer_stats = swap(stats)
    far_slots = exchange(slots)

    layer_out = jnp.dot(att, w_out, preferred_element_type=F32).astype(BF16)
    dwo_t = jnp.einsum("rc,ra->ca", layer_cot, att, preferred_element_type=F32).astype(BF16)
    dwq = jnp.einsum("rd,rc->dc", node_feats, dq, preferred_element_type=F32).astype(BF16)

    def pieces(w):
        return w.reshape(doms, width // doms, groups, span).transpose(0, 2, 1, 3).reshape(devices, width // doms, span)

    def summed(ws):
        moved = exchange(jnp.concatenate([pieces(w) for w in ws], axis=2))
        return jnp.sum(moved.astype(F32), axis=0)

    early = summed([dwo_t, dwq])

    (acc,) = call(
        peer_kernel, 2, own,
        [
            pl.BlockSpec((bs, width), lambda i, *s: (own + i, 0)),
            pl.BlockSpec((bs, width), step),
            pl.BlockSpec((1, STATS, bs), lambda i, *s: (i, 0, 0)),
            pl.BlockSpec((1, NBR, bs, bs), lambda i, ids, meta: (own - meta[0] + i, 0, 0, 0)),
            pl.BlockSpec((own, bs, width), lambda i, *s: (0, 0, 1), pipeline_mode=pl.Buffered(1)),
            pl.BlockSpec((own, bs, width), lambda i, *s: (0, 0, 2), pipeline_mode=pl.Buffered(1)),
            once((own, bs, 2 * width)),
        ],
        [pl.BlockSpec((own, bs, 2 * width), lambda i, *s: (0, 0, 0))],
        [jax.ShapeDtypeStruct((own, bs, 2 * width), F32)],
        [
            pltpu.VMEM((width // LANES, 2 * bs, LANES), BF16),
            pltpu.VMEM((width // LANES, 2 * bs, LANES), BF16),
        ],
        own * 16 * pair_flops, 20 << 20, "peer_queries",
    )(near_ids, meta, part_qkv, peer_cot, peer_stats, tiles, part_blk, part_blk, acc)

    (dkv,) = call(
        far_kernel, 1, own,
        [
            pl.BlockSpec((bs, width), step),
            pl.BlockSpec((bs, width), step),
            pl.BlockSpec((1, STATS, bs), lambda i, meta: (meta[1 + i], 0, 0)),
            pl.BlockSpec((1, bs, width), lambda i, *s: (i, 0, 1)),
            pl.BlockSpec((1, bs, width), lambda i, *s: (i, 0, 2)),
            pl.BlockSpec((1, bs, 2 * width), lambda i, *s: (i, 0, 0)),
        ],
        [pl.BlockSpec((bs, 2 * width), step)],
        [jax.ShapeDtypeStruct((rows, 2 * width), BF16)],
        [], own * 8 * pair_flops, 10 << 20, "far_queries",
    )(meta, far_qkv, far_cot, far_slots, part_blk, part_blk, acc)

    dwkv = jnp.einsum("rd,rc->dc", node_feats, dkv, preferred_element_type=F32).astype(BF16)
    late = summed([dwkv[:, :width], dwkv[:, width:]])
    w_plain = w_by.transpose(1, 0, 2).reshape(width, 3 * width)
    feat_grad = (
        lax.dot_general(dq, w_plain[:, :width], (((1,), (1,)), ((), ())), preferred_element_type=F32)
        + lax.dot_general(dkv, w_plain[:, width:], (((1,), (1,)), ((), ())), preferred_element_type=F32)
    ).astype(BF16)
    dw_out = early[:, :span].T
    dw_qkv = jnp.concatenate([early[:, span:], late], axis=1)
    return (layer_out, feat_grad, dw_qkv, dw_out)


def solution(mesh):
    placed = (
        P(DEVICES, None),
        P(),
        P(),
        P("dom", None),
        P("dom", None, None, None),
        P("dom"),
        P(DEVICES, None),
    )
    return jax.shard_map(
        body,
        mesh=mesh,
        in_specs=placed,
        out_specs=(P(DEVICES, None), P(DEVICES, None), P("dom", "head"), P("head", "dom")),
        check_vma=False,
    )
```

time: 1390 us -> 311 us (0.22)
  waiting for transfers between devices: 880 us -> 32 us
  local copies, waits for them, and re-layouts: 215 us -> 27.2 us
  matrix products: 131 us -> 40.8 us
  Pallas kernels: 0 us -> 72.1 us
  other arithmetic: 69.3 us -> 5 us
  starting transfers between devices: 58.6 us -> 111 us
  blocking collectives: 0 us -> 19.4 us
  loops' own time: 15.4 us -> 0 us
    unnamed x6 -> x0, waiting for transfers between devices: 565 us -> none
    all_to_all x6 -> x7, waiting for transfers between devices: 263 us -> 32 us  [exchange(): return lax.all_to_all(x, DEVICES, split_axis=0, concat_axis=0, tiled=True)]
    dot_general x38 -> x13, matrix products: 131 us -> 40.8 us  [the longest x2 7.97 us: turned(): jnp.einsum('dc,brd->bcr', w_all[:, width:], feats.reshape(-1, bs, width),...]
    pallas_call x0 -> x3, Pallas kernels: none -> 72.1 us  [the longest x1 40.8 us: body(): call(query_kernel, 2, own, [pl.BlockSpec((bs, width), step), pl.BlockSpec...]
    reshape x17 -> x5, local copies, waits for them, and re-layouts: 61.2 us -> 2.04 us  [the longest x1 1.54 us: far(): spread = exchange(x.reshape(own, bs, width).transpose(1, 0, 2))]
    reduce_scatter x2 -> x0, waiting for transfers between devices: 51.8 us -> none  [the longest x1 49.7 us: body(): lax.psum_scatter(full_qkv.astype(jnp.bfloat16), 'head', scatter_dimension...]
    all_to_all x6 -> x7, starting transfers between devices: 58.4 us -> 105 us  [exchange(): return lax.all_to_all(x, DEVICES, split_axis=0, concat_axis=0, tiled=True)]
    gather x10 -> x0, local copies, waits for them, and re-layouts: 39.5 us -> none  [the longest x8 28.6 us: key_sets(): near_kv = kv_all[ids].reshape(GB, NBR * block_size, 2 * span)]
  transfers between devices with their start and end apart: 10 -> 10, of which waited for: 10 -> 4; matrix products, arithmetic and copies ran while one was open for 5% -> 21% of each run, Pallas kernels for 0% -> 23%
where the time goes in v1:
time: 311 us; the launch traced here: 309 us
  starting transfers between devices  111 us (36%)
  Pallas kernels  72.1 us (23%)
  matrix products  40.8 us (13%)
  waiting for transfers between devices  32 us (10%)
  local copies, waits for them, and re-layouts  27.2 us (9%)
  blocking collectives  19.4 us (6%)
  other arithmetic  5 us (2%)
    all_to_all x7, starting transfers between devices, exchange(): return lax.all_to_all(x, DEVICES, split_axis=0, concat_axis=0, tiled=True)  105 us
    pallas_call x1, Pallas kernels, body(): call(query_kernel, 2, own, [pl.BlockSpec((bs, width), step), pl.BlockSpec...  40.8 us
    all_to_all x7, waiting for transfers between devices, exchange(): return lax.all_to_all(x, DEVICES, split_axis=0, concat_axis=0, tiled=True)  32 us
    pallas_call x1, Pallas kernels, body(): call(peer_kernel, 2, own, [pl.BlockSpec((bs, width), lambda i, *s: (own +...  19.9 us
    unnamed x1, blocking collectives  19.4 us
    pallas_call x1, Pallas kernels, body(): call(far_kernel, 1, own, [pl.BlockSpec((bs, width), step), pl.BlockSpec((...  11.4 us
    unnamed x46, local copies, waits for them, and re-layouts  8.5 us
    dot_general x2, matrix products, turned(): jnp.einsum('dc,brd->bcr', w_all[:, width:], feats.reshape(-1, bs, width),...  7.97 us
  transfers between devices with their start and end apart: 10, of which 4 were waited for; matrix products, arithmetic and copies ran while one was open for 21% of the time, Pallas kernels for 23%

profile of v1, /device:TPU:0, one launch (start us, length us, event | category | flops | bytes accessed | tf_op | source)
XLA Modules:
  0.0 309.4 jit_solution(15375075016935561850)
XLA Ops:
  0.6 2.9 copy.61
  3.5 11.7 %all-to-all-start = ((bf16[128,8,512]{2,1,0:T(8,128)(2,1)}), bf16[128,8,512]{2,1,0:T(8,128)(2,1)}, u32[]{:S(2)}, u32[]{:S(2)}) async-start(bf16[128,8,512]{2,1,0:T(8,128)(2,1)} %copy.61), calls=%async_computation | async-start | bytes 2097152 | tf_op jit(solution)/shard_map/all_to_all | solution.py:220
  15.2 2.9 collective-permute-start
  23.2 10.3 %all-to-all-done = bf16[128,8,512]{2,1,0:T(8,128)(2,1)} async-done(((bf16[128,8,512]{2,1,0:T(8,128)(2,1)}), bf16[128,8,512]{2,1,0:T(8,128)(2,1)}, u32[]{:S(2)}, u32[]{:S(2)}) %all-to-all-start) | async-done | bytes 1048608 | tf_op jit(solution)/shard_map/all_to_all | solution.py:220
  33.5 25.8 %all-to-all-start.2 = ((bf16[128,8,512]{2,1,0:T(8,128)(2,1)}), bf16[128,8,512]{2,1,0:T(8,128)(2,1)}, u32[]{:S(2)}, u32[]{:S(2)}) async-start(bf16[128,8,512]{2,1,0:T(8,128)(2,1)} %bitcast.90), calls=%async_computation.2 | async-start | bytes 2097152 | tf_op jit(solution)/shard_map/all_to_all | solution.py:220
  61.1 2.0 copy.78
  63.1 2.1 copy.79
  67.7 19.4 %all-reduce = s32[1024]{0:T(1024)S(1)} all-reduce(s32[1024]{0:T(1024)S(1)} %dynamic-update-slice), channel_id=1, replica_groups=mesh['dom'=64,'head'=2] {'dom'}, use_global_device_ids=true, to_apply=%add | all-reduce | flops 1024 | bytes 8192
  87.7 2.3 constant_dynamic-update-slice_fusion.1
  90.0 3.5 %fusion.8 = bf16[128,8,512]{2,1,0:T(8,128)(2,1)} fusion(s32[1024]{0:T(1024)S(1)} %all-reduce, bf16[128,8,512]{2,1,0:T(8,128)(2,1)} %all-to-all-done), kind=kOutput, calls=%fused_computation.20 | convolution fusion | flops 1075314688 | bytes 2101248 | tf_op jit(solution)/shard_map/dot_general | solution.py:224
  93.5 6.4 %all-to-all-start.1 = ((bf16[128,8,512]{2,1,0:T(8,128)(2,1)}), bf16[128,8,512]{2,1,0:T(8,128)(2,1)}, u32[]{:S(2)}, u32[]{:S(2)}) async-start(bf16[128,8,512]{2,1,0:T(8,128)(2,1)} %fusion.8), calls=%async_computation.1 | async-start | bytes 2097152 | tf_op jit(solution)/shard_map/all_to_all | solution.py:220
  99.9 3.7 %fusion.7 = bf16[128,8,512]{2,1,0:T(8,128)(2,1)} fusion(s32[1024]{0:T(1024)S(1)} %all-reduce, bf16[128,8,512]{2,1,0:T(8,128)(2,1)} %all-to-all-done.2), kind=kOutput, calls=%fused_computation.19 | convolution fusion | flops 1075314688 | bytes 2101248 | tf_op jit(solution)/shard_map/dot_general | solution.py:224
  105.2 4.0 %convert_bitcast_fusion.kt_ref.vt_ref = bf16[16,1024,128]{2,1,0:T(8,128)(2,1)} fusion(bf16[16,128,512]{2,1,0:T(8,128)(2,1)S(1)} %bitcast.106, bf16[512,512]{1,0:T(8,128)(2,1)S(1)} %copy-done.8, bf16[512,512]{1,0:T(8,128)(2,1)S(1)} %copy-done.7), kind=kOutput, calls=%fused_computation.4 | convolution fusion | flops 2151677952 | bytes 7340032 | tf_op jit(solution)/shard_map/dc,brd->bcr/dot_general | solution.py:239
  109.2 5.7 %convolution_convert_fusion.q_ref = bf16[2048,1536]{1,0:T(8,128)(2,1)} fusion(bf16[2048,512]{1,0:T(8,128)(2,1)S(1)} %constant_dynamic-update-slice_fusion, bf16[512,512]{1,0:T(8,128)(2,1)S(1)} %copy-done.8, bf16[512,512]{1,0:T(8,128)(2,1)S(1)} %copy-done.7, bf16[512,512]{1,0:T(8,128)(2,1)S(1)} %copy-done.10), kind=kOutput, calls=%fused_computation | convolution fusion | flops 3229089792 | bytes 9961472 | tf_op jit(solution)/shard_map/dot_general | solution.py:235
  114.8 3.2 %all-to-all-done.1 = bf16[128,8,512]{2,1,0:T(8,128)(2,1)} async-done(((bf16[128,8,512]{2,1,0:T(8,128)(2,1)}), bf16[128,8,512]{2,1,0:T(8,128)(2,1)}, u32[]{:S(2)}, u32[]{:S(2)}) %all-to-all-start.1) | async-done | bytes 1048608 | tf_op jit(solution)/shard_map/all_to_all | solution.py:220
  118.1 7.0 %all-to-all-start.3 = ((bf16[128,8,512]{2,1,0:T(8,128)(2,1)}), bf16[128,8,512]{2,1,0:T(8,128)(2,1)}, u32[]{:S(2)}, u32[]{:S(2)}) async-start(bf16[128,8,512]{2,1,0:T(8,128)(2,1)} %fusion.7), calls=%async_computation.3 | async-start | bytes 2097152 | tf_op jit(solution)/shard_map/all_to_all | solution.py:220
  126.7 3.5 %convolution_convert_fusion.1.q_ref = bf16[1024,1536]{1,0:T(8,128)(2,1)} fusion(bf16[1024,512]{1,0:T(8,128)(2,1)S(1)} %bitcast.105, bf16[512,512]{1,0:T(8,128)(2,1)S(1)} %copy-done.9, bf16[512,512]{1,0:T(8,128)(2,1)S(1)} %copy-done.7, bf16[512,512]{1,0:T(8,128)(2,1)S(1)} %copy-done.11), kind=kOutput, calls=%fused_computation.5 | convolution fusion | flops 1616904192 | bytes 5767168 | tf_op jit(solution)/shard_map/dot_general | solution.py:236
  130.3 4.0 %convert_bitcast_fusion.1.fkt_ref.fvt_ref = bf16[8,1024,128]{2,1,0:T(8,128)(2,1)} fusion(bf16[512,512]{1,0:T(8,128)(2,1)S(1)} %copy-done.9, bf16[512,512]{1,0:T(8,128)(2,1)S(1)} %copy-done.7, bf16[128,8,512]{2,1,0:T(8,128)(2,1)} %all-to-all-done.1), kind=kOutput, calls=%fused_computation.9 | convolution fusion | flops 1076887552 | bytes 4194304 | tf_op jit(solution)/shard_map/dc,brd->bcr/dot_general | solution.py:239
  134.2 40.8 %own_queries.1 = (bf16[1024,512]{1,0:T(8,128)(2,1)}, bf16[1024,512]{1,0:T(8,128)(2,1)}, f32[8,128,1024]{2,1,0:T(8,128)}, f32[8,24,128]{2,1,0:T(8,128)}, f32[128,24,128]{2,1,0:T(8,128)}) custom-call(s32[16,4]{1,0:T(8,128)} %copy.80.near_ids, s32[9]{0:T(128)} %pad_add_fusion.1.meta, bf16[2048,1536]{1,0:T(8,128)(2,1)} %convolution_convert_fusion.q_ref, ...), custom_call_target="tpu_custom_call" | custom-call | flops 10737418240 | bytes 31457280 | tf_op jit(solution)/shard_map/own_queries/pallas_call | solution.py:248
  175.1 12.2 %all-to-all-start.4 = ((f32[128,24,128]{2,1,0:T(8,128)}), f32[128,24,128]{2,1,0:T(8,128)}, u32[]{:S(2)}, u32[]{:S(2)}) async-start(f32[128,24,128]{2,1,0:T(8,128)} %get-tuple-element.11), calls=%async_computation.4 | async-start | bytes 3145728 | tf_op jit(solution)/shard_map/all_to_all | solution.py:220
  187.3 2.9 collective-permute-start.1
  197.0 2.5 copy.66
  199.6 3.1 fusion.15
  203.7 7.6 %all-to-all-done.4.stats_ref = f32[128,24,128]{2,1,0:T(8,128)} async-done(((f32[128,24,128]{2,1,0:T(8,128)}), f32[128,24,128]{2,1,0:T(8,128)}, u32[]{:S(2)}, u32[]{:S(2)}) %all-to-all-start.4) | async-done | bytes 1572896 | tf_op jit(solution)/shard_map/all_to_all | solution.py:220
  211.2 27.0 %all-to-all-start.5 = ((bf16[128,8,512]{2,1,0:T(8,128)(2,1)}), bf16[128,8,512]{2,1,0:T(8,128)(2,1)S(1)}, u32[]{:S(2)}, u32[]{:S(2)}) async-start(bf16[128,8,512]{2,1,0:T(8,128)(2,1)} %pad_maximum_fusion.1), calls=%async_computation.5 | async-start | bytes 2097152 | tf_op jit(solution)/shard_map/all_to_all | solution.py:220
  238.9 19.9 %peer_queries.1.acc_ref = f32[8,128,1024]{2,1,0:T(8,128)} custom-call(s32[16,4]{1,0:T(8,128)} %copy.80.near_ids, s32[9]{0:T(128)} %pad_add_fusion.1.meta, bf16[2048,1536]{1,0:T(8,128)(2,1)} %convolution_convert_fusion.q_ref, bf16[1024,512]{1,0:T(8,128)(2,1)} %collective-permute-done.1.cot_ref, f32[8,24,128]{2,1,0:T(8,128)} %copy-done.12, ...), custom_call_target="tpu_custom_call" | custom-call | flops 4294967296 | bytes 20971520 | tf_op jit(solution)/shard_map/peer_queries/pallas_call | solution.py:303
  258.8 11.4 %far_queries.1 = bf16[1024,1024]{1,0:T(8,128)(2,1)} custom-call(s32[9]{0:T(128)} %pad_add_fusion.1.meta, bf16[1024,1536]{1,0:T(8,128)(2,1)} %convolution_convert_fusion.1.q_ref, bf16[1024,512]{1,0:T(8,128)(2,1)} %bitcast.91, f32[128,24,128]{2,1,0:T(8,128)} %all-to-all-done.4.stats_ref, bf16[16,128,1536]{2,1,0:T(8,128)(2,1)} %bitcast.83, ...), custom_call_target="tpu_custom_call" | custom-call | flops 2147483648 | bytes 10485760 | tf_op jit(solution)/shard_map/far_queries/pallas_call | solution.py:323
  270.2 3.1 %fusion.6 = bf16[512,1024]{0,1:T(8,128)(2,1)S(1)} fusion(bf16[1024,1024]{1,0:T(8,128)(2,1)} %far_queries.1, bf16[1024,512]{1,0:T(8,128)(2,1)} %param.7), kind=kOutput, calls=%fused_computation.18 | convolution fusion | flops 1074266112 | bytes 4194304 | tf_op jit(solution)/shard_map/rd,rc->dc/dot_general | solution.py:338
  275.4 14.6 %all-to-all-start.6 = ((bf16[128,8,512]{2,1,0:T(8,128)(2,1)}), bf16[128,8,512]{2,1,0:T(8,128)(2,1)S(1)}, u32[]{:S(2)}, u32[]{:S(2)}) async-start(bf16[128,8,512]{2,1,0:T(8,128)(2,1)} %pad_maximum_fusion.2), calls=%async_computation.6 | async-start | bytes 2097152 | tf_op jit(solution)/shard_map/all_to_all | solution.py:220
  290.0 2.9 convolution_convert_fusion.3
  293.7 3.9 %add_convert_fusion = bf16[1024,512]{1,0:T(8,128)(2,1)} fusion(f32[1024,512]{1,0:T(8,128)S(1)} %copy-done.4, bf16[1024,1024]{1,0:T(8,128)(2,1)} %far_queries.1, bf16[512,1536]{0,1:T(8,128)(2,1)S(1)} %bitcast.93), kind=kOutput, calls=%fused_computation.8 | convolution fusion | flops 1074790400 | bytes 6291456 | tf_op jit(solution)/shard_map/dot_general | solution.py:343
  297.6 10.9 %all-to-all-done.6 = bf16[128,8,512]{2,1,0:T(8,128)(2,1)S(1)} async-done(((bf16[128,8,512]{2,1,0:T(8,128)(2,1)}), bf16[128,8,512]{2,1,0:T(8,128)(2,1)S(1)}, u32[]{:S(2)}, u32[]{:S(2)}) %all-to-all-start.6) | async-done | bytes 1048608 | tf_op jit(solution)/shard_map/all_to_all | solution.py:220
  (85 shorter events, 24.7 us)
Async XLA Ops:
  0.6 19.2 %copy-start = (bf16[1024,512]{1,0:T(8,128)(2,1)S(1)}, bf16[1024,512]{1,0:T(8,128)(2,1)}, u32[]{:S(2)}) copy-start(bf16[1024,512]{1,0:T(8,128)(2,1)} %param.13) | copy-start | bytes 3145732
  3.5 29.9 %all-to-all-start = ((bf16[128,8,512]{2,1,0:T(8,128)(2,1)}), bf16[128,8,512]{2,1,0:T(8,128)(2,1)}, u32[]{:S(2)}, u32[]{:S(2)}) async-start(bf16[128,8,512]{2,1,0:T(8,128)(2,1)} %copy.61), calls=%async_computation | async-start | bytes 2097152 | tf_op jit(solution)/shard_map/all_to_all | solution.py:220
  15.2 4.6 %copy-start.16 = (bf16[512,512]{1,0:T(8,128)(2,1)S(1)}, bf16[512,512]{1,0:T(8,128)(2,1)}, u32[]{:S(2)}) copy-start(bf16[512,512]{1,0:T(8,128)(2,1)} %param.9) | copy-start | bytes 1572868
  15.2 88.4 %collective-permute-start = (bf16[1024,512]{1,0:T(8,128)(2,1)}, bf16[1024,512]{1,0:T(8,128)(2,1)}, u32[]{:S(2)}, u32[]{:S(2)}) collective-permute-start(bf16[1024,512]{1,0:T(8,128)(2,1)} %param.7), channel_id=1, source_target_pairs={{0,1},{1,0},{2,3},{3,2},{4,5},{5,4},{6,7},{7,6},{8,9},{9,8},{10,11... | collective-permute-start | bytes 3145736 | tf_op jit(solution)/shard_map/ppermute | solution.py:217
  19.8 3.3 %copy-start.13 = (s32[16,4]{0,1:T(4,128)S(1)}, s32[16,4]{0,1:T(4,128)}, u32[]{:S(2)}) copy-start(s32[16,4]{0,1:T(4,128)} %param.10) | copy-start | bytes 772
  20.6 1.0 copy-start.2
  33.5 60.0 %all-to-all-start.2 = ((bf16[128,8,512]{2,1,0:T(8,128)(2,1)}), bf16[128,8,512]{2,1,0:T(8,128)(2,1)}, u32[]{:S(2)}, u32[]{:S(2)}) async-start(bf16[128,8,512]{2,1,0:T(8,128)(2,1)} %bitcast.90), calls=%async_computation.2 | async-start | bytes 2097152 | tf_op jit(solution)/shard_map/all_to_all | solution.py:220
  60.4 5.9 %copy-start.19 = (u32[128]{0:T(128)S(1)}, u32[128]{0:T(128)}, u32[]{:S(2)}) copy-start(u32[128]{0:T(128)} %constant.61) | copy-start | bytes 1540
  60.4 7.1 %copy-start.18 = (s32[16]{0:T(128)S(1)}, s32[16]{0:T(128)}, u32[]{:S(2)}) copy-start(s32[16]{0:T(128)} %param.12) | copy-start | bytes 196
  93.5 24.5 %all-to-all-start.1 = ((bf16[128,8,512]{2,1,0:T(8,128)(2,1)}), bf16[128,8,512]{2,1,0:T(8,128)(2,1)}, u32[]{:S(2)}, u32[]{:S(2)}) async-start(bf16[128,8,512]{2,1,0:T(8,128)(2,1)} %fusion.8), calls=%async_computation.1 | async-start | bytes 2097152 | tf_op jit(solution)/shard_map/all_to_all | solution.py:220
  99.9 3.7 %copy-start.6 = (bf16[2048,512]{1,0:T(8,128)(2,1)S(1)}, bf16[2048,512]{1,0:T(8,128)(2,1)}, u32[]{:S(2)}) copy-start(bf16[2048,512]{1,0:T(8,128)(2,1)} %constant_dynamic-update-slice_fusion.1) | copy-start | bytes 6291460
  103.6 1.4 copy-start.7
  103.6 1.5 copy-start.8
  105.1 4.0 %copy-start.10 = (bf16[512,512]{1,0:T(8,128)(2,1)S(1)}, bf16[512,512]{1,0:T(8,128)(2,1)}, u32[]{:S(2)}) copy-start(bf16[512,512]{1,0:T(8,128)(2,1)} %copy.77) | copy-start | bytes 1572868
  118.1 57.0 %all-to-all-start.3 = ((bf16[128,8,512]{2,1,0:T(8,128)(2,1)}), bf16[128,8,512]{2,1,0:T(8,128)(2,1)}, u32[]{:S(2)}, u32[]{:S(2)}) async-start(bf16[128,8,512]{2,1,0:T(8,128)(2,1)} %fusion.7), calls=%async_computation.3 | async-start | bytes 2097152 | tf_op jit(solution)/shard_map/all_to_all | solution.py:220
  125.1 1.6 copy-start.9
  125.1 1.6 copy-start.11
  175.1 36.2 %all-to-all-start.4 = ((f32[128,24,128]{2,1,0:T(8,128)}), f32[128,24,128]{2,1,0:T(8,128)}, u32[]{:S(2)}, u32[]{:S(2)}) async-start(f32[128,24,128]{2,1,0:T(8,128)} %get-tuple-element.11), calls=%async_computation.4 | async-start | bytes 3145728 | tf_op jit(solution)/shard_map/all_to_all | solution.py:220
  187.3 4.1 %copy-start.14 = (bf16[1024,512]{1,0:T(8,128)(2,1)S(1)}, bf16[1024,512]{1,0:T(8,128)(2,1)}, u32[]{:S(2)}) copy-start(bf16[1024,512]{1,0:T(8,128)(2,1)} %get-tuple-element.9) | copy-start | bytes 3145732
  187.3 50.9 %collective-permute-start.1 = (bf16[1024,512]{1,0:T(8,128)(2,1)}, bf16[1024,512]{1,0:T(8,128)(2,1)}, u32[]{:S(2)}, u32[]{:S(2)}) collective-permute-start(bf16[1024,512]{1,0:T(8,128)(2,1)} %copy-done.2), channel_id=1, source_target_pairs={{0,1},{1,0},{2,3},{3,2},{4,5},{5,4},{6,7},{7,6},{8,9},{9,8},{10,11... | collective-permute-start | bytes 3145736 | tf_op jit(solution)/shard_map/ppermute | solution.py:217
  192.2 1.2 copy-start.5
  195.4 0.9 copy-start.17
  196.3 42.0 %collective-permute-start.2 = (f32[8,24,128]{2,1,0:T(8,128)S(1)}, f32[8,24,128]{2,1,0:T(8,128)S(1)}, u32[]{:S(2)}, u32[]{:S(2)}) collective-permute-start(f32[8,24,128]{2,1,0:T(8,128)S(1)} %copy-done.17), channel_id=1, source_target_pairs={{0,1},{1,0},{2,3},{3,2},{4,5},{5,4},{6,7},{7,6},{8,9},{9,8},{10,11... | collective-permute-start | bytes 294920 | tf_op jit(solution)/shard_map/ppermute | solution.py:217
  211.2 64.1 %all-to-all-start.5 = ((bf16[128,8,512]{2,1,0:T(8,128)(2,1)}), bf16[128,8,512]{2,1,0:T(8,128)(2,1)S(1)}, u32[]{:S(2)}, u32[]{:S(2)}) async-start(bf16[128,8,512]{2,1,0:T(8,128)(2,1)} %pad_maximum_fusion.1), calls=%async_computation.5 | async-start | bytes 2097152 | tf_op jit(solution)/shard_map/all_to_all | solution.py:220
  238.3 0.6 copy-start.12
  275.4 14.7 %copy-start.15 = (bf16[1024,512]{1,0:T(8,128)(2,1)S(1)}, bf16[1024,512]{1,0:T(8,128)(2,1)}, u32[]{:S(2)}) copy-start(bf16[1024,512]{1,0:T(8,128)(2,1)} %get-tuple-element.9) | copy-start | bytes 3145732
  275.4 33.2 %all-to-all-start.6 = ((bf16[128,8,512]{2,1,0:T(8,128)(2,1)}), bf16[128,8,512]{2,1,0:T(8,128)(2,1)S(1)}, u32[]{:S(2)}, u32[]{:S(2)}) async-start(bf16[128,8,512]{2,1,0:T(8,128)(2,1)} %pad_maximum_fusion.2), calls=%async_computation.6 | async-start | bytes 2097152 | tf_op jit(solution)/shard_map/all_to_all | solution.py:220
  290.0 3.7 %copy-start.3 = (bf16[3,512,2,256]{1,3,2,0:T(8,128)(2,1)S(1)}, bf16[3,512,2,256]{1,3,2,0:T(8,128)(2,1)}, u32[]{:S(2)}) copy-start(bf16[3,512,2,256]{1,3,2,0:T(8,128)(2,1)} %copy.64) | copy-start | bytes 4718596
  290.0 3.7 %copy-start.4 = (f32[1024,512]{1,0:T(8,128)S(1)}, f32[1024,512]{1,0:T(8,128)}, u32[]{:S(2)}) copy-start(f32[1024,512]{1,0:T(8,128)} %fusion.15) | copy-start | bytes 6291460
  293.7 15.7 %copy-start.1 = (bf16[1024,512]{1,0:T(8,128)(2,1)S(1)}, bf16[1024,512]{1,0:T(8,128)(2,1)}, u32[]{:S(2)}) copy-start(bf16[1024,512]{1,0:T(8,128)(2,1)} %param.13) | copy-start | bytes 3145732

commit v2 on v1

--- a/solution.py
+++ b/solution.py
@@ -1,3 +1,5 @@
+import functools
+
 import jax
 import jax.numpy as jnp
 from jax import lax
@@ -12,6 +14,7 @@
 NEG = -1e30
 LANES = 128
 STATS = 3 * H
+DIGIT = 32
 VMEM_LIMIT = 58 * 1024 * 1024
 
 
@@ -45,10 +48,15 @@
     return row[:, : row.shape[1] // 2], row[:, row.shape[1] // 2 :]
 
 
-def query_kernel(near_ids, meta, q_ref, cot_ref, tile_ref, k_ref, v_ref, kt_ref, vt_ref, fk_ref,
-                 fv_ref, fkt_ref, fvt_ref, att_ref, dq_ref, acc_ref, stats_ref, slot_ref, p_scr, ds_scr,
-                 qz_scr, cz_scr, bias_scr):
+def query_kernel(first, near_ids, meta, q_ref, cot_ref, tile_ref, k_ref, v_ref, kt_ref, vt_ref, fk_ref,
+                 fv_ref, fkt_ref, fvt_ref, *rest):
+    if first:
+        acc_in = None
+    else:
+        acc_in, rest = rest[0], rest[5:]
+    att_ref, dq_ref, acc_ref, stats_ref, slot_ref, p_scr, ds_scr, qz_scr, cz_scr, bias_scr = rest
     i = pl.program_id(0)
+    block = i if first else i + pl.num_programs(0)
     pairs = q_ref.shape[1] // LANES
     bs = q_ref.shape[0]
     width = q_ref.shape[1]
@@ -56,11 +64,11 @@
 
     @pl.when(i == 0)
     def _():
-        acc_ref[...] = jnp.zeros_like(acc_ref)
+        acc_ref[...] = jnp.zeros_like(acc_ref) if first else acc_in[...]
 
     for j in range(NBR):
         bias_scr[j] = bias_of(tile_ref[0, j])
-    ids = [near_ids[i, j] for j in range(NBR)]
+    ids = [near_ids[block, j] for j in range(NBR)]
     for c in range(pairs):
         cols = slice(c * LANES, (c + 1) * LANES)
         cot = cot_ref[:, cols]
@@ -176,13 +184,14 @@
         dkv_ref[:, vcols] = (acc_ref[0, :, vcols] + dv.astype(BF16).astype(F32)).astype(BF16)
 
 
-def call(kernel, scalars, steps, in_specs, out_specs, out_shape, scratch, flops, touched, name):
+def call(kernel, scalars, steps, in_specs, out_specs, out_shape, scratch, flops, touched, name, aliases={}):
     return pl.pallas_call(
         kernel,
         grid_spec=pltpu.PrefetchScalarGridSpec(
             num_scalar_prefetch=scalars, grid=(steps,), in_specs=in_specs, out_specs=out_specs, scratch_shapes=scratch
         ),
         out_shape=out_shape,
+        input_output_aliases=aliases,
         compiler_params=pltpu.CompilerParams(dimension_semantics=("arbitrary",), vmem_limit_bytes=VMEM_LIMIT),
         cost_estimate=pl.CostEstimate(flops=flops, bytes_accessed=touched, transcendentals=0),
         name=name,
@@ -207,8 +216,6 @@
     near_ids = jnp.roll((neighbours - base) % blocks, -base, axis=0)
     mine = lax.dynamic_slice_in_dim(partner, base, own, 0)
     meta = jnp.concatenate([base[None].astype(jnp.int32), mine // own])
-    table = lax.all_gather(partner, "dom", axis=0, tiled=True)
-    one_hot = (table[:, None] == jnp.arange(table.shape[0], dtype=jnp.int32)[None, :]).astype(BF16)
 
     w_by = w_qkv.reshape(width, groups, 3, span).transpose(2, 0, 1, 3).reshape(3, width, width)
     w_all = jnp.concatenate([w_by[0] * jnp.asarray(0.125, BF16), w_by[1], w_by[2]], axis=1)
@@ -219,70 +226,99 @@
     def exchange(x):
         return lax.all_to_all(x, DEVICES, split_axis=0, concat_axis=0, tiled=True)
 
-    def far(x):
-        spread = exchange(x.reshape(own, bs, width).transpose(1, 0, 2))
-        picked = jnp.dot(one_hot, spread.reshape(-1, width), preferred_element_type=F32).astype(BF16)
-        back = exchange(picked.reshape(devices, own, width))
-        return back.transpose(1, 0, 2).reshape(rows, width)
-
+    def spread(x):
+        return x.reshape(own, bs, width).transpose(1, 0, 2)
+
+    def gathered(x):
+        return jnp.dot(one_hot, x.reshape(-1, width), preferred_element_type=F32).astype(BF16).reshape(
+            devices, own, width
+        )
+
+    digits = jnp.stack([mine // DIGIT, mine % DIGIT], axis=1).astype(BF16)
+    digits = jnp.pad(digits, ((0, 0), (0, LANES - 2)))
+    digits = jnp.broadcast_to(digits[None], (devices, own, LANES))
+    rows_in = exchange(jnp.concatenate([spread(node_feats), digits], axis=2))
+    peer_feats = swap(node_feats)
     cot = jnp.dot(layer_cot, w_out.T, preferred_element_type=F32).astype(BF16)
-    far_feats = far(node_feats)
-    peer_feats = swap(node_feats)
-    far_cot = far(cot)
-    peer_cot = swap(cot)
+    ids = rows_in[:, :, width].astype(F32) * DIGIT + rows_in[:, :, width + 1].astype(F32)
+    ids = ids.astype(jnp.int32).reshape(-1)
+    one_hot = (ids[:, None] == jnp.arange(ids.shape[0], dtype=jnp.int32)[None, :]).astype(BF16)
+    far_rows = exchange(gathered(rows_in[:, :, :width]))
 
     part_feats = jnp.concatenate([node_feats, peer_feats], axis=0)
     part_qkv = jnp.dot(part_feats, w_all, preferred_element_type=F32).astype(BF16)
-    far_qkv = jnp.dot(far_feats, w_all, preferred_element_type=F32).astype(BF16)
 
     def turned(feats):
         flat = jnp.einsum("dc,brd->bcr", w_all[:, width:], feats.reshape(-1, bs, width), preferred_element_type=F32)
         return flat.astype(BF16)
 
-    part_t, far_t = turned(part_feats), turned(far_feats)
+    part_t = turned(part_feats)
+    far_rows, part_qkv, part_t, cot = lax.optimization_barrier((far_rows, part_qkv, part_t, cot))
+    far_feats = far_rows.transpose(1, 0, 2).reshape(rows, width)
+    cot_in = exchange(spread(cot))
+    peer_cot = swap(cot)
+    far_qkv = jnp.dot(far_feats, w_all, preferred_element_type=F32).astype(BF16)
+    far_t = turned(far_feats)
     part_blk = part_qkv.reshape(blocks, bs, 3 * width)
     far_blk = far_qkv.reshape(own, bs, 3 * width)
 
     step = lambda i, *s: (i, 0)
     pair_flops = 2 * bs * bs * width * 2
-    att, dq, acc, stats, slots = call(
-        query_kernel, 2, own,
-        [
-            pl.BlockSpec((bs, width), step),
-            pl.BlockSpec((bs, width), step),
-            pl.BlockSpec((1, NBR, bs, bs), lambda i, ids, meta: (meta[0] + i, 0, 0, 0)),
-            pl.BlockSpec((blocks, bs, width), lambda i, *s: (0, 0, 1), pipeline_mode=pl.Buffered(1)),
-            pl.BlockSpec((blocks, bs, width), lambda i, *s: (0, 0, 2), pipeline_mode=pl.Buffered(1)),
-            pl.BlockSpec((blocks, width, bs), lambda i, *s: (0, 0, 0), pipeline_mode=pl.Buffered(1)),
-            pl.BlockSpec((blocks, width, bs), lambda i, *s: (0, 1, 0), pipeline_mode=pl.Buffered(1)),
-            pl.BlockSpec((1, bs, width), lambda i, *s: (i, 0, 1)),
-            pl.BlockSpec((1, bs, width), lambda i, *s: (i, 0, 2)),
-            pl.BlockSpec((1, width, bs), lambda i, *s: (i, 0, 0)),
-            pl.BlockSpec((1, width, bs), lambda i, *s: (i, 1, 0)),
-        ],
-        [
-            pl.BlockSpec((bs, width), step),
-            pl.BlockSpec((bs, width), step),
-            pl.BlockSpec((own, bs, 2 * width), lambda i, *s: (0, 0, 0)),
-            pl.BlockSpec((1, STATS, bs), lambda i, *s: (i, 0, 0)),
-            pl.BlockSpec((1, STATS, bs), lambda i, ids, meta: (meta[1 + i], 0, 0)),
-        ],
-        [
-            jax.ShapeDtypeStruct((rows, width), BF16),
-            jax.ShapeDtypeStruct((rows, width), BF16),
-            jax.ShapeDtypeStruct((own, bs, 2 * width), F32),
-            jax.ShapeDtypeStruct((own, STATS, bs), F32),
-            jax.ShapeDtypeStruct((devices, STATS, bs), F32),
-        ],
-        [
-            pltpu.VMEM((width // LANES, NBR * bs, 2 * bs), BF16),
-            pltpu.VMEM((width // LANES, NBR * bs, 2 * bs), BF16),
-            pltpu.VMEM((width // LANES, 2 * bs, LANES), BF16),
-            pltpu.VMEM((width // LANES, 2 * bs, LANES), BF16),
-            pltpu.VMEM((NBR, bs, 2 * bs), F32),
-        ],
-        own * 40 * pair_flops, 30 << 20, "own_queries",
-    )(near_ids, meta, part_qkv, cot, tiles, part_blk, part_blk, part_t, part_t, far_blk, far_blk, far_t, far_t)
+    hold = pl.BlockSpec(memory_space=pl.ANY)
+
+    def own_queries(first, carried=()):
+        steps = own // 2
+        off = 0 if first else steps
+        at = lambda i, *s: (off + i, 0)
+        return call(
+            functools.partial(query_kernel, first), 2, steps,
+            [
+                pl.BlockSpec((bs, width), at),
+                pl.BlockSpec((bs, width), at),
+                pl.BlockSpec((1, NBR, bs, bs), lambda i, ids, meta: (meta[0] + off + i, 0, 0, 0)),
+                pl.BlockSpec((blocks, bs, width), lambda i, *s: (0, 0, 1), pipeline_mode=pl.Buffered(1)),
+                pl.BlockSpec((blocks, bs, width), lambda i, *s: (0, 0, 2), pipeline_mode=pl.Buffered(1)),
+                pl.BlockSpec((blocks, width, bs), lambda i, *s: (0, 0, 0), pipeline_mode=pl.Buffered(1)),
+                pl.BlockSpec((blocks, width, bs), lambda i, *s: (0, 1, 0), pipeline_mode=pl.Buffered(1)),
+                pl.BlockSpec((1, bs, width), lambda i, *s: (off + i, 0, 1)),
+                pl.BlockSpec((1, bs, width), lambda i, *s: (off + i, 0, 2)),
+                pl.BlockSpec((1, width, bs), lambda i, *s: (off + i, 0, 0)),
+                pl.BlockSpec((1, width, bs), lambda i, *s: (off + i, 1, 0)),
+            ]
+            + ([] if first else [once((own, bs, 2 * width)), hold, hold, hold, hold]),
+            [
+                pl.BlockSpec((bs, width), at),
+                pl.BlockSpec((bs, width), at),
+                pl.BlockSpec((own, bs, 2 * width), lambda i, *s: (0, 0, 0)),
+                pl.BlockSpec((1, STATS, bs), lambda i, *s: (off + i, 0, 0)),
+                pl.BlockSpec((1, STATS, bs), lambda i, ids, meta: (meta[1 + off + i], 0, 0)),
+            ],
+            [
+                jax.ShapeDtypeStruct((rows, width), BF16),
+                jax.ShapeDtypeStruct((rows, width), BF16),
+                jax.ShapeDtypeStruct((own, bs, 2 * width), F32),
+                jax.ShapeDtypeStruct((own, STATS, bs), F32),
+                jax.ShapeDtypeStruct((devices, STATS, bs), F32),
+            ],
+            [
+                pltpu.VMEM((width // LANES, NBR * bs, 2 * bs), BF16),
+                pltpu.VMEM((width // LANES, NBR * bs, 2 * bs), BF16),
+                pltpu.VMEM((width // LANES, 2 * bs, LANES), BF16),
+                pltpu.VMEM((width // LANES, 2 * bs, LANES), BF16),
+                pltpu.VMEM((NBR, bs, 2 * bs), F32),
+            ],
+            steps * 40 * pair_flops, 30 << 20, "own_first" if first else "own_second",
+            aliases={} if first else {13: 2, 14: 0, 15: 1, 16: 3, 17: 4},
+        )(near_ids, meta, part_qkv, cot, tiles, part_blk, part_blk, part_t, part_t, far_blk, far_blk, far_t, far_t,
+          *carried)
+
+    att, dq, acc, stats, slots = own_queries(True)
+    acc, cot_in = lax.optimization_barrier((acc, cot_in))
+    picked, acc = lax.optimization_barrier((gathered(cot_in), acc))
+    far_cot = exchange(picked)
+    att, dq, acc, stats, slots = own_queries(False, (acc, att, dq, stats, slots))
+    far_cot, slots = lax.optimization_barrier((far_cot, slots))
+    far_cot = far_cot.transpose(1, 0, 2).reshape(rows, width)
 
     peer_stats = swap(stats)
     far_slots = exchange(slots)
@@ -290,15 +326,6 @@
     layer_out = jnp.dot(att, w_out, preferred_element_type=F32).astype(BF16)
     dwo_t = jnp.einsum("rc,ra->ca", layer_cot, att, preferred_element_type=F32).astype(BF16)
     dwq = jnp.einsum("rd,rc->dc", node_feats, dq, preferred_element_type=F32).astype(BF16)
-
-    def pieces(w):
-        return w.reshape(doms, width // doms, groups, span).transpose(0, 2, 1, 3).reshape(devices, width // doms, span)
-
-    def summed(ws):
-        moved = exchange(jnp.concatenate([pieces(w) for w in ws], axis=2))
-        return jnp.sum(moved.astype(F32), axis=0)
-
-    early = summed([dwo_t, dwq])
 
     (acc,) = call(
         peer_kernel, 2, own,
@@ -336,14 +363,19 @@
     )(meta, far_qkv, far_cot, far_slots, part_blk, part_blk, acc)
 
     dwkv = jnp.einsum("rd,rc->dc", node_feats, dkv, preferred_element_type=F32).astype(BF16)
-    late = summed([dwkv[:, :width], dwkv[:, width:]])
+    parts = [w.reshape(doms, width // doms, width) for w in (dwo_t, dwq, dwkv[:, :width], dwkv[:, width:])]
+    split = jnp.stack(
+        [jnp.concatenate([w[:, :, g * span : (g + 1) * span] for w in parts], axis=2) for g in range(groups)], axis=1
+    )
+    moved = exchange(split.reshape(devices, width // doms, 4 * span))
+    summed = jnp.sum(moved.astype(F32), axis=0)
     w_plain = w_by.transpose(1, 0, 2).reshape(width, 3 * width)
     feat_grad = (
         lax.dot_general(dq, w_plain[:, :width], (((1,), (1,)), ((), ())), preferred_element_type=F32)
         + lax.dot_general(dkv, w_plain[:, width:], (((1,), (1,)), ((), ())), preferred_element_type=F32)
     ).astype(BF16)
-    dw_out = early[:, :span].T
-    dw_qkv = jnp.concatenate([early[:, span:], late], axis=1)
+    dw_out = summed[:, :span].T
+    dw_qkv = summed[:, span:]
     return (layer_out, feat_grad, dw_qkv, dw_out)
 
 

time: 311 us -> 305 us (0.981)
  starting transfers between devices: 111 us -> 64.2 us
  waiting for transfers between devices: 32 us -> 76.2 us
  blocking collectives: 19.4 us -> 0 us
  Pallas kernels: 72.1 us -> 84.7 us
    ppermute x3, waiting for transfers between devices: 0.01 us -> 49.3 us  [swap(): return lax.ppermute(x, 'head', [(0, 1), (1, 0)])]
    all_to_all x7 -> x6, starting transfers between devices: 105 us -> 56.5 us  [exchange(): return lax.all_to_all(x, DEVICES, split_axis=0, concat_axis=0, tiled=True)]
    unnamed x1 -> x0, blocking collectives: 19.4 us -> none
    pallas_call x1 -> x2, Pallas kernels: 40.8 us -> 50.7 us  [own_queries(): call(functools.partial(query_kernel, first), 2, steps, [pl.BlockSpec((bs,...]
    all_to_all x7 -> x6, waiting for transfers between devices: 32 us -> 26.9 us  [exchange(): return lax.all_to_all(x, DEVICES, split_axis=0, concat_axis=0, tiled=True)]
    transpose x7 -> x2, local copies, waits for them, and re-layouts: 6.34 us -> 3.1 us  [the longest x1 2.5 us: body(): far_cot = far_cot.transpose(1, 0, 2).reshape(rows, width)]
  transfers between devices with their start and end apart: 10 -> 9, of which waited for: 4 -> 5; matrix products, arithmetic and copies ran while one was open for 21% -> 17% of each run, Pallas kernels for 23% -> 24%
where the time goes in v2:
time: 305 us; the launch traced here: 303 us
  Pallas kernels  84.7 us (28%)
  waiting for transfers between devices  76.2 us (25%)
  starting transfers between devices  64.2 us (21%)
  matrix products  40.5 us (13%)
  local copies, waits for them, and re-layouts  28.5 us (9%)
  other arithmetic  7.66 us (3%)
    all_to_all x6, starting transfers between devices, exchange(): return lax.all_to_all(x, DEVICES, split_axis=0, concat_axis=0, tiled=True)  56.5 us
    pallas_call x2, Pallas kernels, own_queries(): call(functools.partial(query_kernel, first), 2, steps, [pl.BlockSpec((bs,...  50.7 us
    ppermute x3, waiting for transfers between devices, swap(): return lax.ppermute(x, 'head', [(0, 1), (1, 0)])  49.3 us
    all_to_all x6, waiting for transfers between devices, exchange(): return lax.all_to_all(x, DEVICES, split_axis=0, concat_axis=0, tiled=True)  26.9 us
    pallas_call x1, Pallas kernels, body(): call(peer_kernel, 2, own, [pl.BlockSpec((bs, width), lambda i, *s: (own +...  22.4 us
    pallas_call x1, Pallas kernels, body(): call(far_kernel, 1, own, [pl.BlockSpec((bs, width), step), pl.BlockSpec((...  11.5 us
    dot_general x2, matrix products, turned(): jnp.einsum('dc,brd->bcr', w_all[:, width:], feats.reshape(-1, bs, width),...  10.4 us
    unnamed x46, local copies, waits for them, and re-layouts  8.71 us
  transfers between devices with their start and end apart: 9, of which 5 were waited for; matrix products, arithmetic and copies ran while one was open for 17% of the time, Pallas kernels for 24%

profile of v2, /device:TPU:0, one launch (start us, length us, event | category | flops | bytes accessed | tf_op | source)
XLA Modules:
  0.0 302.6 jit_solution(59134359988865903)
XLA Ops:
  0.6 4.0 %collective-permute-start = (bf16[1024,512]{1,0:T(8,128)(2,1)}, bf16[1024,512]{1,0:T(8,128)(2,1)}, u32[]{:S(2)}, u32[]{:S(2)}) collective-permute-start(bf16[1024,512]{1,0:T(8,128)(2,1)} %param.7), channel_id=1, source_target_pairs={{0,1},{1,0},{2,3},{3,2},{4,5},{5,4},{6,7},{7,6},{8,9},{9,8},{10,11... | collective-permute-start | bytes 3145736 | tf_op jit(solution)/shard_map/ppermute | solution.py:224
  8.8 8.5 %all-to-all-start = ((bf16[128,8,640]{2,1,0:T(8,128)(2,1)}), bf16[128,8,640]{2,1,0:T(8,128)(2,1)}, u32[]{:S(2)}, u32[]{:S(2)}) async-start(bf16[128,8,640]{2,1,0:T(8,128)(2,1)} %copy.80), calls=%async_computation | async-start | bytes 2621440 | tf_op jit(solution)/shard_map/all_to_all | solution.py:227
  20.1 2.1 copy.98
  22.2 2.0 copy.99
  26.7 2.3 constant_dynamic-update-slice_fusion.1
  30.7 11.3 %collective-permute-done = bf16[1024,512]{1,0:T(8,128)(2,1)} collective-permute-done((bf16[1024,512]{1,0:T(8,128)(2,1)}, bf16[1024,512]{1,0:T(8,128)(2,1)}, u32[]{:S(2)}, u32[]{:S(2)}) %collective-permute-start) | collective-permute-done | bytes 1048608 | tf_op jit(solution)/shard_map/ppermute | solution.py:224
  42.0 2.3 constant_dynamic-update-slice_fusion
  46.1 3.5 %fusion.8 = bf16[128,8,512]{2,1,0:T(8,128)(2,1)} fusion(s32[1024]{0:T(1024)S(1)} %convert_element_type.86, bf16[128,8,640]{2,1,0:T(8,128)(2,1)} %all-to-all-done), kind=kOutput, calls=%fused_computation.20 | convolution fusion | flops 1075314688 | bytes 2101248 | tf_op jit(solution)/shard_map/dot_general | solution.py:233
  49.6 11.2 %all-to-all-start.1 = ((bf16[128,8,512]{2,1,0:T(8,128)(2,1)}), bf16[128,8,512]{2,1,0:T(8,128)(2,1)}, u32[]{:S(2)}, u32[]{:S(2)}) async-start(bf16[128,8,512]{2,1,0:T(8,128)(2,1)} %fusion.8), calls=%async_computation.1 | async-start | bytes 2097152 | tf_op jit(solution)/shard_map/all_to_all | solution.py:227
  60.8 6.2 %convert_bitcast_fusion.kt_ref.vt_ref = bf16[16,1024,128]{2,1,0:T(8,128)(2,1)} fusion(bf16[16,128,512]{2,1,0:T(8,128)(2,1)} %bitcast.13, bf16[512,512]{1,0:T(8,128)(2,1)} %copy.99, bf16[512,512]{1,0:T(8,128)(2,1)S(1)} %copy-done.10), kind=kOutput, calls=%fused_computation.2 | convolution fusion | flops 2151677952 | bytes 7340032 | tf_op jit(solution)/shard_map/dc,brd->bcr/dot_general | solution.py:252
  67.1 7.3 %convolution_convert_fusion.q_ref = bf16[2048,1536]{1,0:T(8,128)(2,1)} fusion(bf16[2048,512]{1,0:T(8,128)(2,1)} %constant_dynamic-update-slice_fusion, bf16[512,512]{1,0:T(8,128)(2,1)S(1)} %copy-done.11, bf16[512,512]{1,0:T(8,128)(2,1)S(1)} %copy-done.10, bf16[512,512]{1,0:T(8,128)(2,1)S(1)} %copy-done.13), kind=kOutput, calls=%fused_computation | convolution fusion | flops 3229089792 | bytes 9961472 | tf_op jit(solution)/shard_map/dot_general | solution.py:249
  74.4 4.6 %all-to-all-done.1 = bf16[128,8,512]{2,1,0:T(8,128)(2,1)} async-done(((bf16[128,8,512]{2,1,0:T(8,128)(2,1)}), bf16[128,8,512]{2,1,0:T(8,128)(2,1)}, u32[]{:S(2)}, u32[]{:S(2)}) %all-to-all-start.1) | async-done | bytes 1048608 | tf_op jit(solution)/shard_map/all_to_all | solution.py:227
  78.9 2.6 copy.89
  83.1 5.9 %all-to-all-start.2 = ((bf16[128,8,512]{2,1,0:T(8,128)(2,1)}), bf16[128,8,512]{2,1,0:T(8,128)(2,1)}, u32[]{:S(2)}, u32[]{:S(2)}) async-start(bf16[128,8,512]{2,1,0:T(8,128)(2,1)} %bitcast.108), calls=%async_computation.2 | async-start | bytes 2097152 | tf_op jit(solution)/shard_map/all_to_all | solution.py:227
  89.1 4.2 %convert_bitcast_fusion.1.fkt_ref.fvt_ref = bf16[8,1024,128]{2,1,0:T(8,128)(2,1)} fusion(bf16[512,512]{1,0:T(8,128)(2,1)} %copy.99, bf16[512,512]{1,0:T(8,128)(2,1)S(1)} %copy-done.10, bf16[128,8,512]{2,1,0:T(8,128)(2,1)} %all-to-all-done.1), kind=kOutput, calls=%fused_computation.9 | convolution fusion | flops 1076887552 | bytes 4194304 | tf_op jit(solution)/shard_map/dc,brd->bcr/dot_general | solution.py:252
  93.3 3.4 %convolution_convert_fusion.1.q_ref = bf16[1024,1536]{1,0:T(8,128)(2,1)} fusion(bf16[1024,512]{1,0:T(8,128)(2,1)S(1)} %bitcast.115, bf16[512,512]{1,0:T(8,128)(2,1)S(1)} %copy-done.12, bf16[512,512]{1,0:T(8,128)(2,1)S(1)} %copy-done.10, bf16[512,512]{1,0:T(8,128)(2,1)S(1)} %copy-done.14), kind=kOutput, calls=%fused_computation.6 | convolution fusion | flops 1616904192 | bytes 5767168 | tf_op jit(solution)/shard_map/dot_general | solution.py:260
  96.8 24.9 %own_first.1 = (bf16[1024,512]{1,0:T(8,128)(2,1)}, bf16[1024,512]{1,0:T(8,128)(2,1)}, f32[8,128,1024]{2,1,0:T(8,128)}, f32[8,24,128]{2,1,0:T(8,128)}, f32[128,24,128]{2,1,0:T(8,128)}) custom-call(s32[16,4]{1,0:T(8,128)} %copy.100.near_ids, s32[9]{0:T(128)} %pad_add_fusion.1.meta, bf16[2048,1536]{1,0:T(8,128)(2,1)} %convolution_convert_fusion.q_ref, ...), custom_call_target="tpu_custom_call" | custom-call | flops 5368709120 | bytes 31457280 | tf_op jit(solution)/shard_map/own_first/pallas_call | solution.py:273
  121.7 3.5 %fusion.7 = bf16[128,8,512]{2,1,0:T(8,128)(2,1)} fusion(s32[1024]{0:T(1024)S(1)} %convert_element_type.86, bf16[128,8,512]{2,1,0:T(8,128)(2,1)} %all-to-all-done.2), kind=kOutput, calls=%fused_computation.19 | convolution fusion | flops 1075314688 | bytes 2101248 | tf_op jit(solution)/shard_map/dot_general | solution.py:233
  125.2 9.9 %all-to-all-start.3 = ((bf16[128,8,512]{2,1,0:T(8,128)(2,1)}), bf16[128,8,512]{2,1,0:T(8,128)(2,1)}, u32[]{:S(2)}, u32[]{:S(2)}) async-start(bf16[128,8,512]{2,1,0:T(8,128)(2,1)} %fusion.7), calls=%async_computation.3 | async-start | bytes 2097152 | tf_op jit(solution)/shard_map/all_to_all | solution.py:227
  135.1 25.8 %own_second.1 = (bf16[1024,512]{1,0:T(8,128)(2,1)}, bf16[1024,512]{1,0:T(8,128)(2,1)}, f32[8,128,1024]{2,1,0:T(8,128)}, f32[8,24,128]{2,1,0:T(8,128)}, f32[128,24,128]{2,1,0:T(8,128)}) custom-call(s32[16,4]{1,0:T(8,128)} %copy.100.near_ids, s32[9]{0:T(128)} %pad_add_fusion.1.meta, ...), custom_call_target="tpu_custom_call", output_to_operand_aliasing={{2}: (13, {}), {0}: (14, {}), {1}: (15, {}), {3}: (16, {}),... | custom-call | flops 5368709120 | bytes 31457280 | tf_op jit(solution)/shard_map/own_second/pallas_call | solution.py:273
  161.0 10.7 %all-to-all-start.4 = ((f32[128,24,128]{2,1,0:T(8,128)}), f32[128,24,128]{2,1,0:T(8,128)}, u32[]{:S(2)}, u32[]{:S(2)}) async-start(f32[128,24,128]{2,1,0:T(8,128)} %get-tuple-element.41), calls=%async_computation.4 | async-start | bytes 3145728 | tf_op jit(solution)/shard_map/all_to_all | solution.py:227
  171.7 2.9 collective-permute-start.1
  175.3 2.4 fusion.10
  179.2 36.5 %collective-permute-done.1.cot_ref = bf16[1024,512]{1,0:T(8,128)(2,1)S(1)} collective-permute-done((bf16[1024,512]{1,0:T(8,128)(2,1)}, bf16[1024,512]{1,0:T(8,128)(2,1)S(1)}, u32[]{:S(2)}, u32[]{:S(2)}) %collective-permute-start.1) | collective-permute-done | bytes 1048608 | tf_op jit(solution)/shard_map/ppermute | solution.py:224
  217.9 22.4 %peer_queries.1.acc_ref = f32[8,128,1024]{2,1,0:T(8,128)} custom-call(s32[16,4]{1,0:T(8,128)} %copy.100.near_ids, s32[9]{0:T(128)} %pad_add_fusion.1.meta, bf16[2048,1536]{1,0:T(8,128)(2,1)} %convolution_convert_fusion.q_ref, bf16[1024,512]{1,0:T(8,128)(2,1)} %copy-done.7, f32[8,24,128]{2,1,0:T(8,128)} %copy-done.16, s32[16,4,128,128]{3,2,1,0:T(8,128)} %tile_ref.5, ...), custom_call_target="tpu_custom_call" | custom-call | flops 4294967296 | bytes 20971520 | tf_op jit(solution)/shard_map/peer_queries/pallas_call | solution.py:330
  240.4 2.5 copy.93
  242.9 11.5 %far_queries.1 = bf16[1024,1024]{1,0:T(8,128)(2,1)} custom-call(s32[9]{0:T(128)} %pad_add_fusion.1.meta, bf16[1024,1536]{1,0:T(8,128)(2,1)} %convolution_convert_fusion.1.q_ref, bf16[1024,512]{1,0:T(8,128)(2,1)} %bitcast.109, f32[128,24,128]{2,1,0:T(8,128)} %all-to-all-done.4.stats_ref, bf16[16,128,1536]{2,1,0:T(8,128)(2,1)} %bitcast.97, ...), custom_call_target="tpu_custom_call" | custom-call | flops 2147483648 | bytes 10485760 | tf_op jit(solution)/shard_map/far_queries/pallas_call | solution.py:350
  254.4 2.9 fusion.6
  260.0 10.3 %all-to-all-start.5 = ((bf16[128,8,1024]{2,1,0:T(8,128)(2,1)}), bf16[128,8,1024]{2,1,0:T(8,128)(2,1)}, u32[]{:S(2)}, u32[]{:S(2)}) async-start(bf16[128,8,1024]{2,1,0:T(8,128)(2,1)} %bitcast.106), calls=%async_computation.5 | async-start | bytes 4194304 | tf_op jit(solution)/shard_map/all_to_all | solution.py:227
  275.0 2.2 add_convert_fusion
  277.2 22.3 %all-to-all-done.5 = bf16[128,8,1024]{2,1,0:T(8,128)(2,1)} async-done(((bf16[128,8,1024]{2,1,0:T(8,128)(2,1)}), bf16[128,8,1024]{2,1,0:T(8,128)(2,1)}, u32[]{:S(2)}, u32[]{:S(2)}) %all-to-all-start.5) | async-done | bytes 2097184 | tf_op jit(solution)/shard_map/all_to_all | solution.py:227
  299.5 2.0 convert_reduce_fusion
  (82 shorter events, 27.5 us)
Async XLA Ops:
  0.6 28.4 %copy-start = (bf16[1024,512]{1,0:T(8,128)(2,1)S(1)}, bf16[1024,512]{1,0:T(8,128)(2,1)}, u32[]{:S(2)}) copy-start(bf16[1024,512]{1,0:T(8,128)(2,1)} %param.13) | copy-start | bytes 3145732
  0.6 41.3 %collective-permute-start = (bf16[1024,512]{1,0:T(8,128)(2,1)}, bf16[1024,512]{1,0:T(8,128)(2,1)}, u32[]{:S(2)}, u32[]{:S(2)}) collective-permute-start(bf16[1024,512]{1,0:T(8,128)(2,1)} %param.7), channel_id=1, source_target_pairs={{0,1},{1,0},{2,3},{3,2},{4,5},{5,4},{6,7},{7,6},{8,9},{9,8},{10,11... | collective-permute-start | bytes 3145736 | tf_op jit(solution)/shard_map/ppermute | solution.py:224
  8.8 35.5 %all-to-all-start = ((bf16[128,8,640]{2,1,0:T(8,128)(2,1)}), bf16[128,8,640]{2,1,0:T(8,128)(2,1)}, u32[]{:S(2)}, u32[]{:S(2)}) async-start(bf16[128,8,640]{2,1,0:T(8,128)(2,1)} %copy.80), calls=%async_computation | async-start | bytes 2621440 | tf_op jit(solution)/shard_map/all_to_all | solution.py:227
  20.1 5.1 %copy-start.17 = (s32[16,4]{0,1:T(4,128)S(1)}, s32[16,4]{0,1:T(4,128)}, u32[]{:S(2)}) copy-start(s32[16,4]{0,1:T(4,128)} %param.10) | copy-start | bytes 772
  25.2 3.8 %copy-start.18 = (bf16[512,512]{1,0:T(8,128)(2,1)S(1)}, bf16[512,512]{1,0:T(8,128)(2,1)}, u32[]{:S(2)}) copy-start(bf16[512,512]{1,0:T(8,128)(2,1)} %param.9) | copy-start | bytes 1572868
  49.6 11.2 %copy-start.10 = (bf16[512,512]{1,0:T(8,128)(2,1)S(1)}, bf16[512,512]{1,0:T(8,128)(2,1)}, u32[]{:S(2)}) copy-start(bf16[512,512]{1,0:T(8,128)(2,1)} %copy.98) | copy-start | bytes 1572868
  49.6 29.3 %all-to-all-start.1 = ((bf16[128,8,512]{2,1,0:T(8,128)(2,1)}), bf16[128,8,512]{2,1,0:T(8,128)(2,1)}, u32[]{:S(2)}, u32[]{:S(2)}) async-start(bf16[128,8,512]{2,1,0:T(8,128)(2,1)} %fusion.8), calls=%async_computation.1 | async-start | bytes 2097152 | tf_op jit(solution)/shard_map/all_to_all | solution.py:227
  60.8 6.2 %copy-start.11 = (bf16[512,512]{1,0:T(8,128)(2,1)S(1)}, bf16[512,512]{1,0:T(8,128)(2,1)}, u32[]{:S(2)}) copy-start(bf16[512,512]{1,0:T(8,128)(2,1)} %copy.99) | copy-start | bytes 1572868
  60.8 6.2 %copy-start.13 = (bf16[512,512]{1,0:T(8,128)(2,1)S(1)}, bf16[512,512]{1,0:T(8,128)(2,1)}, u32[]{:S(2)}) copy-start(bf16[512,512]{1,0:T(8,128)(2,1)} %copy.97) | copy-start | bytes 1572868
  78.9 2.6 copy-start.1
  83.1 38.5 %all-to-all-start.2 = ((bf16[128,8,512]{2,1,0:T(8,128)(2,1)}), bf16[128,8,512]{2,1,0:T(8,128)(2,1)}, u32[]{:S(2)}, u32[]{:S(2)}) async-start(bf16[128,8,512]{2,1,0:T(8,128)(2,1)} %bitcast.108), calls=%async_computation.2 | async-start | bytes 2097152 | tf_op jit(solution)/shard_map/all_to_all | solution.py:227
  89.1 4.3 %copy-start.8 = (bf16[128,8,512]{2,0,1:T(8,128)(2,1)S(1)}, bf16[128,8,512]{2,0,1:T(8,128)(2,1)}, u32[]{:S(2)}) copy-start(bf16[128,8,512]{2,0,1:T(8,128)(2,1)} %copy.89) | copy-start | bytes 3145732
  89.1 4.3 %copy-start.12 = (bf16[512,512]{1,0:T(8,128)(2,1)S(1)}, bf16[512,512]{1,0:T(8,128)(2,1)}, u32[]{:S(2)}) copy-start(bf16[512,512]{1,0:T(8,128)(2,1)} %copy.99) | copy-start | bytes 1572868
  89.1 4.2 %copy-start.14 = (bf16[512,512]{1,0:T(8,128)(2,1)S(1)}, bf16[512,512]{1,0:T(8,128)(2,1)}, u32[]{:S(2)}) copy-start(bf16[512,512]{1,0:T(8,128)(2,1)} %copy.97) | copy-start | bytes 1572868
  125.2 35.8 %all-to-all-start.3 = ((bf16[128,8,512]{2,1,0:T(8,128)(2,1)}), bf16[128,8,512]{2,1,0:T(8,128)(2,1)}, u32[]{:S(2)}, u32[]{:S(2)}) async-start(bf16[128,8,512]{2,1,0:T(8,128)(2,1)} %fusion.7), calls=%async_computation.3 | async-start | bytes 2097152 | tf_op jit(solution)/shard_map/all_to_all | solution.py:227
  160.9 13.6 %copy-start.15 = (f32[8,24,128]{2,1,0:T(8,128)S(1)}, f32[8,24,128]{2,1,0:T(8,128)}, u32[]{:S(2)}) copy-start(f32[8,24,128]{2,1,0:T(8,128)} %get-tuple-element.42) | copy-start | bytes 294916
  161.0 81.9 %all-to-all-start.4 = ((f32[128,24,128]{2,1,0:T(8,128)}), f32[128,24,128]{2,1,0:T(8,128)}, u32[]{:S(2)}, u32[]{:S(2)}) async-start(f32[128,24,128]{2,1,0:T(8,128)} %get-tuple-element.41), calls=%async_computation.4 | async-start | bytes 3145728 | tf_op jit(solution)/shard_map/all_to_all | solution.py:227
  171.7 44.1 %collective-permute-start.1 = (bf16[1024,512]{1,0:T(8,128)(2,1)}, bf16[1024,512]{1,0:T(8,128)(2,1)S(1)}, u32[]{:S(2)}, u32[]{:S(2)}) collective-permute-start(bf16[1024,512]{1,0:T(8,128)(2,1)} %convolution_convert_fusion.4.cot_ref), channel_id=1, source_target_pairs={{0,1},{1,0},{2,3},{3,2},{4,5},{5,4},{6,7},{7,6},{8,9},{9,8},{10,11... | collective-permute-start | bytes 3145736 | tf_op jit(solution)/shard_map/ppermute | solution.py:224
  174.6 42.7 %collective-permute-start.2 = (f32[8,24,128]{2,1,0:T(8,128)S(1)}, f32[8,24,128]{2,1,0:T(8,128)S(1)}, u32[]{:S(2)}, u32[]{:S(2)}) collective-permute-start(f32[8,24,128]{2,1,0:T(8,128)S(1)} %copy-done.15), channel_id=1, source_target_pairs={{0,1},{1,0},{2,3},{3,2},{4,5},{5,4},{6,7},{7,6},{8,9},{9,8},{10,11... | collective-permute-start | bytes 294920 | tf_op jit(solution)/shard_map/ppermute | solution.py:224
  175.3 2.4 copy-start.5
  215.8 1.5 copy-start.7
  217.3 0.6 copy-start.16
  242.9 11.5 %copy-start.3 = (bf16[1024,512]{1,0:T(8,128)(2,1)S(1)}, bf16[1024,512]{1,0:T(8,128)(2,1)}, u32[]{:S(2)}) copy-start(bf16[1024,512]{1,0:T(8,128)(2,1)} %param.7) | copy-start | bytes 3145732
  257.3 1.0 copy-start.9
  260.0 39.4 %all-to-all-start.5 = ((bf16[128,8,1024]{2,1,0:T(8,128)(2,1)}), bf16[128,8,1024]{2,1,0:T(8,128)(2,1)}, u32[]{:S(2)}, u32[]{:S(2)}) async-start(bf16[128,8,1024]{2,1,0:T(8,128)(2,1)} %bitcast.106), calls=%async_computation.5 | async-start | bytes 4194304 | tf_op jit(solution)/shard_map/all_to_all | solution.py:227
  270.3 1.2 copy-start.6
  270.3 1.3 copy-start.19
  271.7 1.7 copy-start.2
  273.4 1.6 copy-start.4

commit v3 on v2

--- a/solution.py
+++ b/solution.py
@@ -1,5 +1,3 @@
-import functools
-
 import jax
 import jax.numpy as jnp
 from jax import lax
@@ -48,15 +46,10 @@
     return row[:, : row.shape[1] // 2], row[:, row.shape[1] // 2 :]
 
 
-def query_kernel(first, near_ids, meta, q_ref, cot_ref, tile_ref, k_ref, v_ref, kt_ref, vt_ref, fk_ref,
-                 fv_ref, fkt_ref, fvt_ref, *rest):
-    if first:
-        acc_in = None
-    else:
-        acc_in, rest = rest[0], rest[5:]
-    att_ref, dq_ref, acc_ref, stats_ref, slot_ref, p_scr, ds_scr, qz_scr, cz_scr, bias_scr = rest
+def query_kernel(near_ids, meta, q_ref, cot_ref, tile_ref, k_ref, v_ref, kt_ref, vt_ref, fk_ref,
+                 fv_ref, fkt_ref, fvt_ref, att_ref, dq_ref, acc_ref, stats_ref, slot_ref, p_scr, ds_scr,
+                 qz_scr, cz_scr, bias_scr):
     i = pl.program_id(0)
-    block = i if first else i + pl.num_programs(0)
     pairs = q_ref.shape[1] // LANES
     bs = q_ref.shape[0]
     width = q_ref.shape[1]
@@ -64,11 +57,11 @@
 
     @pl.when(i == 0)
     def _():
-        acc_ref[...] = jnp.zeros_like(acc_ref) if first else acc_in[...]
+        acc_ref[...] = jnp.zeros_like(acc_ref)
 
     for j in range(NBR):
         bias_scr[j] = bias_of(tile_ref[0, j])
-    ids = [near_ids[block, j] for j in range(NBR)]
+    ids = [near_ids[i, j] for j in range(NBR)]
     for c in range(pairs):
         cols = slice(c * LANES, (c + 1) * LANES)
         cot = cot_ref[:, cols]
@@ -184,6 +177,14 @@
         dkv_ref[:, vcols] = (acc_ref[0, :, vcols] + dv.astype(BF16).astype(F32)).astype(BF16)
 
 
+def project_kernel(x_ref, w_ref, wt_ref, *rest):
+    qkv_ref, t_ref = rest[-2:]
+    bs = t_ref.shape[2]
+    qkv_ref[...] = nn(x_ref[...], w_ref[...]).astype(BF16)
+    for b in range(t_ref.shape[0]):
+        t_ref[b] = nt(wt_ref[...], x_ref[b * bs : (b + 1) * bs, :]).astype(BF16)
+
+
 def call(kernel, scalars, steps, in_specs, out_specs, out_shape, scratch, flops, touched, name, aliases={}):
     return pl.pallas_call(
         kernel,
@@ -237,61 +238,83 @@
     digits = jnp.stack([mine // DIGIT, mine % DIGIT], axis=1).astype(BF16)
     digits = jnp.pad(digits, ((0, 0), (0, LANES - 2)))
     digits = jnp.broadcast_to(digits[None], (devices, own, LANES))
-    rows_in = exchange(jnp.concatenate([spread(node_feats), digits], axis=2))
-    peer_feats = swap(node_feats)
+    first_hop = jnp.concatenate([spread(node_feats), digits], axis=2)
+    first_hop, feats_out = lax.optimization_barrier((first_hop, node_feats))
+    rows_in = exchange(first_hop)
+    peer_feats = swap(feats_out)
     cot = jnp.dot(layer_cot, w_out.T, preferred_element_type=F32).astype(BF16)
+    cot_rows = spread(cot)
+
+    w_turned = w_all[:, width:].T
+    hold = pl.BlockSpec(memory_space=pl.ANY)
+
+    def project(feats, total, at, carried, name):
+        per = 2
+        return call(
+            project_kernel, 0, own // per,
+            [
+                pl.BlockSpec((per * bs, width), lambda i: (i, 0)),
+                once((width, 3 * width)),
+                once((2 * width, width)),
+            ]
+            + [hold] * len(carried),
+            [
+                pl.BlockSpec((per * bs, 3 * width), lambda i: (at // per + i, 0)),
+                pl.BlockSpec((per, 2 * width, bs), lambda i: (at // per + i, 0, 0)),
+            ],
+            [
+                jax.ShapeDtypeStruct((total * bs, 3 * width), BF16),
+                jax.ShapeDtypeStruct((total, 2 * width, bs), BF16),
+            ],
+            [], 2 * rows * width * 5 * width, 8 << 20, name, aliases={3: 0, 4: 1} if carried else {},
+        )(feats, w_all, w_turned, *carried)
+
+    own_part = project(node_feats, blocks, 0, (), "project_own")
+    rows_in, cot_rows, own_part, peer_feats = lax.optimization_barrier((rows_in, cot_rows, own_part, peer_feats))
+
     ids = rows_in[:, :, width].astype(F32) * DIGIT + rows_in[:, :, width + 1].astype(F32)
     ids = ids.astype(jnp.int32).reshape(-1)
     one_hot = (ids[:, None] == jnp.arange(ids.shape[0], dtype=jnp.int32)[None, :]).astype(BF16)
-    far_rows = exchange(gathered(rows_in[:, :, :width]))
-
-    part_feats = jnp.concatenate([node_feats, peer_feats], axis=0)
-    part_qkv = jnp.dot(part_feats, w_all, preferred_element_type=F32).astype(BF16)
-
-    def turned(feats):
-        flat = jnp.einsum("dc,brd->bcr", w_all[:, width:], feats.reshape(-1, bs, width), preferred_element_type=F32)
-        return flat.astype(BF16)
-
-    part_t = turned(part_feats)
-    far_rows, part_qkv, part_t, cot = lax.optimization_barrier((far_rows, part_qkv, part_t, cot))
-    far_feats = far_rows.transpose(1, 0, 2).reshape(rows, width)
-    cot_in = exchange(spread(cot))
-    peer_cot = swap(cot)
-    far_qkv = jnp.dot(far_feats, w_all, preferred_element_type=F32).astype(BF16)
-    far_t = turned(far_feats)
+    second = jnp.concatenate([gathered(rows_in[:, :, :width]), cot_rows], axis=2)
+    second, cot_out = lax.optimization_barrier((second, cot))
+    second = exchange(second)
+    peer_cot = swap(cot_out)
+    part_qkv, part_t = project(peer_feats, blocks, own, own_part, "project_peer")
+    second, peer_cot, part_qkv, part_t = lax.optimization_barrier((second, peer_cot, part_qkv, part_t))
+
+    picked = gathered(second[:, :, width:])
+    far_feats = second[:, :, :width].transpose(1, 0, 2).reshape(rows, width)
+    picked, far_feats = lax.optimization_barrier((picked, far_feats))
+    far_cot = exchange(picked)
+    far_qkv, far_t = project(far_feats, own, 0, (), "project_far")
     part_blk = part_qkv.reshape(blocks, bs, 3 * width)
     far_blk = far_qkv.reshape(own, bs, 3 * width)
 
     step = lambda i, *s: (i, 0)
     pair_flops = 2 * bs * bs * width * 2
-    hold = pl.BlockSpec(memory_space=pl.ANY)
-
-    def own_queries(first, carried=()):
-        steps = own // 2
-        off = 0 if first else steps
-        at = lambda i, *s: (off + i, 0)
+    def own_queries():
+        at = lambda i, *s: (i, 0)
         return call(
-            functools.partial(query_kernel, first), 2, steps,
+            query_kernel, 2, own,
             [
                 pl.BlockSpec((bs, width), at),
                 pl.BlockSpec((bs, width), at),
-                pl.BlockSpec((1, NBR, bs, bs), lambda i, ids, meta: (meta[0] + off + i, 0, 0, 0)),
+                pl.BlockSpec((1, NBR, bs, bs), lambda i, ids, meta: (meta[0] + i, 0, 0, 0)),
                 pl.BlockSpec((blocks, bs, width), lambda i, *s: (0, 0, 1), pipeline_mode=pl.Buffered(1)),
                 pl.BlockSpec((blocks, bs, width), lambda i, *s: (0, 0, 2), pipeline_mode=pl.Buffered(1)),
                 pl.BlockSpec((blocks, width, bs), lambda i, *s: (0, 0, 0), pipeline_mode=pl.Buffered(1)),
                 pl.BlockSpec((blocks, width, bs), lambda i, *s: (0, 1, 0), pipeline_mode=pl.Buffered(1)),
-                pl.BlockSpec((1, bs, width), lambda i, *s: (off + i, 0, 1)),
-                pl.BlockSpec((1, bs, width), lambda i, *s: (off + i, 0, 2)),
-                pl.BlockSpec((1, width, bs), lambda i, *s: (off + i, 0, 0)),
-                pl.BlockSpec((1, width, bs), lambda i, *s: (off + i, 1, 0)),
-            ]
-            + ([] if first else [once((own, bs, 2 * width)), hold, hold, hold, hold]),
+                pl.BlockSpec((1, bs, width), lambda i, *s: (i, 0, 1)),
+                pl.BlockSpec((1, bs, width), lambda i, *s: (i, 0, 2)),
+                pl.BlockSpec((1, width, bs), lambda i, *s: (i, 0, 0)),
+                pl.BlockSpec((1, width, bs), lambda i, *s: (i, 1, 0)),
+            ],
             [
                 pl.BlockSpec((bs, width), at),
                 pl.BlockSpec((bs, width), at),
                 pl.BlockSpec((own, bs, 2 * width), lambda i, *s: (0, 0, 0)),
-                pl.BlockSpec((1, STATS, bs), lambda i, *s: (off + i, 0, 0)),
-                pl.BlockSpec((1, STATS, bs), lambda i, ids, meta: (meta[1 + off + i], 0, 0)),
+                pl.BlockSpec((1, STATS, bs), lambda i, *s: (i, 0, 0)),
+                pl.BlockSpec((1, STATS, bs), lambda i, ids, meta: (meta[1 + i], 0, 0)),
             ],
             [
                 jax.ShapeDtypeStruct((rows, width), BF16),
@@ -307,16 +330,10 @@
                 pltpu.VMEM((width // LANES, 2 * bs, LANES), BF16),
                 pltpu.VMEM((NBR, bs, 2 * bs), F32),
             ],
-            steps * 40 * pair_flops, 30 << 20, "own_first" if first else "own_second",
-            aliases={} if first else {13: 2, 14: 0, 15: 1, 16: 3, 17: 4},
-        )(near_ids, meta, part_qkv, cot, tiles, part_blk, part_blk, part_t, part_t, far_blk, far_blk, far_t, far_t,
-          *carried)
-
-    att, dq, acc, stats, slots = own_queries(True)
-    acc, cot_in = lax.optimization_barrier((acc, cot_in))
-    picked, acc = lax.optimization_barrier((gathered(cot_in), acc))
-    far_cot = exchange(picked)
-    att, dq, acc, stats, slots = own_queries(False, (acc, att, dq, stats, slots))
+            own * 40 * pair_flops, 30 << 20, "own_queries",
+        )(near_ids, meta, part_qkv, cot, tiles, part_blk, part_blk, part_t, part_t, far_blk, far_blk, far_t, far_t)
+
+    att, dq, acc, stats, slots = own_queries()
     far_cot, slots = lax.optimization_barrier((far_cot, slots))
     far_cot = far_cot.transpose(1, 0, 2).reshape(rows, width)
 

time: 305 us -> 305 us (level)
  matrix products: 40.5 us -> 19.8 us
  waiting for transfers between devices: 76.2 us -> 93.3 us
  Pallas kernels: 84.7 us -> 98.5 us
  starting transfers between devices: 64.2 us -> 55.9 us
  local copies, waits for them, and re-layouts: 28.5 us -> 24.7 us
  other arithmetic: 7.66 us -> 11.3 us
    ppermute x3, waiting for transfers between devices: 49.3 us -> 71 us  [swap(): return lax.ppermute(x, 'head', [(0, 1), (1, 0)])]
    dot_general x4 -> x0, matrix products: 21.2 us -> none  [the longest x2 10.4 us: turned(): jnp.einsum('dc,brd->bcr', w_all[:, width:], feats.reshape(-1, bs, width),...]
    pallas_call x2 -> x4, Pallas kernels: 50.7 us -> 63.8 us  [the longest x1 42.4 us: own_queries(): call(query_kernel, 2, own, [pl.BlockSpec((bs, width), at), pl.BlockSpec((...]
    all_to_all x6 -> x5, starting transfers between devices: 56.5 us -> 47.3 us  [exchange(): return lax.all_to_all(x, DEVICES, split_axis=0, concat_axis=0, tiled=True)]
    all_to_all x6 -> x5, waiting for transfers between devices: 26.9 us -> 22.3 us  [exchange(): return lax.all_to_all(x, DEVICES, split_axis=0, concat_axis=0, tiled=True)]
    squeeze x2 -> x0, local copies, waits for them, and re-layouts: 4.11 us -> none  [the longest x1 2.07 us: body(): w_by[1]]
    unnamed x46 -> x33, local copies, waits for them, and re-layouts: 8.71 us -> 7.76 us
  transfers between devices with their start and end apart: 9 -> 8, of which waited for: 5 -> 4; matrix products, arithmetic and copies ran while one was open for 17% -> 8% of each run, Pallas kernels for 24% -> 29%
where the time goes in v3:
time: 305 us; the launch traced here: 304 us
  Pallas kernels  98.5 us (32%)
  waiting for transfers between devices  93.3 us (31%)
  starting transfers between devices  55.9 us (18%)
  local copies, waits for them, and re-layouts  24.7 us (8%)
  matrix products  19.8 us (6%)
  other arithmetic  11.3 us (4%)
    ppermute x3, waiting for transfers between devices, swap(): return lax.ppermute(x, 'head', [(0, 1), (1, 0)])  71 us
    all_to_all x5, starting transfers between devices, exchange(): return lax.all_to_all(x, DEVICES, split_axis=0, concat_axis=0, tiled=True)  47.3 us
    pallas_call x1, Pallas kernels, own_queries(): call(query_kernel, 2, own, [pl.BlockSpec((bs, width), at), pl.BlockSpec((...  42.4 us
    pallas_call x1, Pallas kernels, body(): call(peer_kernel, 2, own, [pl.BlockSpec((bs, width), lambda i, *s: (own +...  23.3 us
    all_to_all x5, waiting for transfers between devices, exchange(): return lax.all_to_all(x, DEVICES, split_axis=0, concat_axis=0, tiled=True)  22.3 us
    pallas_call x3, Pallas kernels, project(): call(project_kernel, 0, own // per, [pl.BlockSpec((per * bs, width), lamb...  21.4 us
    pallas_call x1, Pallas kernels, body(): call(far_kernel, 1, own, [pl.BlockSpec((bs, width), step), pl.BlockSpec((...  11.4 us
    ppermute x3, starting transfers between devices, swap(): return lax.ppermute(x, 'head', [(0, 1), (1, 0)])  8.6 us
  transfers between devices with their start and end apart: 8, of which 4 were waited for; matrix products, arithmetic and copies ran while one was open for 8% of the time, Pallas kernels for 29%

profile of v3, /device:TPU:0, one launch (start us, length us, event | category | flops | bytes accessed | tf_op | source)
XLA Modules:
  0.0 304.4 jit_solution(2440379877673630472)
XLA Ops:
  3.0 1.9 copy.58
  4.9 11.6 %all-to-all-start = ((bf16[128,8,640]{2,1,0:T(8,128)(2,1)}), bf16[128,8,640]{2,1,0:T(8,128)(2,1)}, u32[]{:S(2)}, u32[]{:S(2)}) async-start(bf16[128,8,640]{2,1,0:T(8,128)(2,1)} %copy.58), calls=%async_computation | async-start | bytes 2621440 | tf_op jit(solution)/shard_map/all_to_all | solution.py:228
  16.5 2.9 collective-permute-start
  19.4 1.7 copy.60
  23.3 2.6 copy.61.w_ref
  25.9 1.8 convolution_convert_fusion.2.cot_ref
  31.3 7.2 %project_own.1 = (bf16[2048,1536]{1,0:T(8,128)(2,1)}, bf16[16,1024,128]{2,1,0:T(8,128)(2,1)}) custom-call(bf16[1024,512]{1,0:T(8,128)(2,1)} %x_ref.1, bf16[512,1536]{1,0:T(8,128)(2,1)} %copy.61.w_ref, bf16[1024,512]{1,0:T(8,128)(2,1)} %maximum_bitcast_fusion.wt_ref), custom_call_target="tpu_custom_call" | custom-call | flops 2684354560 | bytes 8388608 | tf_op jit(solution)/shard_map/project_own/pallas_call | solution.py:253
  38.5 18.4 %collective-permute-done.x_ref = bf16[1024,512]{1,0:T(8,128)(2,1)} collective-permute-done((bf16[1024,512]{1,0:T(8,128)(2,1)}, bf16[1024,512]{1,0:T(8,128)(2,1)}, u32[]{:S(2)}, u32[]{:S(2)}) %collective-permute-start) | collective-permute-done | bytes 1048608 | tf_op jit(solution)/shard_map/ppermute | solution.py:225
  56.8 3.2 %copy.62 = bf16[128,8,640]{0,1,2:T(8,128)(2,1)} copy(bf16[128,8,640]{2,1,0:T(8,128)(2,1)} %all-to-all-done) | data formatting | bytes 2621440 | tf_op jit(solution)/shard_map/optimization_barrier | solution.py:273
  60.9 2.6 fusion.8
  65.1 7.5 %all-to-all-start.1 = ((bf16[128,8,1024]{2,1,0:T(8,128)(2,1)}), bf16[128,8,1024]{2,1,0:T(8,128)(2,1)}, u32[]{:S(2)}, u32[]{:S(2)}) async-start(bf16[128,8,1024]{2,1,0:T(8,128)(2,1)} %pad_maximum_fusion), calls=%async_computation.1 | async-start | bytes 4194304 | tf_op jit(solution)/shard_map/all_to_all | solution.py:228
  72.6 2.9 collective-permute-start.1
  76.9 7.1 %project_peer.1 = (bf16[2048,1536]{1,0:T(8,128)(2,1)}, bf16[16,1024,128]{2,1,0:T(8,128)(2,1)}) custom-call(bf16[1024,512]{1,0:T(8,128)(2,1)} %collective-permute-done.x_ref, bf16[512,1536]{1,0:T(8,128)(2,1)} %copy.61.w_ref, bf16[1024,512]{1,0:T(8,128)(2,1)} %maximum_bitcast_fusion.wt_ref, ...), custom_call_target="tpu_custom_call", output_to_operand_aliasing={{0}: (3, {}), {1}: (4, {})} | custom-call | flops 2684354560 | bytes 8388608 | tf_op jit(solution)/shard_map/project_peer/pallas_call | solution.py:253
  84.0 38.2 %collective-permute-done.1.cot_ref = bf16[1024,512]{1,0:T(8,128)(2,1)} collective-permute-done((bf16[1024,512]{1,0:T(8,128)(2,1)}, bf16[1024,512]{1,0:T(8,128)(2,1)}, u32[]{:S(2)}, u32[]{:S(2)}) %collective-permute-start.1) | collective-permute-done | bytes 1048608 | tf_op jit(solution)/shard_map/ppermute | solution.py:225
  123.6 3.6 %fusion.7 = bf16[128,8,512]{2,1,0:T(8,128)(2,1)} fusion(s32[1024]{0:T(1024)S(1)} %convert_element_type.70, bf16[128,8,1024]{2,1,0:T(8,128)(2,1)} %all-to-all-done.1), kind=kOutput, calls=%fused_computation.16 | convolution fusion | flops 1075314688 | bytes 2101248 | tf_op jit(solution)/shard_map/dot_general | solution.py:234
  128.4 6.6 %all-to-all-start.2 = ((bf16[128,8,512]{2,1,0:T(8,128)(2,1)}), bf16[128,8,512]{2,1,0:T(8,128)(2,1)}, u32[]{:S(2)}, u32[]{:S(2)}) async-start(bf16[128,8,512]{2,1,0:T(8,128)(2,1)} %fusion.7), calls=%async_computation.2 | async-start | bytes 2097152 | tf_op jit(solution)/shard_map/all_to_all | solution.py:228
  135.1 7.1 %project_far.1 = (bf16[1024,1536]{1,0:T(8,128)(2,1)}, bf16[8,1024,128]{2,1,0:T(8,128)(2,1)}) custom-call(bf16[1024,512]{1,0:T(8,128)(2,1)} %bitcast.100, bf16[512,1536]{1,0:T(8,128)(2,1)} %copy.61.w_ref, bf16[1024,512]{1,0:T(8,128)(2,1)} %maximum_bitcast_fusion.wt_ref), custom_call_target="tpu_custom_call" | custom-call | flops 2684354560 | bytes 8388608 | tf_op jit(solution)/shard_map/project_far/pallas_call | solution.py:253
  142.2 42.4 %own_queries.1 = (bf16[1024,512]{1,0:T(8,128)(2,1)}, bf16[1024,512]{1,0:T(8,128)(2,1)}, f32[8,128,1024]{2,1,0:T(8,128)}, f32[8,24,128]{2,1,0:T(8,128)}, f32[128,24,128]{2,1,0:T(8,128)}) custom-call(s32[16,4]{1,0:T(8,128)} %copy.71.near_ids, s32[9]{0:T(128)} %pad_add_fusion.1.meta, bf16[2048,1536]{1,0:T(8,128)(2,1)} %get-tuple-element.45.q_ref, ...), custom_call_target="tpu_custom_call" | custom-call | flops 10737418240 | bytes 31457280 | tf_op jit(solution)/shard_map/own_queries/pallas_call | solution.py:297
  184.6 10.8 %all-to-all-start.3 = ((f32[128,24,128]{2,1,0:T(8,128)}), f32[128,24,128]{2,1,0:T(8,128)}, u32[]{:S(2)}, u32[]{:S(2)}) async-start(f32[128,24,128]{2,1,0:T(8,128)} %get-tuple-element.56), calls=%async_computation.3 | async-start | bytes 3145728 | tf_op jit(solution)/shard_map/all_to_all | solution.py:228
  195.5 2.9 collective-permute-start.2
  198.3 2.1 fusion.9
  200.5 2.0 fusion.10
  203.2 14.4 %collective-permute-done.2.stats_ref = f32[8,24,128]{2,1,0:T(8,128)S(1)} collective-permute-done((f32[8,24,128]{2,1,0:T(8,128)S(1)}, f32[8,24,128]{2,1,0:T(8,128)S(1)}, u32[]{:S(2)}, u32[]{:S(2)}) %collective-permute-start.2) | collective-permute-done | bytes 98336 | tf_op jit(solution)/shard_map/ppermute | solution.py:225
  218.3 23.3 %peer_queries.1.acc_ref = f32[8,128,1024]{2,1,0:T(8,128)} custom-call(s32[16,4]{1,0:T(8,128)} %copy.71.near_ids, s32[9]{0:T(128)} %pad_add_fusion.1.meta, bf16[2048,1536]{1,0:T(8,128)(2,1)} %get-tuple-element.45.q_ref, bf16[1024,512]{1,0:T(8,128)(2,1)} %collective-permute-done.1.cot_ref, f32[8,24,128]{2,1,0:T(8,128)} %copy-done.10, ...), custom_call_target="tpu_custom_call" | custom-call | flops 4294967296 | bytes 20971520 | tf_op jit(solution)/shard_map/peer_queries/pallas_call | solution.py:347
  241.5 2.5 copy.69
  244.0 11.4 %far_queries.1 = bf16[1024,1024]{1,0:T(8,128)(2,1)} custom-call(s32[9]{0:T(128)} %pad_add_fusion.1.meta, bf16[1024,1536]{1,0:T(8,128)(2,1)} %get-tuple-element.49.q_ref, bf16[1024,512]{1,0:T(8,128)(2,1)} %bitcast.96, f32[128,24,128]{2,1,0:T(8,128)} %all-to-all-done.3.stats_ref, bf16[16,128,1536]{2,1,0:T(8,128)(2,1)} %bitcast.83, ...), custom_call_target="tpu_custom_call" | custom-call | flops 2147483648 | bytes 10485760 | tf_op jit(solution)/shard_map/far_queries/pallas_call | solution.py:367
  255.4 3.1 %fusion.6 = bf16[512,1024]{1,0:T(8,128)(2,1)S(1)} fusion(bf16[1024,1024]{1,0:T(8,128)(2,1)} %far_queries.1, bf16[1024,512]{1,0:T(8,128)(2,1)} %x_ref.1), kind=kOutput, calls=%fused_computation.15 | convolution fusion | flops 1074266112 | bytes 4194304 | tf_op jit(solution)/shard_map/rd,rc->dc/dot_general | solution.py:382
  261.4 10.7 %all-to-all-start.4 = ((bf16[128,8,1024]{2,1,0:T(8,128)(2,1)}), bf16[128,8,1024]{2,1,0:T(8,128)(2,1)}, u32[]{:S(2)}, u32[]{:S(2)}) async-start(bf16[128,8,1024]{2,1,0:T(8,128)(2,1)} %bitcast.89), calls=%async_computation.4 | async-start | bytes 4194304 | tf_op jit(solution)/shard_map/all_to_all | solution.py:228
  273.5 1.7 convolution_convert_fusion.1
  276.7 2.2 add_convert_fusion
  278.9 22.3 %all-to-all-done.4 = bf16[128,8,1024]{2,1,0:T(8,128)(2,1)} async-done(((bf16[128,8,1024]{2,1,0:T(8,128)(2,1)}), bf16[128,8,1024]{2,1,0:T(8,128)(2,1)}, u32[]{:S(2)}, u32[]{:S(2)}) %all-to-all-start.4) | async-done | bytes 2097184 | tf_op jit(solution)/shard_map/all_to_all | solution.py:228
  301.2 2.0 convert_reduce_fusion
  (67 shorter events, 22.8 us)
Async XLA Ops:
  0.6 25.2 %copy-start = (bf16[1024,512]{1,0:T(8,128)(2,1)S(1)}, bf16[1024,512]{1,0:T(8,128)(2,1)}, u32[]{:S(2)}) copy-start(bf16[1024,512]{1,0:T(8,128)(2,1)} %param.13) | copy-start | bytes 3145732
  4.9 52.0 %all-to-all-start = ((bf16[128,8,640]{2,1,0:T(8,128)(2,1)}), bf16[128,8,640]{2,1,0:T(8,128)(2,1)}, u32[]{:S(2)}, u32[]{:S(2)}) async-start(bf16[128,8,640]{2,1,0:T(8,128)(2,1)} %copy.58), calls=%async_computation | async-start | bytes 2621440 | tf_op jit(solution)/shard_map/all_to_all | solution.py:228
  16.5 40.3 %collective-permute-start = (bf16[1024,512]{1,0:T(8,128)(2,1)}, bf16[1024,512]{1,0:T(8,128)(2,1)}, u32[]{:S(2)}, u32[]{:S(2)}) collective-permute-start(bf16[1024,512]{1,0:T(8,128)(2,1)} %x_ref.1), channel_id=1, source_target_pairs={{0,1},{1,0},{2,3},{3,2},{4,5},{5,4},{6,7},{7,6},{8,9},{9,8},{10,11... | collective-permute-start | bytes 3145736 | tf_op jit(solution)/shard_map/ppermute | solution.py:225
  21.2 0.8 copy-start.2
  25.9 4.4 %copy-start.3 = (bf16[1,512,2,256]{1,3,0,2:T(8,128)(2,1)S(1)}, bf16[1,512,2,256]{1,3,0,2:T(8,128)(2,1)}, u32[]{:S(2)}) copy-start(bf16[1,512,2,256]{1,3,0,2:T(8,128)(2,1)} %copy-done.2) | copy-start | bytes 1572868
  27.7 1.0 copy-start.4
  60.9 2.6 copy-start.5
  65.1 10.3 %copy-start.11 = (s32[16,4]{0,1:T(4,128)S(1)}, s32[16,4]{0,1:T(4,128)}, u32[]{:S(2)}) copy-start(s32[16,4]{0,1:T(4,128)} %param.10) | copy-start | bytes 772
  65.1 57.1 %all-to-all-start.1 = ((bf16[128,8,1024]{2,1,0:T(8,128)(2,1)}), bf16[128,8,1024]{2,1,0:T(8,128)(2,1)}, u32[]{:S(2)}, u32[]{:S(2)}) async-start(bf16[128,8,1024]{2,1,0:T(8,128)(2,1)} %pad_maximum_fusion), calls=%async_computation.1 | async-start | bytes 4194304 | tf_op jit(solution)/shard_map/all_to_all | solution.py:228
  72.6 49.6 %collective-permute-start.1 = (bf16[1024,512]{1,0:T(8,128)(2,1)}, bf16[1024,512]{1,0:T(8,128)(2,1)}, u32[]{:S(2)}, u32[]{:S(2)}) collective-permute-start(bf16[1024,512]{1,0:T(8,128)(2,1)} %copy-done.4), channel_id=1, source_target_pairs={{0,1},{1,0},{2,3},{3,2},{4,5},{5,4},{6,7},{7,6},{8,9},{9,8},{10,11... | collective-permute-start | bytes 3145736 | tf_op jit(solution)/shard_map/ppermute | solution.py:225
  128.4 56.2 %all-to-all-start.2 = ((bf16[128,8,512]{2,1,0:T(8,128)(2,1)}), bf16[128,8,512]{2,1,0:T(8,128)(2,1)}, u32[]{:S(2)}, u32[]{:S(2)}) async-start(bf16[128,8,512]{2,1,0:T(8,128)(2,1)} %fusion.7), calls=%async_computation.2 | async-start | bytes 2097152 | tf_op jit(solution)/shard_map/all_to_all | solution.py:228
  184.6 10.9 %copy-start.14 = (f32[8,24,128]{2,1,0:T(8,128)S(1)}, f32[8,24,128]{2,1,0:T(8,128)}, u32[]{:S(2)}) copy-start(f32[8,24,128]{2,1,0:T(8,128)} %get-tuple-element.58) | copy-start | bytes 294916
  184.6 59.4 %all-to-all-start.3 = ((f32[128,24,128]{2,1,0:T(8,128)}), f32[128,24,128]{2,1,0:T(8,128)}, u32[]{:S(2)}, u32[]{:S(2)}) async-start(f32[128,24,128]{2,1,0:T(8,128)} %get-tuple-element.56), calls=%async_computation.3 | async-start | bytes 3145728 | tf_op jit(solution)/shard_map/all_to_all | solution.py:228
  195.5 22.1 %collective-permute-start.2 = (f32[8,24,128]{2,1,0:T(8,128)S(1)}, f32[8,24,128]{2,1,0:T(8,128)S(1)}, u32[]{:S(2)}, u32[]{:S(2)}) collective-permute-start(f32[8,24,128]{2,1,0:T(8,128)S(1)} %copy-done.14), channel_id=1, source_target_pairs={{0,1},{1,0},{2,3},{3,2},{4,5},{5,4},{6,7},{7,6},{8,9},{9,8},{10,11... | collective-permute-start | bytes 294920 | tf_op jit(solution)/shard_map/ppermute | solution.py:225
  198.3 2.1 copy-start.7
  217.6 0.6 copy-start.10
  258.6 1.0 copy-start.9
  261.4 39.9 %all-to-all-start.4 = ((bf16[128,8,1024]{2,1,0:T(8,128)(2,1)}), bf16[128,8,1024]{2,1,0:T(8,128)(2,1)}, u32[]{:S(2)}, u32[]{:S(2)}) async-start(bf16[128,8,1024]{2,1,0:T(8,128)(2,1)} %bitcast.89), calls=%async_computation.4 | async-start | bytes 4194304 | tf_op jit(solution)/shard_map/all_to_all | solution.py:228
  272.1 1.2 copy-start.12
  272.1 1.3 copy-start.13
  273.5 1.7 copy-start.8
  275.1 1.6 copy-start.6
  276.7 27.7 %copy-start.1 = (bf16[1024,512]{1,0:T(8,128)(2,1)S(1)}, bf16[1024,512]{1,0:T(8,128)(2,1)}, u32[]{:S(2)}) copy-start(bf16[1024,512]{1,0:T(8,128)(2,1)} %param.13) | copy-start | bytes 3145732

commit v4 on v3

--- a/solution.py
+++ b/solution.py
@@ -46,13 +46,59 @@
     return row[:, : row.shape[1] // 2], row[:, row.shape[1] // 2 :]
 
 
-def query_kernel(near_ids, meta, q_ref, cot_ref, tile_ref, k_ref, v_ref, kt_ref, vt_ref, fk_ref,
-                 fv_ref, fkt_ref, fvt_ref, att_ref, dq_ref, acc_ref, stats_ref, slot_ref, p_scr, ds_scr,
-                 qz_scr, cz_scr, bias_scr):
+def near_kernel(near_ids, meta, q_ref, tile_ref, k_ref, vt_ref, out_ref, sums_ref, bias_scr):
     i = pl.program_id(0)
-    pairs = q_ref.shape[1] // LANES
-    bs = q_ref.shape[0]
-    width = q_ref.shape[1]
+    for j in range(NBR):
+        bias_scr[j] = bias_of(tile_ref[0, j])
+    ids = [near_ids[i, j] for j in range(NBR)]
+    for c in range(q_ref.shape[1] // LANES):
+        cols = slice(c * LANES, (c + 1) * LANES)
+        qz = two_heads(q_ref[:, cols])
+        scores = jnp.concatenate([nt(k_ref[ids[j], :, cols], qz) + bias_scr[j] for j in range(NBR)], axis=0)
+        peak = jnp.max(scores, axis=0, keepdims=True)
+        terms = jnp.exp(scores - peak)
+        total = jnp.sum(terms, axis=0, keepdims=True)
+        vt = jnp.concatenate([vt_ref[ids[j], cols, :] for j in range(NBR)], axis=1)
+        out_ref[0, cols, :] = own_heads(nn(vt, terms.astype(BF16)))
+        store_rows(sums_ref, c, (peak, total))
+
+
+def store_rows(ref, c, rows):
+    for s, row in enumerate(rows):
+        for e, part in enumerate(split_stat(row)):
+            at = s * H + 2 * c + e
+            ref[0, at : at + 1, :] = part
+
+
+def merge_kernel(meta, q_ref, cot_ref, fk_ref, fvt_ref, out_ref, sums_ref, att_ref, stats_ref, slot_ref):
+    mid = LANES // 2
+    for c in range(q_ref.shape[1] // LANES):
+        cols = slice(c * LANES, (c + 1) * LANES)
+        near_peak, near_total = load_rows(sums_ref, c, 2)
+        scores = nt(fk_ref[0, :, cols], two_heads(q_ref[:, cols]))
+        peak = jnp.maximum(near_peak, jnp.max(scores, axis=0, keepdims=True))
+        terms = jnp.exp(scores - peak)
+        kept = jnp.exp(near_peak - peak)
+        inv = 1.0 / (near_total * kept + jnp.sum(terms, axis=0, keepdims=True))
+        far_out = own_heads(nn(fvt_ref[0, cols, :], (terms * inv).astype(BF16)))
+        first, second = split_stat(kept * inv)
+        near_out = out_ref[0, cols, :]
+        near_out = jnp.concatenate([near_out[:mid] * first, near_out[mid:] * second], axis=0)
+        att = (far_out + near_out).astype(BF16).astype(F32)
+        att_ref[:, cols] = att.T.astype(BF16)
+        prod = cot_ref[:, cols].astype(F32).T * att
+        delta = jnp.concatenate(
+            [jnp.sum(prod[:mid], axis=0, keepdims=True), jnp.sum(prod[mid:], axis=0, keepdims=True)], axis=1
+        )
+        store_rows(stats_ref, c, (peak, inv, delta))
+        store_rows(slot_ref, c, (peak, inv, delta))
+
+
+def own_kernel(near_ids, meta, q_ref, cot_ref, tile_ref, stats_ref, k_ref, v_ref, kt_ref, fk_ref, fv_ref, fkt_ref,
+               dq_ref, acc_ref, p_scr, ds_scr, qz_scr, cz_scr, bias_scr):
+    i = pl.program_id(0)
+    bs, width = q_ref.shape
+    pairs = width // LANES
     own = acc_ref.shape[0]
 
     @pl.when(i == 0)
@@ -64,42 +110,28 @@
     ids = [near_ids[i, j] for j in range(NBR)]
     for c in range(pairs):
         cols = slice(c * LANES, (c + 1) * LANES)
-        cot = cot_ref[:, cols]
         qz = two_heads(q_ref[:, cols])
-        cz = two_heads(cot)
+        cz = two_heads(cot_ref[:, cols])
         qz_scr[c] = qz
         cz_scr[c] = cz
-        scores = [nt(k_ref[ids[j], :, cols], qz) + bias_scr[j] for j in range(NBR)]
-        scores.append(nt(fk_ref[0, :, cols], qz))
-        scores = jnp.concatenate(scores, axis=0)
-        peak = jnp.max(scores, axis=0, keepdims=True)
-        probs = jnp.exp(scores - peak)
-        inv = 1.0 / jnp.sum(probs, axis=0, keepdims=True)
-        probs = probs * inv
-        low = probs.astype(BF16)
-        vt = jnp.concatenate([vt_ref[ids[j], cols, :] for j in range(NBR)] + [fvt_ref[0, cols, :]], axis=1)
-        att = own_heads(nn(vt, low)).astype(BF16).astype(F32)
-        att_ref[:, cols] = att.T.astype(BF16)
-        prod = cot.astype(F32).T * att
-        delta = jnp.concatenate(
-            [jnp.sum(prod[: LANES // 2], axis=0, keepdims=True), jnp.sum(prod[LANES // 2 :], axis=0, keepdims=True)],
-            axis=1,
-        )
-        grad_probs = jnp.concatenate(
-            [nt(v_ref[ids[j], :, cols], cz) for j in range(NBR)] + [nt(fv_ref[0, :, cols], cz)], axis=0
-        )
-        ds = (probs * (grad_probs - delta)).astype(BF16)
+        peak, inv, delta = load_rows(stats_ref, c, 3)
+        parts = []
+        for j in range(NBR + 1):
+            if j < NBR:
+                scores = nt(k_ref[ids[j], :, cols], qz) + bias_scr[j]
+                grad_probs = nt(v_ref[ids[j], :, cols], cz)
+            else:
+                scores = nt(fk_ref[0, :, cols], qz)
+                grad_probs = nt(fv_ref[0, :, cols], cz)
+            probs = jnp.exp(scores - peak) * inv
+            parts.append((probs * (grad_probs - delta)).astype(BF16))
+            if j < NBR:
+                rows = slice(j * bs, (j + 1) * bs)
+                p_scr[c, rows, :] = probs.astype(BF16)
+                ds_scr[c, rows, :] = parts[j]
         kt = jnp.concatenate([kt_ref[ids[j], cols, :] for j in range(NBR)] + [fkt_ref[0, cols, :]], axis=1)
-        dq = own_heads(nn(kt, ds)) * 0.125
+        dq = own_heads(nn(kt, jnp.concatenate(parts, axis=0))) * 0.125
         dq_ref[:, cols] = dq.T.astype(BF16)
-        p_scr[c] = low[: NBR * bs]
-        ds_scr[c] = ds[: NBR * bs]
-        for s, row in enumerate((peak, inv, delta)):
-            first, second = split_stat(row)
-            for e, part in enumerate((first, second)):
-                at = s * H + 2 * c + e
-                stats_ref[0, at : at + 1, :] = part
-                slot_ref[0, at : at + 1, :] = part
 
     for j in range(NBR):
 
@@ -114,12 +146,12 @@
                 acc_ref[n, :, vcols] += nn(p_scr[c, rows, :], cz_scr[c])
 
 
-def load_stats(ref, c):
+def load_rows(ref, c, count):
     return [
         jnp.concatenate(
             [ref[0, s * H + 2 * c : s * H + 2 * c + 1, :], ref[0, s * H + 2 * c + 1 : s * H + 2 * c + 2, :]], axis=1
         )
-        for s in range(3)
+        for s in range(count)
     ]
 
 
@@ -157,7 +189,7 @@
                 cols = slice(c * LANES, (c + 1) * LANES)
                 vcols = slice(width + c * LANES, width + (c + 1) * LANES)
                 dk, dv = key_terms(
-                    k_ref[n, :, cols], v_ref[n, :, cols], qz_scr[c], cz_scr[c], bias, load_stats(stats_ref, c)
+                    k_ref[n, :, cols], v_ref[n, :, cols], qz_scr[c], cz_scr[c], bias, load_rows(stats_ref, c, 3)
                 )
                 acc_ref[n, :, cols] += dk
                 acc_ref[n, :, vcols] += dv
@@ -171,7 +203,7 @@
         vcols = slice(width + c * LANES, width + (c + 1) * LANES)
         dk, dv = key_terms(
             k_ref[0, :, cols], v_ref[0, :, cols], two_heads(q_ref[:, cols]), two_heads(cot_ref[:, cols]), None,
-            load_stats(stats_ref, c),
+            load_rows(stats_ref, c, 3),
         )
         dkv_ref[:, cols] = (acc_ref[0, :, cols] + dk.astype(BF16).astype(F32)).astype(BF16)
         dkv_ref[:, vcols] = (acc_ref[0, :, vcols] + dv.astype(BF16).astype(F32)).astype(BF16)
@@ -272,73 +304,77 @@
     own_part = project(node_feats, blocks, 0, (), "project_own")
     rows_in, cot_rows, own_part, peer_feats = lax.optimization_barrier((rows_in, cot_rows, own_part, peer_feats))
 
-    ids = rows_in[:, :, width].astype(F32) * DIGIT + rows_in[:, :, width + 1].astype(F32)
-    ids = ids.astype(jnp.int32).reshape(-1)
-    one_hot = (ids[:, None] == jnp.arange(ids.shape[0], dtype=jnp.int32)[None, :]).astype(BF16)
+    weigh = jnp.pad(jnp.asarray([DIGIT, 1], F32), (0, LANES - 2))
+    ids = jnp.sum(rows_in.reshape(-1, width + LANES)[:, width:].astype(F32) * weigh[None], axis=1, keepdims=True)
+    one_hot = (ids == jnp.arange(ids.shape[0], dtype=jnp.int32)[None, :].astype(F32)).astype(BF16)
     second = jnp.concatenate([gathered(rows_in[:, :, :width]), cot_rows], axis=2)
-    second, cot_out = lax.optimization_barrier((second, cot))
     second = exchange(second)
-    peer_cot = swap(cot_out)
     part_qkv, part_t = project(peer_feats, blocks, own, own_part, "project_peer")
-    second, peer_cot, part_qkv, part_t = lax.optimization_barrier((second, peer_cot, part_qkv, part_t))
+    part_blk = part_qkv.reshape(blocks, bs, 3 * width)
+    pair_flops = 2 * bs * bs * width * 2
+    step = lambda i, *s: (i, 0)
+    row_step = lambda i, *s: (i, 0, 0)
+    rows_spec = pl.BlockSpec((bs, width), step)
+    tile_spec = pl.BlockSpec((1, NBR, bs, bs), lambda i, ids, meta: (meta[0] + i, 0, 0, 0))
+    k_spec = pl.BlockSpec((blocks, bs, width), lambda i, *s: (0, 0, 1), pipeline_mode=pl.Buffered(1))
+    v_spec = pl.BlockSpec((blocks, bs, width), lambda i, *s: (0, 0, 2), pipeline_mode=pl.Buffered(1))
+    kt_spec = pl.BlockSpec((blocks, width, bs), lambda i, *s: (0, 0, 0), pipeline_mode=pl.Buffered(1))
+    vt_spec = pl.BlockSpec((blocks, width, bs), lambda i, *s: (0, 1, 0), pipeline_mode=pl.Buffered(1))
+    stats_spec = pl.BlockSpec((1, STATS, bs), row_step)
+    near_out, sums = call(
+        near_kernel, 2, own,
+        [rows_spec, tile_spec, k_spec, vt_spec],
+        [pl.BlockSpec((1, width, bs), row_step), pl.BlockSpec((1, 2 * H, bs), row_step)],
+        [jax.ShapeDtypeStruct((own, width, bs), F32), jax.ShapeDtypeStruct((own, 2 * H, bs), F32)],
+        [pltpu.VMEM((NBR, bs, 2 * bs), F32)],
+        own * 16 * pair_flops, 10 << 20, "near_forward",
+    )(near_ids, meta, part_qkv, tiles, part_blk, part_t)
+    second, near_out, sums, cot_out = lax.optimization_barrier((second, near_out, sums, cot))
 
     picked = gathered(second[:, :, width:])
     far_feats = second[:, :, :width].transpose(1, 0, 2).reshape(rows, width)
     picked, far_feats = lax.optimization_barrier((picked, far_feats))
     far_cot = exchange(picked)
     far_qkv, far_t = project(far_feats, own, 0, (), "project_far")
-    part_blk = part_qkv.reshape(blocks, bs, 3 * width)
     far_blk = far_qkv.reshape(own, bs, 3 * width)
-
-    step = lambda i, *s: (i, 0)
-    pair_flops = 2 * bs * bs * width * 2
-    def own_queries():
-        at = lambda i, *s: (i, 0)
-        return call(
-            query_kernel, 2, own,
-            [
-                pl.BlockSpec((bs, width), at),
-                pl.BlockSpec((bs, width), at),
-                pl.BlockSpec((1, NBR, bs, bs), lambda i, ids, meta: (meta[0] + i, 0, 0, 0)),
-                pl.BlockSpec((blocks, bs, width), lambda i, *s: (0, 0, 1), pipeline_mode=pl.Buffered(1)),
-                pl.BlockSpec((blocks, bs, width), lambda i, *s: (0, 0, 2), pipeline_mode=pl.Buffered(1)),
-                pl.BlockSpec((blocks, width, bs), lambda i, *s: (0, 0, 0), pipeline_mode=pl.Buffered(1)),
-                pl.BlockSpec((blocks, width, bs), lambda i, *s: (0, 1, 0), pipeline_mode=pl.Buffered(1)),
-                pl.BlockSpec((1, bs, width), lambda i, *s: (i, 0, 1)),
-                pl.BlockSpec((1, bs, width), lambda i, *s: (i, 0, 2)),
-                pl.BlockSpec((1, width, bs), lambda i, *s: (i, 0, 0)),
-                pl.BlockSpec((1, width, bs), lambda i, *s: (i, 1, 0)),
-            ],
-            [
-                pl.BlockSpec((bs, width), at),
-                pl.BlockSpec((bs, width), at),
-                pl.BlockSpec((own, bs, 2 * width), lambda i, *s: (0, 0, 0)),
-                pl.BlockSpec((1, STATS, bs), lambda i, *s: (i, 0, 0)),
-                pl.BlockSpec((1, STATS, bs), lambda i, ids, meta: (meta[1 + i], 0, 0)),
-            ],
-            [
-                jax.ShapeDtypeStruct((rows, width), BF16),
-                jax.ShapeDtypeStruct((rows, width), BF16),
-                jax.ShapeDtypeStruct((own, bs, 2 * width), F32),
-                jax.ShapeDtypeStruct((own, STATS, bs), F32),
-                jax.ShapeDtypeStruct((devices, STATS, bs), F32),
-            ],
-            [
-                pltpu.VMEM((width // LANES, NBR * bs, 2 * bs), BF16),
-                pltpu.VMEM((width // LANES, NBR * bs, 2 * bs), BF16),
-                pltpu.VMEM((width // LANES, 2 * bs, LANES), BF16),
-                pltpu.VMEM((width // LANES, 2 * bs, LANES), BF16),
-                pltpu.VMEM((NBR, bs, 2 * bs), F32),
-            ],
-            own * 40 * pair_flops, 30 << 20, "own_queries",
-        )(near_ids, meta, part_qkv, cot, tiles, part_blk, part_blk, part_t, part_t, far_blk, far_blk, far_t, far_t)
-
-    att, dq, acc, stats, slots = own_queries()
-    far_cot, slots = lax.optimization_barrier((far_cot, slots))
-    far_cot = far_cot.transpose(1, 0, 2).reshape(rows, width)
-
+    peer_cot = swap(cot_out)
+
+    far_k_spec = pl.BlockSpec((1, bs, width), lambda i, *s: (i, 0, 1))
+    far_v_spec = pl.BlockSpec((1, bs, width), lambda i, *s: (i, 0, 2))
+    far_kt_spec = pl.BlockSpec((1, width, bs), row_step)
+    far_vt_spec = pl.BlockSpec((1, width, bs), lambda i, *s: (i, 1, 0))
+    att, stats, slots = call(
+        merge_kernel, 1, own,
+        [rows_spec, rows_spec, far_k_spec, far_vt_spec, pl.BlockSpec((1, width, bs), row_step),
+         pl.BlockSpec((1, 2 * H, bs), row_step)],
+        [rows_spec, stats_spec, pl.BlockSpec((1, STATS, bs), lambda i, meta: (meta[1 + i], 0, 0))],
+        [
+            jax.ShapeDtypeStruct((rows, width), BF16),
+            jax.ShapeDtypeStruct((own, STATS, bs), F32),
+            jax.ShapeDtypeStruct((devices, STATS, bs), F32),
+        ],
+        [], own * 4 * pair_flops, 6 << 20, "far_forward",
+    )(meta, part_qkv, cot, far_blk, far_t, near_out, sums)
+    far_cot, slots, stats = lax.optimization_barrier((far_cot, slots, stats))
     peer_stats = swap(stats)
     far_slots = exchange(slots)
+    pairs = width // LANES
+    dq, acc = call(
+        own_kernel, 2, own,
+        [rows_spec, rows_spec, tile_spec, stats_spec, k_spec, v_spec, kt_spec, far_k_spec, far_v_spec, far_kt_spec],
+        [rows_spec, pl.BlockSpec((own, bs, 2 * width), lambda i, *s: (0, 0, 0))],
+        [jax.ShapeDtypeStruct((rows, width), BF16), jax.ShapeDtypeStruct((own, bs, 2 * width), F32)],
+        [
+            pltpu.VMEM((pairs, NBR * bs, 2 * bs), BF16),
+            pltpu.VMEM((pairs, NBR * bs, 2 * bs), BF16),
+            pltpu.VMEM((pairs, 2 * bs, LANES), BF16),
+            pltpu.VMEM((pairs, 2 * bs, LANES), BF16),
+            pltpu.VMEM((NBR, bs, 2 * bs), F32),
+        ],
+        own * 24 * pair_flops, 30 << 20, "own_backward",
+    )(near_ids, meta, part_qkv, cot, tiles, stats, part_blk, part_blk, part_t, far_blk, far_blk, far_t)
+    acc, peer_stats, peer_cot = lax.optimization_barrier((acc, peer_stats, peer_cot))
+    far_cot = far_cot.transpose(1, 0, 2).reshape(rows, width)
 
     layer_out = jnp.dot(att, w_out, preferred_element_type=F32).astype(BF16)
     dwo_t = jnp.einsum("rc,ra->ca", layer_cot, att, preferred_element_type=F32).astype(BF16)

time: 305 us -> 276 us (0.905)
  waiting for transfers between devices: 93.3 us -> 45.9 us
  starting transfers between devices: 55.9 us -> 66.9 us
  Pallas kernels: 98.5 us -> 107 us
  local copies, waits for them, and re-layouts: 24.7 us -> 20.4 us
    ppermute x3, waiting for transfers between devices: 71 us -> 18.4 us  [swap(): return lax.ppermute(x, 'head', [(0, 1), (1, 0)])]
    all_to_all x5, starting transfers between devices: 47.3 us -> 58.1 us  [exchange(): return lax.all_to_all(x, DEVICES, split_axis=0, concat_axis=0, tiled=True)]
    pallas_call x1 -> x3, Pallas kernels: 42.4 us -> 50.5 us  [the longest x1 23.8 us: body(): call(own_kernel, 2, own, [rows_spec, rows_spec, tile_spec, stats_spec, k_...]
    all_to_all x5, waiting for transfers between devices: 22.3 us -> 27.4 us  [exchange(): return lax.all_to_all(x, DEVICES, split_axis=0, concat_axis=0, tiled=True)]
    optimization_barrier x1 -> x0, local copies, waits for them, and re-layouts: 3.21 us -> none  [body(): lax.optimization_barrier((rows_in, cot_rows, own_part, peer_feats))]
  transfers between devices with their start and end apart: 8 -> 8, of which waited for: 4 -> 3; matrix products, arithmetic and copies ran while one was open for 8% -> 9% of each run, Pallas kernels for 29% -> 35%
where the time goes in v4:
time: 276 us; the launch traced here: 273 us
  Pallas kernels  107 us (39%)
  starting transfers between devices  66.9 us (24%)
  waiting for transfers between devices  45.9 us (17%)
  local copies, waits for them, and re-layouts  20.4 us (7%)
  matrix products  18.9 us (7%)
  other arithmetic  12.9 us (5%)
    all_to_all x5, starting transfers between devices, exchange(): return lax.all_to_all(x, DEVICES, split_axis=0, concat_axis=0, tiled=True)  58.1 us
    all_to_all x5, waiting for transfers between devices, exchange(): return lax.all_to_all(x, DEVICES, split_axis=0, concat_axis=0, tiled=True)  27.4 us
    pallas_call x1, Pallas kernels, body(): call(peer_kernel, 2, own, [pl.BlockSpec((bs, width), lambda i, *s: (own +...  24.1 us
    pallas_call x1, Pallas kernels, body(): call(own_kernel, 2, own, [rows_spec, rows_spec, tile_spec, stats_spec, k_...  23.8 us
    pallas_call x3, Pallas kernels, project(): call(project_kernel, 0, own // per, [pl.BlockSpec((per * bs, width), lamb...  21.4 us
    ppermute x3, waiting for transfers between devices, swap(): return lax.ppermute(x, 'head', [(0, 1), (1, 0)])  18.4 us
    pallas_call x1, Pallas kernels, body(): call(near_kernel, 2, own, [rows_spec, tile_spec, k_spec, vt_spec], [pl.Bl...  16.2 us
    pallas_call x1, Pallas kernels, body(): call(far_kernel, 1, own, [pl.BlockSpec((bs, width), step), pl.BlockSpec((...  11.4 us
  transfers between devices with their start and end apart: 8, of which 3 were waited for; matrix products, arithmetic and copies ran while one was open for 9% of the time, Pallas kernels for 35%

profile of v4, /device:TPU:0, one launch (start us, length us, event | category | flops | bytes accessed | tf_op | source)
XLA Modules:
  0.0 273.3 jit_solution(1798672776188873330)
XLA Ops:
  3.0 1.9 copy.46
  4.9 11.6 %all-to-all-start = ((bf16[128,8,640]{2,1,0:T(8,128)(2,1)}), bf16[128,8,640]{2,1,0:T(8,128)(2,1)}, u32[]{:S(2)}, u32[]{:S(2)}) async-start(bf16[128,8,640]{2,1,0:T(8,128)(2,1)} %copy.46), calls=%async_computation | async-start | bytes 2621440 | tf_op jit(solution)/shard_map/all_to_all | solution.py:260
  16.5 2.9 %collective-permute-start = (bf16[1024,512]{1,0:T(8,128)(2,1)}, bf16[1024,512]{1,0:T(8,128)(2,1)}, u32[]{:S(2)}, u32[]{:S(2)}) collective-permute-start(bf16[1024,512]{1,0:T(8,128)(2,1)} %x_ref.1), channel_id=1, source_target_pairs={{0,1},{1,0},{2,3},{3,2},{4,5},{5,4},{6,7},{7,6},{8,9},{9,8},{10,11... | collective-permute-start | bytes 3145736 | tf_op jit(solution)/shard_map/ppermute | solution.py:257
  22.6 1.7 copy.48
  26.6 2.6 copy.49.w_ref
  29.2 2.1 maximum_bitcast_fusion.wt_ref
  31.2 7.2 %project_own.1 = (bf16[2048,1536]{1,0:T(8,128)(2,1)}, bf16[16,1024,128]{2,1,0:T(8,128)(2,1)}) custom-call(bf16[1024,512]{1,0:T(8,128)(2,1)} %x_ref.1, bf16[512,1536]{1,0:T(8,128)(2,1)} %copy.49.w_ref, bf16[1024,512]{1,0:T(8,128)(2,1)} %maximum_bitcast_fusion.wt_ref), custom_call_target="tpu_custom_call" | custom-call | flops 2684354560 | bytes 8388608 | tf_op jit(solution)/shard_map/project_own/pallas_call | solution.py:285
  38.4 18.4 %collective-permute-done.x_ref = bf16[1024,512]{1,0:T(8,128)(2,1)} collective-permute-done((bf16[1024,512]{1,0:T(8,128)(2,1)}, bf16[1024,512]{1,0:T(8,128)(2,1)}, u32[]{:S(2)}, u32[]{:S(2)}) %collective-permute-start) | collective-permute-done | bytes 1048608 | tf_op jit(solution)/shard_map/ppermute | solution.py:257
  58.0 2.6 fusion.18
  62.2 7.5 %all-to-all-start.1 = ((bf16[128,8,1024]{2,1,0:T(8,128)(2,1)}), bf16[128,8,1024]{2,1,0:T(8,128)(2,1)}, u32[]{:S(2)}, u32[]{:S(2)}) async-start(bf16[128,8,1024]{2,1,0:T(8,128)(2,1)} %pad_maximum_fusion), calls=%async_computation.1 | async-start | bytes 4194304 | tf_op jit(solution)/shard_map/all_to_all | solution.py:260
  71.2 7.1 %project_peer.1 = (bf16[2048,1536]{1,0:T(8,128)(2,1)}, bf16[16,1024,128]{2,1,0:T(8,128)(2,1)}) custom-call(bf16[1024,512]{1,0:T(8,128)(2,1)} %collective-permute-done.x_ref, bf16[512,1536]{1,0:T(8,128)(2,1)} %copy.49.w_ref, bf16[1024,512]{1,0:T(8,128)(2,1)} %maximum_bitcast_fusion.wt_ref, ...), custom_call_target="tpu_custom_call", output_to_operand_aliasing={{0}: (3, {}), {1}: (4, {})} | custom-call | flops 2684354560 | bytes 8388608 | tf_op jit(solution)/shard_map/project_peer/pallas_call | solution.py:285
  78.4 16.2 %near_forward.1 = (f32[8,512,128]{2,1,0:T(8,128)}, f32[8,16,128]{2,1,0:T(8,128)}) custom-call(s32[16,4]{1,0:T(8,128)} %copy.57.near_ids, s32[9]{0:T(128)} %pad_add_fusion.1.meta, bf16[2048,1536]{1,0:T(8,128)(2,1)} %get-tuple-element.43.q_ref, s32[16,4,128,128]{3,2,1,0:T(8,128)} %tile_ref.5, bf16[16,128,1536]{2,1,0:T(8,128)(2,1)} %bitcast.78, ...), custom_call_target="tpu_custom_call" | custom-call | flops 4294967296 | bytes 10485760 | tf_op jit(solution)/shard_map/near_forward/pallas_call | solution.py:324
  94.5 4.3 %all-to-all-done.1 = bf16[128,8,1024]{2,1,0:T(8,128)(2,1)} async-done(((bf16[128,8,1024]{2,1,0:T(8,128)(2,1)}), bf16[128,8,1024]{2,1,0:T(8,128)(2,1)}, u32[]{:S(2)}, u32[]{:S(2)}) %all-to-all-start.1) | async-done | bytes 2097184 | tf_op jit(solution)/shard_map/all_to_all | solution.py:260
  98.8 3.5 %fusion.15 = bf16[128,8,512]{2,1,0:T(8,128)(2,1)} fusion(f32[1024]{0:T(1024)S(1)} %iota_convert_fusion, f32[1024]{0:T(1024)S(1)} %multiply_reduce_fusion, bf16[128,8,1024]{2,1,0:T(8,128)(2,1)} %all-to-all-done.1), kind=kOutput, calls=%fused_computation.19 | convolution fusion | flops 1075314688 | bytes 2105344 | tf_op jit(solution)/shard_map/dot_general | solution.py:266
  104.9 5.9 %all-to-all-start.2 = ((bf16[128,8,512]{2,1,0:T(8,128)(2,1)}), bf16[128,8,512]{2,1,0:T(8,128)(2,1)}, u32[]{:S(2)}, u32[]{:S(2)}) async-start(bf16[128,8,512]{2,1,0:T(8,128)(2,1)} %fusion.15), calls=%async_computation.2 | async-start | bytes 2097152 | tf_op jit(solution)/shard_map/all_to_all | solution.py:260
  110.9 3.0 %collective-permute-start.2 = (bf16[1024,512]{1,0:T(8,128)(2,1)}, bf16[1024,512]{1,0:T(8,128)(2,1)}, u32[]{:S(2)}, u32[]{:S(2)}) collective-permute-start(bf16[1024,512]{1,0:T(8,128)(2,1)} %copy-done.2), channel_id=1, source_target_pairs={{0,1},{1,0},{2,3},{3,2},{4,5},{5,4},{6,7},{7,6},{8,9},{9,8},{10,11... | collective-permute-start | bytes 3145736 | tf_op jit(solution)/shard_map/ppermute | solution.py:257
  113.9 7.1 %project_far.1 = (bf16[1024,1536]{1,0:T(8,128)(2,1)}, bf16[8,1024,128]{2,1,0:T(8,128)(2,1)}) custom-call(bf16[1024,512]{1,0:T(8,128)(2,1)} %bitcast.101, bf16[512,1536]{1,0:T(8,128)(2,1)} %copy.49.w_ref, bf16[1024,512]{1,0:T(8,128)(2,1)} %maximum_bitcast_fusion.wt_ref), custom_call_target="tpu_custom_call" | custom-call | flops 2684354560 | bytes 8388608 | tf_op jit(solution)/shard_map/project_far/pallas_call | solution.py:285
  121.0 10.5 %far_forward.1 = (bf16[1024,512]{1,0:T(8,128)(2,1)}, f32[8,24,128]{2,1,0:T(8,128)}, f32[128,24,128]{2,1,0:T(8,128)}) custom-call(s32[9]{0:T(128)} %pad_add_fusion.1.meta, bf16[2048,1536]{1,0:T(8,128)(2,1)} %get-tuple-element.43.q_ref, bf16[1024,512]{1,0:T(8,128)(2,1)} %copy-done.2, bf16[8,128,1536]{2,1,0:T(8,128)(2,1)} %bitcast.85, ...), custom_call_target="tpu_custom_call" | custom-call | flops 1073741824 | bytes 6291456 | tf_op jit(solution)/shard_map/far_forward/pallas_call | solution.py:346
  131.5 23.3 %all-to-all-start.3 = ((f32[128,24,128]{2,1,0:T(8,128)}), f32[128,24,128]{2,1,0:T(8,128)}, u32[]{:S(2)}, u32[]{:S(2)}) async-start(f32[128,24,128]{2,1,0:T(8,128)} %get-tuple-element.62), calls=%async_computation.3 | async-start | bytes 3145728 | tf_op jit(solution)/shard_map/all_to_all | solution.py:260
  154.9 2.0 fusion.21
  156.9 2.9 %collective-permute-start.1 = (f32[8,24,128]{2,1,0:T(8,128)S(1)}, f32[8,24,128]{2,1,0:T(8,128)S(1)}, u32[]{:S(2)}, u32[]{:S(2)}) collective-permute-start(f32[8,24,128]{2,1,0:T(8,128)S(1)} %copy-done.8), channel_id=1, source_target_pairs={{0,1},{1,0},{2,3},{3,2},{4,5},{5,4},{6,7},{7,6},{8,9},{9,8},{10,11... | collective-permute-start | bytes 294920 | tf_op jit(solution)/shard_map/ppermute | solution.py:257
  159.8 23.8 %own_backward.1 = (bf16[1024,512]{1,0:T(8,128)(2,1)}, f32[8,128,1024]{2,1,0:T(8,128)}) custom-call(s32[16,4]{1,0:T(8,128)} %copy.57.near_ids, s32[9]{0:T(128)} %pad_add_fusion.1.meta, bf16[2048,1536]{1,0:T(8,128)(2,1)} %get-tuple-element.43.q_ref, bf16[1024,512]{1,0:T(8,128)(2,1)} %copy-done.2, s32[16,4,128,128]{3,2,1,0:T(8,128)} %tile_ref.5, ...), custom_call_target="tpu_custom_call" | custom-call | flops 6442450944 | bytes 31457280 | tf_op jit(solution)/shard_map/own_backward/pallas_call | solution.py:362
  183.6 2.3 fusion.22
  186.7 2.5 copy.55
  189.8 24.1 %peer_queries.1.acc_ref = f32[8,128,1024]{2,1,0:T(8,128)} custom-call(s32[16,4]{1,0:T(8,128)} %copy.57.near_ids, s32[9]{0:T(128)} %pad_add_fusion.1.meta, bf16[2048,1536]{1,0:T(8,128)(2,1)} %get-tuple-element.43.q_ref, bf16[1024,512]{1,0:T(8,128)(2,1)} %collective-permute-done.2.cot_ref, f32[8,24,128]{2,1,0:T(8,128)} %copy-done.9, ...), custom_call_target="tpu_custom_call" | custom-call | flops 4294967296 | bytes 20971520 | tf_op jit(solution)/shard_map/peer_queries/pallas_call | solution.py:383
  214.0 11.4 %far_queries.1 = bf16[1024,1024]{1,0:T(8,128)(2,1)} custom-call(s32[9]{0:T(128)} %pad_add_fusion.1.meta, bf16[1024,1536]{1,0:T(8,128)(2,1)} %get-tuple-element.51.q_ref, bf16[1024,512]{1,0:T(8,128)(2,1)} %bitcast.97, f32[128,24,128]{2,1,0:T(8,128)} %all-to-all-done.3.stats_ref, bf16[16,128,1536]{2,1,0:T(8,128)(2,1)} %bitcast.83, ...), custom_call_target="tpu_custom_call" | custom-call | flops 2147483648 | bytes 10485760 | tf_op jit(solution)/shard_map/far_queries/pallas_call | solution.py:403
  225.3 3.1 %fusion.14 = bf16[512,1024]{1,0:T(8,128)(2,1)S(1)} fusion(bf16[1024,1024]{1,0:T(8,128)(2,1)} %far_queries.1, bf16[1024,512]{1,0:T(8,128)(2,1)} %x_ref.1), kind=kOutput, calls=%fused_computation.18 | convolution fusion | flops 1074266112 | bytes 4194304 | tf_op jit(solution)/shard_map/rd,rc->dc/dot_general | solution.py:418
  231.3 9.8 %all-to-all-start.4 = ((bf16[128,8,1024]{2,1,0:T(8,128)(2,1)}), bf16[128,8,1024]{2,1,0:T(8,128)(2,1)}, u32[]{:S(2)}, u32[]{:S(2)}) async-start(bf16[128,8,1024]{2,1,0:T(8,128)(2,1)} %bitcast.91), calls=%async_computation.4 | async-start | bytes 4194304 | tf_op jit(solution)/shard_map/all_to_all | solution.py:260
  242.4 1.7 convolution_convert_fusion.1
  245.3 1.7 add_convert_fusion
  247.0 23.1 %all-to-all-done.4 = bf16[128,8,1024]{2,1,0:T(8,128)(2,1)} async-done(((bf16[128,8,1024]{2,1,0:T(8,128)(2,1)}), bf16[128,8,1024]{2,1,0:T(8,128)(2,1)}, u32[]{:S(2)}, u32[]{:S(2)}) %all-to-all-start.4) | async-done | bytes 2097184 | tf_op jit(solution)/shard_map/all_to_all | solution.py:260
  270.2 2.0 convert_reduce_fusion
  (66 shorter events, 22.6 us)
Async XLA Ops:
  0.6 18.7 %copy-start = (bf16[1024,512]{1,0:T(8,128)(2,1)S(1)}, bf16[1024,512]{1,0:T(8,128)(2,1)}, u32[]{:S(2)}) copy-start(bf16[1024,512]{1,0:T(8,128)(2,1)} %param.14) | copy-start | bytes 3145732
  3.0 16.4 %copy-start.13 = (bf16[512,512]{1,0:T(8,128)(2,1)S(1)}, bf16[512,512]{1,0:T(8,128)(2,1)}, u32[]{:S(2)}) copy-start(bf16[512,512]{1,0:T(8,128)(2,1)} %param.10) | copy-start | bytes 1572868
  4.9 52.0 %all-to-all-start = ((bf16[128,8,640]{2,1,0:T(8,128)(2,1)}), bf16[128,8,640]{2,1,0:T(8,128)(2,1)}, u32[]{:S(2)}, u32[]{:S(2)}) async-start(bf16[128,8,640]{2,1,0:T(8,128)(2,1)} %copy.46), calls=%async_computation | async-start | bytes 2621440 | tf_op jit(solution)/shard_map/all_to_all | solution.py:260
  16.5 40.3 %collective-permute-start = (bf16[1024,512]{1,0:T(8,128)(2,1)}, bf16[1024,512]{1,0:T(8,128)(2,1)}, u32[]{:S(2)}, u32[]{:S(2)}) collective-permute-start(bf16[1024,512]{1,0:T(8,128)(2,1)} %x_ref.1), channel_id=1, source_target_pairs={{0,1},{1,0},{2,3},{3,2},{4,5},{5,4},{6,7},{7,6},{8,9},{9,8},{10,11... | collective-permute-start | bytes 3145736 | tf_op jit(solution)/shard_map/ppermute | solution.py:257
  20.1 1.0 copy-start.2
  24.5 0.8 copy-start.3
  31.2 25.6 %copy-start.11 = (f32[128]{0:T(128)S(1)}, f32[128]{0:T(128)}, u32[]{:S(2)}) copy-start(f32[128]{0:T(128)} %constant.92) | copy-start | bytes 1540
  58.0 2.6 copy-start.4
  62.2 7.5 %copy-start.10 = (s32[16,4]{0,1:T(4,128)S(1)}, s32[16,4]{0,1:T(4,128)}, u32[]{:S(2)}) copy-start(s32[16,4]{0,1:T(4,128)} %param.11) | copy-start | bytes 772
  62.2 36.6 %all-to-all-start.1 = ((bf16[128,8,1024]{2,1,0:T(8,128)(2,1)}), bf16[128,8,1024]{2,1,0:T(8,128)(2,1)}, u32[]{:S(2)}, u32[]{:S(2)}) async-start(bf16[128,8,1024]{2,1,0:T(8,128)(2,1)} %pad_maximum_fusion), calls=%async_computation.1 | async-start | bytes 4194304 | tf_op jit(solution)/shard_map/all_to_all | solution.py:260
  104.9 26.6 %all-to-all-start.2 = ((bf16[128,8,512]{2,1,0:T(8,128)(2,1)}), bf16[128,8,512]{2,1,0:T(8,128)(2,1)}, u32[]{:S(2)}, u32[]{:S(2)}) async-start(bf16[128,8,512]{2,1,0:T(8,128)(2,1)} %fusion.15), calls=%async_computation.2 | async-start | bytes 2097152 | tf_op jit(solution)/shard_map/all_to_all | solution.py:260
  110.9 78.3 %collective-permute-start.2 = (bf16[1024,512]{1,0:T(8,128)(2,1)}, bf16[1024,512]{1,0:T(8,128)(2,1)}, u32[]{:S(2)}, u32[]{:S(2)}) collective-permute-start(bf16[1024,512]{1,0:T(8,128)(2,1)} %copy-done.2), channel_id=1, source_target_pairs={{0,1},{1,0},{2,3},{3,2},{4,5},{5,4},{6,7},{7,6},{8,9},{9,8},{10,11... | collective-permute-start | bytes 3145736 | tf_op jit(solution)/shard_map/ppermute | solution.py:257
  131.5 82.4 %all-to-all-start.3 = ((f32[128,24,128]{2,1,0:T(8,128)}), f32[128,24,128]{2,1,0:T(8,128)}, u32[]{:S(2)}, u32[]{:S(2)}) async-start(f32[128,24,128]{2,1,0:T(8,128)} %get-tuple-element.62), calls=%async_computation.3 | async-start | bytes 3145728 | tf_op jit(solution)/shard_map/all_to_all | solution.py:260
  154.9 2.0 copy-start.8
  156.9 32.2 %collective-permute-start.1 = (f32[8,24,128]{2,1,0:T(8,128)S(1)}, f32[8,24,128]{2,1,0:T(8,128)S(1)}, u32[]{:S(2)}, u32[]{:S(2)}) collective-permute-start(f32[8,24,128]{2,1,0:T(8,128)S(1)} %copy-done.8), channel_id=1, source_target_pairs={{0,1},{1,0},{2,3},{3,2},{4,5},{5,4},{6,7},{7,6},{8,9},{9,8},{10,11... | collective-permute-start | bytes 294920 | tf_op jit(solution)/shard_map/ppermute | solution.py:257
  189.2 0.6 copy-start.9
  228.5 1.0 copy-start.7
  231.3 38.9 %all-to-all-start.4 = ((bf16[128,8,1024]{2,1,0:T(8,128)(2,1)}), bf16[128,8,1024]{2,1,0:T(8,128)(2,1)}, u32[]{:S(2)}, u32[]{:S(2)}) async-start(bf16[128,8,1024]{2,1,0:T(8,128)(2,1)} %bitcast.91), calls=%async_computation.4 | async-start | bytes 4194304 | tf_op jit(solution)/shard_map/all_to_all | solution.py:260
  241.0 1.2 copy-start.12
  241.0 1.3 copy-start.14
  242.4 1.7 copy-start.5
  244.1 1.3 copy-start.6
  245.3 28.0 %copy-start.1 = (bf16[1024,512]{1,0:T(8,128)(2,1)S(1)}, bf16[1024,512]{1,0:T(8,128)(2,1)}, u32[]{:S(2)}) copy-start(bf16[1024,512]{1,0:T(8,128)(2,1)} %param.14) | copy-start | bytes 3145732

commit v5 on v4

--- a/solution.py
+++ b/solution.py
@@ -51,10 +51,17 @@
     for j in range(NBR):
         bias_scr[j] = bias_of(tile_ref[0, j])
     ids = [near_ids[i, j] for j in range(NBR)]
-    for c in range(q_ref.shape[1] // LANES):
+    pairs = q_ref.shape[1] // LANES
+
+    def scores_of(c):
         cols = slice(c * LANES, (c + 1) * LANES)
         qz = two_heads(q_ref[:, cols])
-        scores = jnp.concatenate([nt(k_ref[ids[j], :, cols], qz) + bias_scr[j] for j in range(NBR)], axis=0)
+        return jnp.concatenate([nt(k_ref[ids[j], :, cols], qz) + bias_scr[j] for j in range(NBR)], axis=0)
+
+    ready = scores_of(0)
+    for c in range(pairs):
+        cols = slice(c * LANES, (c + 1) * LANES)
+        scores, ready = ready, scores_of(c + 1) if c + 1 < pairs else None
         peak = jnp.max(scores, axis=0, keepdims=True)
         terms = jnp.exp(scores - peak)
         total = jnp.sum(terms, axis=0, keepdims=True)
@@ -72,26 +79,36 @@
 
 def merge_kernel(meta, q_ref, cot_ref, fk_ref, fvt_ref, out_ref, sums_ref, att_ref, stats_ref, slot_ref):
     mid = LANES // 2
-    for c in range(q_ref.shape[1] // LANES):
-        cols = slice(c * LANES, (c + 1) * LANES)
+    pairs = q_ref.shape[1] // LANES
+    cols = [slice(c * LANES, (c + 1) * LANES) for c in range(pairs)]
+    scores = [nt(fk_ref[0, :, cols[c]], two_heads(q_ref[:, cols[c]])) for c in range(pairs)]
+    turned_cot = [cot_ref[:, cols[c]].astype(F32).T for c in range(pairs)]
+    peaks, kepts, invs, lows = [], [], [], []
+    for c in range(pairs):
         near_peak, near_total = load_rows(sums_ref, c, 2)
-        scores = nt(fk_ref[0, :, cols], two_heads(q_ref[:, cols]))
-        peak = jnp.maximum(near_peak, jnp.max(scores, axis=0, keepdims=True))
-        terms = jnp.exp(scores - peak)
+        peak = jnp.maximum(near_peak, jnp.max(scores[c], axis=0, keepdims=True))
+        terms = jnp.exp(scores[c] - peak)
         kept = jnp.exp(near_peak - peak)
         inv = 1.0 / (near_total * kept + jnp.sum(terms, axis=0, keepdims=True))
-        far_out = own_heads(nn(fvt_ref[0, cols, :], (terms * inv).astype(BF16)))
-        first, second = split_stat(kept * inv)
-        near_out = out_ref[0, cols, :]
+        lows.append((terms * inv).astype(BF16))
+        peaks.append(peak)
+        kepts.append(kept)
+        invs.append(inv)
+    far_outs = [own_heads(nn(fvt_ref[0, cols[c], :], lows[c])) for c in range(pairs)]
+    atts = []
+    for c in range(pairs):
+        first, second = split_stat(kepts[c] * invs[c])
+        near_out = out_ref[0, cols[c], :]
         near_out = jnp.concatenate([near_out[:mid] * first, near_out[mid:] * second], axis=0)
-        att = (far_out + near_out).astype(BF16).astype(F32)
-        att_ref[:, cols] = att.T.astype(BF16)
-        prod = cot_ref[:, cols].astype(F32).T * att
+        atts.append((far_outs[c] + near_out).astype(BF16).astype(F32))
+    for c in range(pairs):
+        att_ref[:, cols[c]] = atts[c].T.astype(BF16)
+        prod = turned_cot[c] * atts[c]
         delta = jnp.concatenate(
             [jnp.sum(prod[:mid], axis=0, keepdims=True), jnp.sum(prod[mid:], axis=0, keepdims=True)], axis=1
         )
-        store_rows(stats_ref, c, (peak, inv, delta))
-        store_rows(slot_ref, c, (peak, inv, delta))
+        store_rows(stats_ref, c, (peaks[c], invs[c], delta))
+        store_rows(slot_ref, c, (peaks[c], invs[c], delta))
 
 
 def own_kernel(near_ids, meta, q_ref, cot_ref, tile_ref, stats_ref, k_ref, v_ref, kt_ref, fk_ref, fv_ref, fkt_ref,
@@ -155,14 +172,14 @@
     ]
 
 
-def key_terms(k, v, qz, cz, bias, stats):
-    peak, inv, delta = stats
-    scores = nt(k, qz)
-    if bias is not None:
-        scores = scores + bias
-    probs = jnp.exp(scores - peak) * inv
-    ds = (probs * (nt(v, cz) - delta)).astype(BF16)
-    return nn(ds, qz), nn(probs.astype(BF16), cz)
+def key_terms(ks, vs, qzs, czs, bias, stats):
+    scores = [nt(k, qz) for k, qz in zip(ks, qzs)]
+    grads = [nt(v, cz) for v, cz in zip(vs, czs)]
+    probs = [
+        jnp.exp((s if bias is None else s + bias) - peak) * inv for s, (peak, inv, _) in zip(scores, stats)
+    ]
+    ds = [(p * (g - delta)).astype(BF16) for p, g, (_, _, delta) in zip(probs, grads, stats)]
+    return [nn(d, qz) for d, qz in zip(ds, qzs)], [nn(p.astype(BF16), cz) for p, cz in zip(probs, czs)]
 
 
 def peer_kernel(near_ids, meta, q_ref, cot_ref, stats_ref, tile_ref, k_ref, v_ref, acc_in, acc_ref, qz_scr, cz_scr):
@@ -184,37 +201,40 @@
 
         @pl.when(n < own)
         def _(j=j, n=n):
-            bias = bias_of(tile_ref[0, j])
-            for c in range(pairs):
-                cols = slice(c * LANES, (c + 1) * LANES)
-                vcols = slice(width + c * LANES, width + (c + 1) * LANES)
-                dk, dv = key_terms(
-                    k_ref[n, :, cols], v_ref[n, :, cols], qz_scr[c], cz_scr[c], bias, load_rows(stats_ref, c, 3)
-                )
-                acc_ref[n, :, cols] += dk
-                acc_ref[n, :, vcols] += dv
+            every = range(pairs)
+            cols = [slice(c * LANES, (c + 1) * LANES) for c in every]
+            dks, dvs = key_terms(
+                [k_ref[n, :, cols[c]] for c in every], [v_ref[n, :, cols[c]] for c in every],
+                [qz_scr[c] for c in every], [cz_scr[c] for c in every], bias_of(tile_ref[0, j]),
+                [load_rows(stats_ref, c, 3) for c in every],
+            )
+            for c in every:
+                acc_ref[n, :, cols[c]] += dks[c]
+                acc_ref[n, :, width + c * LANES : width + (c + 1) * LANES] += dvs[c]
 
 
 def far_kernel(meta, q_ref, cot_ref, stats_ref, k_ref, v_ref, acc_ref, dkv_ref):
-    pairs = q_ref.shape[1] // LANES
     width = q_ref.shape[1]
-    for c in range(pairs):
-        cols = slice(c * LANES, (c + 1) * LANES)
+    every = range(width // LANES)
+    cols = [slice(c * LANES, (c + 1) * LANES) for c in every]
+    dks, dvs = key_terms(
+        [k_ref[0, :, cols[c]] for c in every], [v_ref[0, :, cols[c]] for c in every],
+        [two_heads(q_ref[:, cols[c]]) for c in every], [two_heads(cot_ref[:, cols[c]]) for c in every], None,
+        [load_rows(stats_ref, c, 3) for c in every],
+    )
+    for c in every:
         vcols = slice(width + c * LANES, width + (c + 1) * LANES)
-        dk, dv = key_terms(
-            k_ref[0, :, cols], v_ref[0, :, cols], two_heads(q_ref[:, cols]), two_heads(cot_ref[:, cols]), None,
-            load_rows(stats_ref, c, 3),
-        )
-        dkv_ref[:, cols] = (acc_ref[0, :, cols] + dk.astype(BF16).astype(F32)).astype(BF16)
-        dkv_ref[:, vcols] = (acc_ref[0, :, vcols] + dv.astype(BF16).astype(F32)).astype(BF16)
+        dkv_ref[:, cols[c]] = (acc_ref[0, :, cols[c]] + dks[c].astype(BF16).astype(F32)).astype(BF16)
+        dkv_ref[:, vcols] = (acc_ref[0, :, vcols] + dvs[c].astype(BF16).astype(F32)).astype(BF16)
 
 
 def project_kernel(x_ref, w_ref, wt_ref, *rest):
     qkv_ref, t_ref = rest[-2:]
     bs = t_ref.shape[2]
     qkv_ref[...] = nn(x_ref[...], w_ref[...]).astype(BF16)
+    turned = nt(wt_ref[...], x_ref[...]).astype(BF16)
     for b in range(t_ref.shape[0]):
-        t_ref[b] = nt(wt_ref[...], x_ref[b * bs : (b + 1) * bs, :]).astype(BF16)
+        t_ref[b] = turned[:, b * bs : (b + 1) * bs]
 
 
 def call(kernel, scalars, steps, in_specs, out_specs, out_shape, scratch, flops, touched, name, aliases={}):
@@ -271,9 +291,8 @@
     digits = jnp.pad(digits, ((0, 0), (0, LANES - 2)))
     digits = jnp.broadcast_to(digits[None], (devices, own, LANES))
     first_hop = jnp.concatenate([spread(node_feats), digits], axis=2)
-    first_hop, feats_out = lax.optimization_barrier((first_hop, node_feats))
     rows_in = exchange(first_hop)
-    peer_feats = swap(feats_out)
+    peer_feats = swap(node_feats)
     cot = jnp.dot(layer_cot, w_out.T, preferred_element_type=F32).astype(BF16)
     cot_rows = spread(cot)
 
@@ -355,9 +374,7 @@
         ],
         [], own * 4 * pair_flops, 6 << 20, "far_forward",
     )(meta, part_qkv, cot, far_blk, far_t, near_out, sums)
-    far_cot, slots, stats = lax.optimization_barrier((far_cot, slots, stats))
     peer_stats = swap(stats)
-    far_slots = exchange(slots)
     pairs = width // LANES
     dq, acc = call(
         own_kernel, 2, own,
@@ -373,7 +390,8 @@
         ],
         own * 24 * pair_flops, 30 << 20, "own_backward",
     )(near_ids, meta, part_qkv, cot, tiles, stats, part_blk, part_blk, part_t, far_blk, far_blk, far_t)
-    acc, peer_stats, peer_cot = lax.optimization_barrier((acc, peer_stats, peer_cot))
+    acc, peer_stats, peer_cot, far_cot, slots = lax.optimization_barrier((acc, peer_stats, peer_cot, far_cot, slots))
+    far_slots = exchange(slots)
     far_cot = far_cot.transpose(1, 0, 2).reshape(rows, width)
 
     layer_out = jnp.dot(att, w_out, preferred_element_type=F32).astype(BF16)

time: 276 us -> 240 us (0.87)
  Pallas kernels: 107 us -> 90.4 us
  starting transfers between devices: 66.9 us -> 54.5 us
  waiting for transfers between devices: 45.9 us -> 39.9 us
    ppermute x3, waiting for transfers between devices: 18.4 us -> 5.14 us  [swap(): return lax.ppermute(x, 'head', [(0, 1), (1, 0)])]
    all_to_all x5, starting transfers between devices: 58.1 us -> 45.8 us  [exchange(): return lax.all_to_all(x, DEVICES, split_axis=0, concat_axis=0, tiled=True)]
    pallas_call x1, Pallas kernels: 24.1 us -> 15.6 us  [body(): call(peer_kernel, 2, own, [pl.BlockSpec((bs, width), lambda i, *s: (own +...]
    all_to_all x5, waiting for transfers between devices: 27.4 us -> 34.8 us  [exchange(): return lax.all_to_all(x, DEVICES, split_axis=0, concat_axis=0, tiled=True)]
    pallas_call x1, Pallas kernels: 16.2 us -> 12.7 us  [body(): call(near_kernel, 2, own, [rows_spec, tile_spec, k_spec, vt_spec], [pl.Bl...]
    unnamed x33 -> x31, local copies, waits for them, and re-layouts: 6.97 us -> 5.37 us
  transfers between devices with their start and end apart: 8 -> 8, of which waited for: 3 -> 5; matrix products, arithmetic and copies ran while one was open for 9% -> 13% of each run, Pallas kernels for 35% -> 34%
where the time goes in v5:
time: 240 us; the launch traced here: 237 us
  Pallas kernels  90.4 us (38%)
  starting transfers between devices  54.5 us (23%)
  waiting for transfers between devices  39.9 us (17%)
  local copies, waits for them, and re-layouts  20.1 us (8%)
  matrix products  18.4 us (8%)
  other arithmetic  12.7 us (5%)
    all_to_all x5, starting transfers between devices, exchange(): return lax.all_to_all(x, DEVICES, split_axis=0, concat_axis=0, tiled=True)  45.8 us
    all_to_all x5, waiting for transfers between devices, exchange(): return lax.all_to_all(x, DEVICES, split_axis=0, concat_axis=0, tiled=True)  34.8 us
    pallas_call x1, Pallas kernels, body(): call(own_kernel, 2, own, [rows_spec, rows_spec, tile_spec, stats_spec, k_...  23.8 us
    pallas_call x3, Pallas kernels, project(): call(project_kernel, 0, own // per, [pl.BlockSpec((per * bs, width), lamb...  19.1 us
    pallas_call x1, Pallas kernels, body(): call(peer_kernel, 2, own, [pl.BlockSpec((bs, width), lambda i, *s: (own +...  15.6 us
    pallas_call x1, Pallas kernels, body(): call(near_kernel, 2, own, [rows_spec, tile_spec, k_spec, vt_spec], [pl.Bl...  12.7 us
    pallas_call x1, Pallas kernels, body(): call(far_kernel, 1, own, [pl.BlockSpec((bs, width), step), pl.BlockSpec((...  9.8 us
    pallas_call x1, Pallas kernels, body(): call(merge_kernel, 1, own, [rows_spec, rows_spec, far_k_spec, far_vt_spec...  9.4 us
  transfers between devices with their start and end apart: 8, of which 5 were waited for; matrix products, arithmetic and copies ran while one was open for 13% of the time, Pallas kernels for 34%

profile of v5, /device:TPU:0, one launch (start us, length us, event | category | flops | bytes accessed | tf_op | source)
XLA Modules:
  0.0 237.1 jit_solution(17013448752559959208)
XLA Ops:
  0.6 4.0 %collective-permute-start = (bf16[1024,512]{1,0:T(8,128)(2,1)}, bf16[1024,512]{1,0:T(8,128)(2,1)}, u32[]{:S(2)}, u32[]{:S(2)}) collective-permute-start(bf16[1024,512]{1,0:T(8,128)(2,1)} %x_ref.1), channel_id=1, source_target_pairs={{0,1},{1,0},{2,3},{3,2},{4,5},{5,4},{6,7},{7,6},{8,9},{9,8},{10,11... | collective-permute-start | bytes 3145736 | tf_op jit(solution)/shard_map/ppermute | solution.py:277
  7.0 1.9 copy.46
  8.8 8.5 %all-to-all-start = ((bf16[128,8,640]{2,1,0:T(8,128)(2,1)}), bf16[128,8,640]{2,1,0:T(8,128)(2,1)}, u32[]{:S(2)}, u32[]{:S(2)}) async-start(bf16[128,8,640]{2,1,0:T(8,128)(2,1)} %copy.46), calls=%async_computation | async-start | bytes 2621440 | tf_op jit(solution)/shard_map/all_to_all | solution.py:280
  17.4 1.7 convolution_convert_fusion.2.cot_ref
  19.1 2.8 %copy.60 = bf16[8,128,512]{2,0,1:T(8,128)(2,1)} copy(bf16[8,128,512]{2,1,0:T(8,128)(2,1)} %bitcast.5) | data formatting | bytes 2097152 | tf_op jit(solution)/shard_map/reshape | solution.py:283
  21.9 1.7 copy.48
  25.8 2.6 %copy.49.w_ref = bf16[512,1536]{1,0:T(8,128)(2,1)} copy(bf16[512,1536]{0,1:T(8,128)(2,1)} %pad_maximum_fusion.2) | data formatting | bytes 3145728 | tf_op jit(solution)/shard_map/concatenate | solution.py:274
  28.4 2.1 maximum_bitcast_fusion.wt_ref
  30.5 6.4 %project_own.1 = (bf16[2048,1536]{1,0:T(8,128)(2,1)}, bf16[16,1024,128]{2,1,0:T(8,128)(2,1)}) custom-call(bf16[1024,512]{1,0:T(8,128)(2,1)} %x_ref.1, bf16[512,1536]{1,0:T(8,128)(2,1)} %copy.49.w_ref, bf16[1024,512]{1,0:T(8,128)(2,1)} %maximum_bitcast_fusion.wt_ref), custom_call_target="tpu_custom_call" | custom-call | flops 2684354560 | bytes 8388608 | tf_op jit(solution)/shard_map/project_own/pallas_call | solution.py:304
  36.8 5.1 %collective-permute-done.x_ref = bf16[1024,512]{1,0:T(8,128)(2,1)} collective-permute-done((bf16[1024,512]{1,0:T(8,128)(2,1)}, bf16[1024,512]{1,0:T(8,128)(2,1)}, u32[]{:S(2)}, u32[]{:S(2)}) %collective-permute-start) | collective-permute-done | bytes 1048608 | tf_op jit(solution)/shard_map/ppermute | solution.py:277
  44.5 2.6 %fusion.18 = bf16[128,8,512]{2,1,0:T(8,128)(2,1)S(1)} fusion(f32[1024]{0:T(1024)S(1)} %iota_convert_fusion, f32[1024]{0:T(1024)S(1)} %multiply_reduce_fusion, bf16[128,8,640]{2,1,0:T(8,128)(2,1)} %all-to-all-done), kind=kOutput, calls=%fused_computation.20 | convolution fusion | flops 1075314688 | bytes 2105344 | tf_op jit(solution)/shard_map/dot_general | solution.py:286
  48.7 10.1 %all-to-all-start.1 = ((bf16[128,8,1024]{2,1,0:T(8,128)(2,1)}), bf16[128,8,1024]{2,1,0:T(8,128)(2,1)}, u32[]{:S(2)}, u32[]{:S(2)}) async-start(bf16[128,8,1024]{2,1,0:T(8,128)(2,1)} %pad_maximum_fusion), calls=%async_computation.1 | async-start | bytes 4194304 | tf_op jit(solution)/shard_map/all_to_all | solution.py:280
  60.3 6.4 %project_peer.1 = (bf16[2048,1536]{1,0:T(8,128)(2,1)}, bf16[16,1024,128]{2,1,0:T(8,128)(2,1)}) custom-call(bf16[1024,512]{1,0:T(8,128)(2,1)} %collective-permute-done.x_ref, bf16[512,1536]{1,0:T(8,128)(2,1)} %copy.49.w_ref, bf16[1024,512]{1,0:T(8,128)(2,1)} %maximum_bitcast_fusion.wt_ref, ...), custom_call_target="tpu_custom_call", output_to_operand_aliasing={{0}: (3, {}), {1}: (4, {})} | custom-call | flops 2684354560 | bytes 8388608 | tf_op jit(solution)/shard_map/project_peer/pallas_call | solution.py:304
  66.6 12.7 %near_forward.1 = (f32[8,512,128]{2,1,0:T(8,128)}, f32[8,16,128]{2,1,0:T(8,128)}) custom-call(s32[16,4]{1,0:T(8,128)} %copy.57.near_ids, s32[9]{0:T(128)} %pad_add_fusion.1.meta, bf16[2048,1536]{1,0:T(8,128)(2,1)} %get-tuple-element.38.q_ref, s32[16,4,128,128]{3,2,1,0:T(8,128)} %tile_ref.5, bf16[16,128,1536]{2,1,0:T(8,128)(2,1)} %bitcast.78, ...), custom_call_target="tpu_custom_call" | custom-call | flops 4294967296 | bytes 10485760 | tf_op jit(solution)/shard_map/near_forward/pallas_call | solution.py:343
  79.3 8.6 %all-to-all-done.1 = bf16[128,8,1024]{2,1,0:T(8,128)(2,1)} async-done(((bf16[128,8,1024]{2,1,0:T(8,128)(2,1)}), bf16[128,8,1024]{2,1,0:T(8,128)(2,1)}, u32[]{:S(2)}, u32[]{:S(2)}) %all-to-all-start.1) | async-done | bytes 2097184 | tf_op jit(solution)/shard_map/all_to_all | solution.py:280
  87.9 3.5 %fusion.15 = bf16[128,8,512]{2,1,0:T(8,128)(2,1)} fusion(f32[1024]{0:T(1024)S(1)} %iota_convert_fusion, f32[1024]{0:T(1024)S(1)} %multiply_reduce_fusion, bf16[128,8,1024]{2,1,0:T(8,128)(2,1)} %all-to-all-done.1), kind=kOutput, calls=%fused_computation.19 | convolution fusion | flops 1075314688 | bytes 2105344 | tf_op jit(solution)/shard_map/dot_general | solution.py:286
  91.4 2.0 collective-permute-start.2
  96.0 5.9 %all-to-all-start.2 = ((bf16[128,8,512]{2,1,0:T(8,128)(2,1)}), bf16[128,8,512]{2,1,0:T(8,128)(2,1)}, u32[]{:S(2)}, u32[]{:S(2)}) async-start(bf16[128,8,512]{2,1,0:T(8,128)(2,1)} %fusion.15), calls=%async_computation.2 | async-start | bytes 2097152 | tf_op jit(solution)/shard_map/all_to_all | solution.py:280
  102.0 6.4 %project_far.1 = (bf16[1024,1536]{1,0:T(8,128)(2,1)}, bf16[8,1024,128]{2,1,0:T(8,128)(2,1)}) custom-call(bf16[1024,512]{1,0:T(8,128)(2,1)} %bitcast.101, bf16[512,1536]{1,0:T(8,128)(2,1)} %copy.49.w_ref, bf16[1024,512]{1,0:T(8,128)(2,1)} %maximum_bitcast_fusion.wt_ref), custom_call_target="tpu_custom_call" | custom-call | flops 2684354560 | bytes 8388608 | tf_op jit(solution)/shard_map/project_far/pallas_call | solution.py:304
  108.4 9.4 %far_forward.1 = (bf16[1024,512]{1,0:T(8,128)(2,1)}, f32[8,24,128]{2,1,0:T(8,128)}, f32[128,24,128]{2,1,0:T(8,128)}) custom-call(s32[9]{0:T(128)} %pad_add_fusion.1.meta, bf16[2048,1536]{1,0:T(8,128)(2,1)} %get-tuple-element.38.q_ref, bf16[1024,512]{1,0:T(8,128)(2,1)} %convolution_convert_fusion.2.cot_ref, bf16[8,128,1536]{2,1,0:T(8,128)(2,1)} %bitcast.85, ...), custom_call_target="tpu_custom_call" | custom-call | flops 1073741824 | bytes 6291456 | tf_op jit(solution)/shard_map/far_forward/pallas_call | solution.py:365
  117.8 2.7 %collective-permute-start.1 = (f32[8,24,128]{2,1,0:T(8,128)}, f32[8,24,128]{2,1,0:T(8,128)S(1)}, u32[]{:S(2)}, u32[]{:S(2)}) collective-permute-start(f32[8,24,128]{2,1,0:T(8,128)} %get-tuple-element.51.stats_ref), channel_id=1, source_target_pairs={{0,1},{1,0},{2,3},{3,2},{4,5},{5,4},{6,7},{7,6},{8,9},{9,8},{10,11... | collective-permute-start | bytes 294920 | tf_op jit(solution)/shard_map/ppermute | solution.py:277
  120.4 23.8 %own_backward.1 = (bf16[1024,512]{1,0:T(8,128)(2,1)}, f32[8,128,1024]{2,1,0:T(8,128)}) custom-call(s32[16,4]{1,0:T(8,128)} %copy.57.near_ids, s32[9]{0:T(128)} %pad_add_fusion.1.meta, bf16[2048,1536]{1,0:T(8,128)(2,1)} %get-tuple-element.38.q_ref, bf16[1024,512]{1,0:T(8,128)(2,1)} %convolution_convert_fusion.2.cot_ref, s32[16,4,128,128]{3,2,1,0:T(8,128)} %tile_ref.5, ...), custom_call_target="tpu_custom_call" | custom-call | flops 6442450944 | bytes 31457280 | tf_op jit(solution)/shard_map/own_backward/pallas_call | solution.py:379
  144.3 9.9 %all-to-all-start.3 = ((f32[128,24,128]{2,1,0:T(8,128)}), f32[128,24,128]{2,1,0:T(8,128)}, u32[]{:S(2)}, u32[]{:S(2)}) async-start(f32[128,24,128]{2,1,0:T(8,128)} %get-tuple-element.58), calls=%async_computation.3 | async-start | bytes 3145728 | tf_op jit(solution)/shard_map/all_to_all | solution.py:280
  154.2 2.4 %fusion.22 = bf16[64,8,512]{2,1,0:T(8,128)(2,1)S(1)} fusion(bf16[1024,512]{1,0:T(8,128)(2,1)} %get-tuple-element.52, bf16[1024,512]{1,0:T(8,128)(2,1)} %x_ref.1), kind=kOutput, calls=%fused_computation.25 | convolution fusion | flops 537133056 | bytes 2621440 | tf_op jit(solution)/shard_map/rd,rc->dc/dot_general | solution.py:399
  158.2 2.5 %copy.55 = bf16[8,128,512]{2,1,0:T(8,128)(2,1)} copy(bf16[8,128,512]{2,0,1:T(8,128)(2,1)} %bitcast.26) | data formatting | bytes 2097152 | tf_op jit(solution)/shard_map/transpose | solution.py:395
  160.7 15.6 %peer_queries.1.acc_ref = f32[8,128,1024]{2,1,0:T(8,128)} custom-call(s32[16,4]{1,0:T(8,128)} %copy.57.near_ids, s32[9]{0:T(128)} %pad_add_fusion.1.meta, bf16[2048,1536]{1,0:T(8,128)(2,1)} %get-tuple-element.38.q_ref, bf16[1024,512]{1,0:T(8,128)(2,1)} %collective-permute-done.2.cot_ref, f32[8,24,128]{2,1,0:T(8,128)} %copy-done.7, ...), custom_call_target="tpu_custom_call" | custom-call | flops 4294967296 | bytes 20971520 | tf_op jit(solution)/shard_map/peer_queries/pallas_call | solution.py:401
  176.3 1.7 all-to-all-done.3.stats_ref
  178.0 9.8 %far_queries.1 = bf16[1024,1024]{1,0:T(8,128)(2,1)} custom-call(s32[9]{0:T(128)} %pad_add_fusion.1.meta, bf16[1024,1536]{1,0:T(8,128)(2,1)} %get-tuple-element.46.q_ref, bf16[1024,512]{1,0:T(8,128)(2,1)} %bitcast.96, f32[128,24,128]{2,1,0:T(8,128)} %all-to-all-done.3.stats_ref, bf16[16,128,1536]{2,1,0:T(8,128)(2,1)} %bitcast.83, ...), custom_call_target="tpu_custom_call" | custom-call | flops 2147483648 | bytes 10485760 | tf_op jit(solution)/shard_map/far_queries/pallas_call | solution.py:421
  187.8 2.9 %fusion.14 = bf16[512,1024]{1,0:T(8,128)(2,1)S(1)} fusion(bf16[1024,1024]{1,0:T(8,128)(2,1)} %far_queries.1, bf16[1024,512]{1,0:T(8,128)(2,1)S(1)} %copy-done.4), kind=kOutput, calls=%fused_computation.18 | convolution fusion | flops 1074266112 | bytes 4194304 | tf_op jit(solution)/shard_map/rd,rc->dc/dot_general | solution.py:436
  193.4 11.3 %all-to-all-start.4 = ((bf16[128,8,1024]{2,1,0:T(8,128)(2,1)}), bf16[128,8,1024]{2,1,0:T(8,128)(2,1)}, u32[]{:S(2)}, u32[]{:S(2)}) async-start(bf16[128,8,1024]{2,1,0:T(8,128)(2,1)} %bitcast.90), calls=%async_computation.4 | async-start | bytes 4194304 | tf_op jit(solution)/shard_map/all_to_all | solution.py:280
  210.7 23.2 %all-to-all-done.4 = bf16[128,8,1024]{2,1,0:T(8,128)(2,1)} async-done(((bf16[128,8,1024]{2,1,0:T(8,128)(2,1)}), bf16[128,8,1024]{2,1,0:T(8,128)(2,1)}, u32[]{:S(2)}, u32[]{:S(2)}) %all-to-all-start.4) | async-done | bytes 2097184 | tf_op jit(solution)/shard_map/all_to_all | solution.py:280
  233.9 2.0 convert_reduce_fusion
  (65 shorter events, 24.0 us)
Async XLA Ops:
  0.6 16.7 %copy-start = (bf16[1024,512]{1,0:T(8,128)(2,1)S(1)}, bf16[1024,512]{1,0:T(8,128)(2,1)}, u32[]{:S(2)}) copy-start(bf16[1024,512]{1,0:T(8,128)(2,1)} %param.14) | copy-start | bytes 3145732
  0.6 41.3 %collective-permute-start = (bf16[1024,512]{1,0:T(8,128)(2,1)}, bf16[1024,512]{1,0:T(8,128)(2,1)}, u32[]{:S(2)}, u32[]{:S(2)}) collective-permute-start(bf16[1024,512]{1,0:T(8,128)(2,1)} %x_ref.1), channel_id=1, source_target_pairs={{0,1},{1,0},{2,3},{3,2},{4,5},{5,4},{6,7},{7,6},{8,9},{9,8},{10,11... | collective-permute-start | bytes 3145736 | tf_op jit(solution)/shard_map/ppermute | solution.py:277
  6.9 10.4 %copy-start.12 = (bf16[512,512]{1,0:T(8,128)(2,1)S(1)}, bf16[512,512]{1,0:T(8,128)(2,1)}, u32[]{:S(2)}) copy-start(bf16[512,512]{1,0:T(8,128)(2,1)} %param.10) | copy-start | bytes 1572868
  8.8 34.4 %all-to-all-start = ((bf16[128,8,640]{2,1,0:T(8,128)(2,1)}), bf16[128,8,640]{2,1,0:T(8,128)(2,1)}, u32[]{:S(2)}, u32[]{:S(2)}) async-start(bf16[128,8,640]{2,1,0:T(8,128)(2,1)} %copy.46), calls=%async_computation | async-start | bytes 2621440 | tf_op jit(solution)/shard_map/all_to_all | solution.py:280
  23.7 0.8 copy-start.1
  30.5 12.8 %copy-start.9 = (f32[128]{0:T(128)S(1)}, f32[128]{0:T(128)}, u32[]{:S(2)}) copy-start(f32[128]{0:T(128)} %constant.92) | copy-start | bytes 1540
  44.5 2.6 %copy-start.2 = (bf16[8,128,512]{2,0,1:T(8,128)(2,1)S(1)}, bf16[8,128,512]{2,0,1:T(8,128)(2,1)}, u32[]{:S(2)}) copy-start(bf16[8,128,512]{2,0,1:T(8,128)(2,1)} %copy.60) | copy-start | bytes 3145732
  48.7 10.1 %copy-start.8 = (s32[16,4]{0,1:T(4,128)S(1)}, s32[16,4]{0,1:T(4,128)}, u32[]{:S(2)}) copy-start(s32[16,4]{0,1:T(4,128)} %param.11) | copy-start | bytes 772
  48.7 39.2 %all-to-all-start.1 = ((bf16[128,8,1024]{2,1,0:T(8,128)(2,1)}), bf16[128,8,1024]{2,1,0:T(8,128)(2,1)}, u32[]{:S(2)}, u32[]{:S(2)}) async-start(bf16[128,8,1024]{2,1,0:T(8,128)(2,1)} %pad_maximum_fusion), calls=%async_computation.1 | async-start | bytes 4194304 | tf_op jit(solution)/shard_map/all_to_all | solution.py:280
  91.4 52.8 %collective-permute-start.2 = (bf16[1024,512]{1,0:T(8,128)(2,1)}, bf16[1024,512]{1,0:T(8,128)(2,1)}, u32[]{:S(2)}, u32[]{:S(2)}) collective-permute-start(bf16[1024,512]{1,0:T(8,128)(2,1)} %convolution_convert_fusion.2.cot_ref), channel_id=1, source_target_pairs={{0,1},{1,0},{2,3},{3,2},{4,5},{5,4},{6,7},{7,6},{8,9},{9,8},{10,11... | collective-permute-start | bytes 3145736 | tf_op jit(solution)/shard_map/ppermute | solution.py:277
  96.0 48.2 %all-to-all-start.2 = ((bf16[128,8,512]{2,1,0:T(8,128)(2,1)}), bf16[128,8,512]{2,1,0:T(8,128)(2,1)}, u32[]{:S(2)}, u32[]{:S(2)}) async-start(bf16[128,8,512]{2,1,0:T(8,128)(2,1)} %fusion.15), calls=%async_computation.2 | async-start | bytes 2097152 | tf_op jit(solution)/shard_map/all_to_all | solution.py:280
  117.8 26.5 %collective-permute-start.1 = (f32[8,24,128]{2,1,0:T(8,128)}, f32[8,24,128]{2,1,0:T(8,128)S(1)}, u32[]{:S(2)}, u32[]{:S(2)}) collective-permute-start(f32[8,24,128]{2,1,0:T(8,128)} %get-tuple-element.51.stats_ref), channel_id=1, source_target_pairs={{0,1},{1,0},{2,3},{3,2},{4,5},{5,4},{6,7},{7,6},{8,9},{9,8},{10,11... | collective-permute-start | bytes 294920 | tf_op jit(solution)/shard_map/ppermute | solution.py:277
  144.2 12.4 %copy-start.7 = (f32[8,24,128]{2,1,0:T(8,128)}, f32[8,24,128]{2,1,0:T(8,128)S(1)}, u32[]{:S(2)}) copy-start(f32[8,24,128]{2,1,0:T(8,128)S(1)} %collective-permute-done.1.stats_ref) | copy-start | bytes 294916
  144.3 33.7 %all-to-all-start.3 = ((f32[128,24,128]{2,1,0:T(8,128)}), f32[128,24,128]{2,1,0:T(8,128)}, u32[]{:S(2)}, u32[]{:S(2)}) async-start(f32[128,24,128]{2,1,0:T(8,128)} %get-tuple-element.58), calls=%async_computation.3 | async-start | bytes 3145728 | tf_op jit(solution)/shard_map/all_to_all | solution.py:280
  154.2 2.5 %copy-start.10 = (bf16[1024,512]{1,0:T(8,128)(2,1)S(1)}, bf16[1024,512]{1,0:T(8,128)(2,1)}, u32[]{:S(2)}) copy-start(bf16[1024,512]{1,0:T(8,128)(2,1)} %get-tuple-element.50) | copy-start | bytes 3145732
  178.0 9.8 %copy-start.4 = (bf16[1024,512]{1,0:T(8,128)(2,1)S(1)}, bf16[1024,512]{1,0:T(8,128)(2,1)}, u32[]{:S(2)}) copy-start(bf16[1024,512]{1,0:T(8,128)(2,1)} %x_ref.1) | copy-start | bytes 3145732
  190.7 1.0 copy-start.6
  193.4 40.5 %all-to-all-start.4 = ((bf16[128,8,1024]{2,1,0:T(8,128)(2,1)}), bf16[128,8,1024]{2,1,0:T(8,128)(2,1)}, u32[]{:S(2)}, u32[]{:S(2)}) async-start(bf16[128,8,1024]{2,1,0:T(8,128)(2,1)} %bitcast.90), calls=%async_computation.4 | async-start | bytes 4194304 | tf_op jit(solution)/shard_map/all_to_all | solution.py:280
  204.8 1.2 copy-start.11
  204.8 1.3 copy-start.13
  206.1 1.7 copy-start.3
  207.8 1.3 copy-start.5

commit v6 on v5

--- a/solution.py
+++ b/solution.py
@@ -56,7 +56,8 @@
     def scores_of(c):
         cols = slice(c * LANES, (c + 1) * LANES)
         qz = two_heads(q_ref[:, cols])
-        return jnp.concatenate([nt(k_ref[ids[j], :, cols], qz) + bias_scr[j] for j in range(NBR)], axis=0)
+        keys = jnp.concatenate([k_ref[ids[j], :, cols] for j in range(NBR)], axis=0)
+        return nt(keys, qz) + bias_scr[...].reshape(keys.shape[0], qz.shape[0])
 
     ready = scores_of(0)
     for c in range(pairs):
@@ -77,12 +78,11 @@
             ref[0, at : at + 1, :] = part
 
 
-def merge_kernel(meta, q_ref, cot_ref, fk_ref, fvt_ref, out_ref, sums_ref, att_ref, stats_ref, slot_ref):
+def merge_kernel(meta, q_ref, cot_t_ref, fk_ref, fvt_ref, out_ref, sums_ref, att_ref, stats_ref, slot_ref):
     mid = LANES // 2
     pairs = q_ref.shape[1] // LANES
     cols = [slice(c * LANES, (c + 1) * LANES) for c in range(pairs)]
     scores = [nt(fk_ref[0, :, cols[c]], two_heads(q_ref[:, cols[c]])) for c in range(pairs)]
-    turned_cot = [cot_ref[:, cols[c]].astype(F32).T for c in range(pairs)]
     peaks, kepts, invs, lows = [], [], [], []
     for c in range(pairs):
         near_peak, near_total = load_rows(sums_ref, c, 2)
@@ -102,8 +102,8 @@
         near_out = jnp.concatenate([near_out[:mid] * first, near_out[mid:] * second], axis=0)
         atts.append((far_outs[c] + near_out).astype(BF16).astype(F32))
     for c in range(pairs):
-        att_ref[:, cols[c]] = atts[c].T.astype(BF16)
-        prod = turned_cot[c] * atts[c]
+        att_ref[0, cols[c], :] = atts[c].astype(BF16)
+        prod = cot_t_ref[0, cols[c], :].astype(F32) * atts[c]
         delta = jnp.concatenate(
             [jnp.sum(prod[:mid], axis=0, keepdims=True), jnp.sum(prod[mid:], axis=0, keepdims=True)], axis=1
         )
@@ -111,8 +111,18 @@
         store_rows(slot_ref, c, (peaks[c], invs[c], delta))
 
 
+def deal(dw_scr, kept_ref, given_ref, core):
+    groups, span = kept_ref.shape[0], kept_ref.shape[3] // 2
+    for g in range(groups):
+        for t in range(2):
+            at = (t * groups + g) * span
+            kept_ref[g, :, :, t * span : (t + 1) * span] = dw_scr[:, core, :, at : at + span]
+            given_ref[g, :, :, t * span : (t + 1) * span] = dw_scr[:, 1 - core, :, at : at + span]
+
+
 def own_kernel(near_ids, meta, q_ref, cot_ref, tile_ref, stats_ref, k_ref, v_ref, kt_ref, fk_ref, fv_ref, fkt_ref,
-               dq_ref, acc_ref, p_scr, ds_scr, qz_scr, cz_scr, bias_scr):
+               xt_ref, ct_ref, att_ref, dq_ref, acc_ref, kept_ref, given_ref, p_scr, ds_scr, qz_scr, cz_scr, bias_scr,
+               dw_scr):
     i = pl.program_id(0)
     bs, width = q_ref.shape
     pairs = width // LANES
@@ -121,6 +131,7 @@
     @pl.when(i == 0)
     def _():
         acc_ref[...] = jnp.zeros_like(acc_ref)
+        dw_scr[...] = jnp.zeros_like(dw_scr)
 
     for j in range(NBR):
         bias_scr[j] = bias_of(tile_ref[0, j])
@@ -132,23 +143,24 @@
         qz_scr[c] = qz
         cz_scr[c] = cz
         peak, inv, delta = load_rows(stats_ref, c, 3)
+        keys = jnp.concatenate([k_ref[ids[j], :, cols] for j in range(NBR)] + [fk_ref[0, :, cols]], axis=0)
+        values = jnp.concatenate([v_ref[ids[j], :, cols] for j in range(NBR)] + [fv_ref[0, :, cols]], axis=0)
+        all_scores = nt(keys, qz)
+        all_grads = nt(values, cz)
         parts = []
         for j in range(NBR + 1):
+            rows = slice(j * bs, (j + 1) * bs)
+            scores = all_scores[rows] + bias_scr[j] if j < NBR else all_scores[rows]
+            probs = jnp.exp(scores - peak) * inv
+            parts.append((probs * (all_grads[rows] - delta)).astype(BF16))
             if j < NBR:
-                scores = nt(k_ref[ids[j], :, cols], qz) + bias_scr[j]
-                grad_probs = nt(v_ref[ids[j], :, cols], cz)
-            else:
-                scores = nt(fk_ref[0, :, cols], qz)
-                grad_probs = nt(fv_ref[0, :, cols], cz)
-            probs = jnp.exp(scores - peak) * inv
-            parts.append((probs * (grad_probs - delta)).astype(BF16))
-            if j < NBR:
-                rows = slice(j * bs, (j + 1) * bs)
                 p_scr[c, rows, :] = probs.astype(BF16)
                 ds_scr[c, rows, :] = parts[j]
         kt = jnp.concatenate([kt_ref[ids[j], cols, :] for j in range(NBR)] + [fkt_ref[0, cols, :]], axis=1)
-        dq = own_heads(nn(kt, jnp.concatenate(parts, axis=0))) * 0.125
-        dq_ref[:, cols] = dq.T.astype(BF16)
+        dq_ref[0, cols, :] = (own_heads(nn(kt, jnp.concatenate(parts, axis=0))) * 0.125).astype(BF16)
+    half = dw_scr.shape[:3] + (width,)
+    dw_scr[:, :, :, :width] += nt(ct_ref[0], att_ref[0]).reshape(half)
+    dw_scr[:, :, :, width:] += nt(xt_ref[0], dq_ref[0]).reshape(half)
 
     for j in range(NBR):
 
@@ -161,6 +173,10 @@
                 rows = slice(j * bs, (j + 1) * bs)
                 acc_ref[n, :, cols] += nn(ds_scr[c, rows, :], qz_scr[c])
                 acc_ref[n, :, vcols] += nn(p_scr[c, rows, :], cz_scr[c])
+
+    @pl.when(i == own - 1)
+    def _():
+        deal(dw_scr, kept_ref, given_ref, meta[1 + own])
 
 
 def load_rows(ref, c, count):
@@ -213,8 +229,15 @@
                 acc_ref[n, :, width + c * LANES : width + (c + 1) * LANES] += dvs[c]
 
 
-def far_kernel(meta, q_ref, cot_ref, stats_ref, k_ref, v_ref, acc_ref, dkv_ref):
+def far_kernel(meta, q_ref, cot_ref, stats_ref, k_ref, v_ref, acc_ref, xt_ref, dkv_ref, kept_ref, given_ref, dw_scr):
     width = q_ref.shape[1]
+    i = pl.program_id(0)
+    own = pl.num_programs(0)
+
+    @pl.when(i == 0)
+    def _():
+        dw_scr[...] = jnp.zeros_like(dw_scr)
+
     every = range(width // LANES)
     cols = [slice(c * LANES, (c + 1) * LANES) for c in every]
     dks, dvs = key_terms(
@@ -226,15 +249,23 @@
         vcols = slice(width + c * LANES, width + (c + 1) * LANES)
         dkv_ref[:, cols[c]] = (acc_ref[0, :, cols[c]] + dks[c].astype(BF16).astype(F32)).astype(BF16)
         dkv_ref[:, vcols] = (acc_ref[0, :, vcols] + dvs[c].astype(BF16).astype(F32)).astype(BF16)
+    dw_scr[...] += nn(xt_ref[0], dkv_ref[...]).reshape(dw_scr.shape)
+
+    @pl.when(i == own - 1)
+    def _():
+        deal(dw_scr, kept_ref, given_ref, meta[1 + own])
 
 
 def project_kernel(x_ref, w_ref, wt_ref, *rest):
     qkv_ref, t_ref = rest[-2:]
     bs = t_ref.shape[2]
     qkv_ref[...] = nn(x_ref[...], w_ref[...]).astype(BF16)
-    turned = nt(wt_ref[...], x_ref[...]).astype(BF16)
-    for b in range(t_ref.shape[0]):
-        t_ref[b] = turned[:, b * bs : (b + 1) * bs]
+
+    @pl.when(pl.program_id(0) < 2)
+    def _():
+        turned = nt(wt_ref[...], x_ref[...]).astype(BF16)
+        for b in range(t_ref.shape[0]):
+            t_ref[b] = turned[:, b * bs : (b + 1) * bs]
 
 
 def call(kernel, scalars, steps, in_specs, out_specs, out_shape, scratch, flops, touched, name, aliases={}):
@@ -268,7 +299,8 @@
 
     near_ids = jnp.roll((neighbours - base) % blocks, -base, axis=0)
     mine = lax.dynamic_slice_in_dim(partner, base, own, 0)
-    meta = jnp.concatenate([base[None].astype(jnp.int32), mine // own])
+    core = lax.axis_index("dom") % 2
+    meta = jnp.concatenate([base[None].astype(jnp.int32), mine // own, core[None].astype(jnp.int32)])
 
     w_by = w_qkv.reshape(width, groups, 3, span).transpose(2, 0, 1, 3).reshape(3, width, width)
     w_all = jnp.concatenate([w_by[0] * jnp.asarray(0.125, BF16), w_by[1], w_by[2]], axis=1)
@@ -295,23 +327,23 @@
     peer_feats = swap(node_feats)
     cot = jnp.dot(layer_cot, w_out.T, preferred_element_type=F32).astype(BF16)
     cot_rows = spread(cot)
+    cot_t = jnp.einsum("ck,brk->bcr", w_out, layer_cot.reshape(own, bs, width), preferred_element_type=F32).astype(BF16)
 
     w_turned = w_all[:, width:].T
     hold = pl.BlockSpec(memory_space=pl.ANY)
 
     def project(feats, total, at, carried, name):
-        per = 2
         return call(
-            project_kernel, 0, own // per,
+            project_kernel, 0, 3,
             [
-                pl.BlockSpec((per * bs, width), lambda i: (i, 0)),
-                once((width, 3 * width)),
-                once((2 * width, width)),
+                once((rows, width)),
+                pl.BlockSpec((width, width), lambda i: (0, (i + 1) % 3)),
+                pl.BlockSpec((width, width), lambda i: (jnp.minimum(i, 1), 0)),
             ]
             + [hold] * len(carried),
             [
-                pl.BlockSpec((per * bs, 3 * width), lambda i: (at // per + i, 0)),
-                pl.BlockSpec((per, 2 * width, bs), lambda i: (at // per + i, 0, 0)),
+                pl.BlockSpec((rows, width), lambda i: (at, (i + 1) % 3)),
+                pl.BlockSpec((own, width, bs), lambda i: (at, jnp.minimum(i, 1), 0)),
             ],
             [
                 jax.ShapeDtypeStruct((total * bs, 3 * width), BF16),
@@ -321,14 +353,18 @@
         )(feats, w_all, w_turned, *carried)
 
     own_part = project(node_feats, blocks, 0, (), "project_own")
-    rows_in, cot_rows, own_part, peer_feats = lax.optimization_barrier((rows_in, cot_rows, own_part, peer_feats))
+    feats_t = node_feats.reshape(own, bs, width).transpose(0, 2, 1)
+    out_t = layer_cot.reshape(own, bs, width).transpose(0, 2, 1)
+    rows_in, cot_rows, own_part, peer_feats, cot_t, feats_t, out_t = lax.optimization_barrier(
+        (rows_in, cot_rows, own_part, peer_feats, cot_t, feats_t, out_t)
+    )
 
     weigh = jnp.pad(jnp.asarray([DIGIT, 1], F32), (0, LANES - 2))
     ids = jnp.sum(rows_in.reshape(-1, width + LANES)[:, width:].astype(F32) * weigh[None], axis=1, keepdims=True)
     one_hot = (ids == jnp.arange(ids.shape[0], dtype=jnp.int32)[None, :].astype(F32)).astype(BF16)
     second = jnp.concatenate([gathered(rows_in[:, :, :width]), cot_rows], axis=2)
     second = exchange(second)
-    part_qkv, part_t = project(peer_feats, blocks, own, own_part, "project_peer")
+    part_qkv, part_t = project(peer_feats, blocks, 1, own_part, "project_peer")
     part_blk = part_qkv.reshape(blocks, bs, 3 * width)
     pair_flops = 2 * bs * bs * width * 2
     step = lambda i, *s: (i, 0)
@@ -340,6 +376,7 @@
     kt_spec = pl.BlockSpec((blocks, width, bs), lambda i, *s: (0, 0, 0), pipeline_mode=pl.Buffered(1))
     vt_spec = pl.BlockSpec((blocks, width, bs), lambda i, *s: (0, 1, 0), pipeline_mode=pl.Buffered(1))
     stats_spec = pl.BlockSpec((1, STATS, bs), row_step)
+    turned_spec = pl.BlockSpec((1, width, bs), row_step)
     near_out, sums = call(
         near_kernel, 2, own,
         [rows_spec, tile_spec, k_spec, vt_spec],
@@ -364,39 +401,53 @@
     far_vt_spec = pl.BlockSpec((1, width, bs), lambda i, *s: (i, 1, 0))
     att, stats, slots = call(
         merge_kernel, 1, own,
-        [rows_spec, rows_spec, far_k_spec, far_vt_spec, pl.BlockSpec((1, width, bs), row_step),
-         pl.BlockSpec((1, 2 * H, bs), row_step)],
-        [rows_spec, stats_spec, pl.BlockSpec((1, STATS, bs), lambda i, meta: (meta[1 + i], 0, 0))],
+        [rows_spec, turned_spec, far_k_spec, far_vt_spec, turned_spec, pl.BlockSpec((1, 2 * H, bs), row_step)],
+        [turned_spec, stats_spec, pl.BlockSpec((1, STATS, bs), lambda i, meta: (meta[1 + i], 0, 0))],
         [
-            jax.ShapeDtypeStruct((rows, width), BF16),
+            jax.ShapeDtypeStruct((own, width, bs), BF16),
             jax.ShapeDtypeStruct((own, STATS, bs), F32),
             jax.ShapeDtypeStruct((devices, STATS, bs), F32),
         ],
         [], own * 4 * pair_flops, 6 << 20, "far_forward",
-    )(meta, part_qkv, cot, far_blk, far_t, near_out, sums)
+    )(meta, part_qkv, cot_t, far_blk, far_t, near_out, sums)
     peer_stats = swap(stats)
     pairs = width // LANES
-    dq, acc = call(
+    piece = (groups, doms // 2, width // doms, width)
+    piece_spec = pl.BlockSpec(piece, lambda i, *s: (0, 0, 0, 0), pipeline_mode=pl.Buffered(1))
+    piece_out = jax.ShapeDtypeStruct(piece, F32)
+    dw_scratch = pltpu.VMEM((doms // 2, 2, width // doms, 2 * width), F32)
+    dq, acc, kept, given = call(
         own_kernel, 2, own,
-        [rows_spec, rows_spec, tile_spec, stats_spec, k_spec, v_spec, kt_spec, far_k_spec, far_v_spec, far_kt_spec],
-        [rows_spec, pl.BlockSpec((own, bs, 2 * width), lambda i, *s: (0, 0, 0))],
-        [jax.ShapeDtypeStruct((rows, width), BF16), jax.ShapeDtypeStruct((own, bs, 2 * width), F32)],
+        [rows_spec, rows_spec, tile_spec, stats_spec, k_spec, v_spec, kt_spec, far_k_spec, far_v_spec, far_kt_spec,
+         turned_spec, turned_spec, turned_spec],
+        [turned_spec, pl.BlockSpec((own, bs, 2 * width), lambda i, *s: (0, 0, 0)), piece_spec, piece_spec],
+        [
+            jax.ShapeDtypeStruct((own, width, bs), BF16),
+            jax.ShapeDtypeStruct((own, bs, 2 * width), F32),
+            piece_out,
+            piece_out,
+        ],
         [
             pltpu.VMEM((pairs, NBR * bs, 2 * bs), BF16),
             pltpu.VMEM((pairs, NBR * bs, 2 * bs), BF16),
             pltpu.VMEM((pairs, 2 * bs, LANES), BF16),
             pltpu.VMEM((pairs, 2 * bs, LANES), BF16),
             pltpu.VMEM((NBR, bs, 2 * bs), F32),
+            dw_scratch,
         ],
         own * 24 * pair_flops, 30 << 20, "own_backward",
-    )(near_ids, meta, part_qkv, cot, tiles, stats, part_blk, part_blk, part_t, far_blk, far_blk, far_t)
+    )(near_ids, meta, part_qkv, cot, tiles, stats, part_blk, part_blk, part_t, far_blk, far_blk, far_t,
+      feats_t, out_t, att)
     acc, peer_stats, peer_cot, far_cot, slots = lax.optimization_barrier((acc, peer_stats, peer_cot, far_cot, slots))
     far_slots = exchange(slots)
     far_cot = far_cot.transpose(1, 0, 2).reshape(rows, width)
 
-    layer_out = jnp.dot(att, w_out, preferred_element_type=F32).astype(BF16)
-    dwo_t = jnp.einsum("rc,ra->ca", layer_cot, att, preferred_element_type=F32).astype(BF16)
-    dwq = jnp.einsum("rd,rc->dc", node_feats, dq, preferred_element_type=F32).astype(BF16)
+    layer_out = jnp.einsum("bar,ac->brc", att, w_out, preferred_element_type=F32).astype(BF16).reshape(rows, width)
+
+    def paired(kept, given):
+        return (kept + lax.ppermute(given, "dom", [(d, d ^ 1) for d in range(doms)])).astype(BF16)
+
+    early = paired(kept, given)
 
     (acc,) = call(
         peer_kernel, 2, own,
@@ -418,7 +469,7 @@
         own * 16 * pair_flops, 20 << 20, "peer_queries",
     )(near_ids, meta, part_qkv, peer_cot, peer_stats, tiles, part_blk, part_blk, acc)
 
-    (dkv,) = call(
+    dkv, kept, given = call(
         far_kernel, 1, own,
         [
             pl.BlockSpec((bs, width), step),
@@ -427,26 +478,25 @@
             pl.BlockSpec((1, bs, width), lambda i, *s: (i, 0, 1)),
             pl.BlockSpec((1, bs, width), lambda i, *s: (i, 0, 2)),
             pl.BlockSpec((1, bs, 2 * width), lambda i, *s: (i, 0, 0)),
+            turned_spec,
         ],
-        [pl.BlockSpec((bs, 2 * width), step)],
-        [jax.ShapeDtypeStruct((rows, 2 * width), BF16)],
-        [], own * 8 * pair_flops, 10 << 20, "far_queries",
-    )(meta, far_qkv, far_cot, far_slots, part_blk, part_blk, acc)
-
-    dwkv = jnp.einsum("rd,rc->dc", node_feats, dkv, preferred_element_type=F32).astype(BF16)
-    parts = [w.reshape(doms, width // doms, width) for w in (dwo_t, dwq, dwkv[:, :width], dwkv[:, width:])]
-    split = jnp.stack(
-        [jnp.concatenate([w[:, :, g * span : (g + 1) * span] for w in parts], axis=2) for g in range(groups)], axis=1
-    )
-    moved = exchange(split.reshape(devices, width // doms, 4 * span))
+        [pl.BlockSpec((bs, 2 * width), step), piece_spec, piece_spec],
+        [jax.ShapeDtypeStruct((rows, 2 * width), BF16), piece_out, piece_out],
+        [dw_scratch], own * 8 * pair_flops, 10 << 20, "far_queries",
+    )(meta, far_qkv, far_cot, far_slots, part_blk, part_blk, acc, feats_t)
+
+    split = jnp.concatenate([early, paired(kept, given)], axis=2).reshape(devices // 2, 2 * width // doms, width)
+    same_core = [[d * groups + g for g in range(groups) for d in range(e, doms, 2)] for e in range(2)]
+    moved = lax.all_to_all(split, DEVICES, split_axis=0, concat_axis=0, axis_index_groups=same_core, tiled=True)
     summed = jnp.sum(moved.astype(F32), axis=0)
     w_plain = w_by.transpose(1, 0, 2).reshape(width, 3 * width)
     feat_grad = (
-        lax.dot_general(dq, w_plain[:, :width], (((1,), (1,)), ((), ())), preferred_element_type=F32)
+        jnp.einsum("bcr,dc->brd", dq, w_plain[:, :width], preferred_element_type=F32).reshape(rows, width)
         + lax.dot_general(dkv, w_plain[:, width:], (((1,), (1,)), ((), ())), preferred_element_type=F32)
     ).astype(BF16)
-    dw_out = summed[:, :span].T
-    dw_qkv = summed[:, span:]
+    deep = width // doms
+    dw_out = summed[:deep, :span].T
+    dw_qkv = jnp.concatenate([summed[:deep, span:], summed[deep:]], axis=1)
     return (layer_out, feat_grad, dw_qkv, dw_out)
 
 

time: 240 us -> 229 us (0.954)
  waiting for transfers between devices: 39.9 us -> 28.6 us
  Pallas kernels: 90.4 us -> 98.9 us
  matrix products: 18.4 us -> 13.4 us
    all_to_all x5 -> x4, waiting for transfers between devices: 34.8 us -> 12.2 us  [exchange(): return lax.all_to_all(x, DEVICES, split_axis=0, concat_axis=0, tiled=True)]
    all_to_all x0 -> x1, waiting for transfers between devices: none -> 13.6 us  [body(): lax.all_to_all(split, DEVICES, split_axis=0, concat_axis=0, axis_index_gr...]
    all_to_all x5 -> x4, starting transfers between devices: 45.8 us -> 35.7 us  [exchange(): return lax.all_to_all(x, DEVICES, split_axis=0, concat_axis=0, tiled=True)]
    all_to_all x0 -> x1, starting transfers between devices: none -> 8.29 us  [body(): lax.all_to_all(split, DEVICES, split_axis=0, concat_axis=0, axis_index_gr...]
    dot_general x5 -> x3, matrix products: 9.35 us -> 4.16 us  [the longest x1 1.71 us: body(): jnp.einsum('ck,brk->bcr', w_out, layer_cot.reshape(own, bs, width), prefe...]
    ppermute x3, waiting for transfers between devices: 5.14 us -> 1.56 us  [swap(): return lax.ppermute(x, 'head', [(0, 1), (1, 0)])]
    pallas_call x1, Pallas kernels: 9.8 us -> 12.5 us  [body(): call(far_kernel, 1, own, [pl.BlockSpec((bs, width), step), pl.BlockSpec((...]
    unnamed x31 -> x33, local copies, waits for them, and re-layouts: 5.37 us -> 4.39 us
  transfers between devices with their start and end apart: 8 -> 10, of which waited for: 5 -> 6; matrix products, arithmetic and copies ran while one was open for 13% -> 14% of each run, Pallas kernels for 34% -> 43%
where the time goes in v6:
time: 229 us; the launch traced here: 227 us
  Pallas kernels  98.9 us (43%)
  starting transfers between devices  53 us (23%)
  waiting for transfers between devices  28.6 us (12%)
  local copies, waits for them, and re-layouts  22.2 us (10%)
  matrix products  13.4 us (6%)
  other arithmetic  10.4 us (5%)
    all_to_all x4, starting transfers between devices, exchange(): return lax.all_to_all(x, DEVICES, split_axis=0, concat_axis=0, tiled=True)  35.7 us
    pallas_call x1, Pallas kernels, body(): call(own_kernel, 2, own, [rows_spec, rows_spec, tile_spec, stats_spec, k_...  26 us
    pallas_call x3, Pallas kernels, project(): call(project_kernel, 0, 3, [once((rows, width)), pl.BlockSpec((width, wid...  20.2 us
    pallas_call x1, Pallas kernels, body(): call(peer_kernel, 2, own, [pl.BlockSpec((bs, width), lambda i, *s: (own +...  17.3 us
    pallas_call x1, Pallas kernels, body(): call(near_kernel, 2, own, [rows_spec, tile_spec, k_spec, vt_spec], [pl.Bl...  13.7 us
    all_to_all x1, waiting for transfers between devices, body(): lax.all_to_all(split, DEVICES, split_axis=0, concat_axis=0, axis_index_gr...  13.6 us
    pallas_call x1, Pallas kernels, body(): call(far_kernel, 1, own, [pl.BlockSpec((bs, width), step), pl.BlockSpec((...  12.5 us
    all_to_all x4, waiting for transfers between devices, exchange(): return lax.all_to_all(x, DEVICES, split_axis=0, concat_axis=0, tiled=True)  12.2 us
  transfers between devices with their start and end apart: 10, of which 6 were waited for; matrix products, arithmetic and copies ran while one was open for 14% of the time, Pallas kernels for 43%

profile of v6, /device:TPU:0, one launch (start us, length us, event | category | flops | bytes accessed | tf_op | source)
XLA Modules:
  0.0 227.5 jit_solution(3254866073546191084)
XLA Ops:
  0.6 4.0 %collective-permute-start = (bf16[1024,512]{1,0:T(8,128)(2,1)}, bf16[1024,512]{1,0:T(8,128)(2,1)}, u32[]{:S(2)}, u32[]{:S(2)}) collective-permute-start(bf16[1024,512]{1,0:T(8,128)(2,1)} %x_ref.1), channel_id=1, source_target_pairs={{0,1},{1,0},{2,3},{3,2},{4,5},{5,4},{6,7},{7,6},{8,9},{9,8},{10,11... | collective-permute-start | bytes 3145736 | tf_op jit(solution)/shard_map/ppermute | solution.py:309
  7.0 1.9 copy.63
  8.8 8.5 %all-to-all-start = ((bf16[128,8,640]{2,1,0:T(8,128)(2,1)}), bf16[128,8,640]{2,1,0:T(8,128)(2,1)}, u32[]{:S(2)}, u32[]{:S(2)}) async-start(bf16[128,8,640]{2,1,0:T(8,128)(2,1)} %copy.63), calls=%async_computation | async-start | bytes 2621440 | tf_op jit(solution)/shard_map/all_to_all | solution.py:312
  20.7 1.7 copy.65
  23.8 2.6 %copy.66.w_ref = bf16[512,1536]{1,0:T(8,128)(2,1)} copy(bf16[512,1536]{0,1:T(8,128)(2,1)} %pad_maximum_fusion.1) | data formatting | bytes 3145728 | tf_op jit(solution)/shard_map/concatenate | solution.py:306
  26.4 2.3 copy.68
  28.7 2.3 %copy.69 = bf16[8,128,512]{1,2,0:T(8,128)(2,1)} copy(bf16[8,128,512]{2,1,0:T(8,128)(2,1)} %bitcast.100) | data formatting | bytes 2097152 | tf_op jit(solution)/shard_map/reshape | solution.py:330
  32.0 6.7 %project_own.1 = (bf16[2048,1536]{1,0:T(8,128)(2,1)}, bf16[16,1024,128]{2,1,0:T(8,128)(2,1)}) custom-call(bf16[1024,512]{1,0:T(8,128)(2,1)} %x_ref.1, bf16[512,1536]{1,0:T(8,128)(2,1)} %copy.66.w_ref, bf16[1024,512]{1,0:T(8,128)(2,1)} %maximum_bitcast_fusion.wt_ref), custom_call_target="tpu_custom_call" | custom-call | flops 2684354560 | bytes 8388608 | tf_op jit(solution)/shard_map/project_own/pallas_call | solution.py:336
  38.7 1.7 fusion.21.cot_t_ref
  40.4 1.6 collective-permute-done.x_ref
  44.5 2.6 %fusion.18 = bf16[128,8,512]{2,1,0:T(8,128)(2,1)S(1)} fusion(f32[1024]{0:T(1024)S(1)} %iota_convert_fusion, f32[1024]{0:T(1024)S(1)} %multiply_reduce_fusion, bf16[128,8,640]{2,1,0:T(8,128)(2,1)} %all-to-all-done), kind=kOutput, calls=%fused_computation.19 | convolution fusion | flops 1075314688 | bytes 2105344 | tf_op jit(solution)/shard_map/dot_general | solution.py:318
  47.1 1.6 pad_maximum_fusion
  48.7 10.1 %all-to-all-start.1 = ((bf16[128,8,1024]{2,1,0:T(8,128)(2,1)}), bf16[128,8,1024]{2,1,0:T(8,128)(2,1)}, u32[]{:S(2)}, u32[]{:S(2)}) async-start(bf16[128,8,1024]{2,1,0:T(8,128)(2,1)} %pad_maximum_fusion), calls=%async_computation.1 | async-start | bytes 4194304 | tf_op jit(solution)/shard_map/all_to_all | solution.py:312
  60.3 6.8 %project_peer.1 = (bf16[2048,1536]{1,0:T(8,128)(2,1)}, bf16[16,1024,128]{2,1,0:T(8,128)(2,1)}) custom-call(bf16[1024,512]{1,0:T(8,128)(2,1)} %collective-permute-done.x_ref, bf16[512,1536]{1,0:T(8,128)(2,1)} %copy.66.w_ref, bf16[1024,512]{1,0:T(8,128)(2,1)} %maximum_bitcast_fusion.wt_ref, ...), custom_call_target="tpu_custom_call", output_to_operand_aliasing={{0}: (3, {}), {1}: (4, {})} | custom-call | flops 2684354560 | bytes 8388608 | tf_op jit(solution)/shard_map/project_peer/pallas_call | solution.py:336
  67.1 13.7 %near_forward.1 = (f32[8,512,128]{2,1,0:T(8,128)}, f32[8,16,128]{2,1,0:T(8,128)}) custom-call(s32[16,4]{1,0:T(8,128)} %copy.82.near_ids, s32[10]{0:T(128)} %pad_add_fusion.1.meta, bf16[2048,1536]{1,0:T(8,128)(2,1)} %get-tuple-element.46.q_ref, s32[16,4,128,128]{3,2,1,0:T(8,128)} %tile_ref.5, bf16[16,128,1536]{2,1,0:T(8,128)(2,1)} %bitcast.72, ...), custom_call_target="tpu_custom_call" | custom-call | flops 4294967296 | bytes 10485760 | tf_op jit(solution)/shard_map/near_forward/pallas_call | solution.py:380
  80.9 7.0 %all-to-all-done.1 = bf16[128,8,1024]{2,1,0:T(8,128)(2,1)} async-done(((bf16[128,8,1024]{2,1,0:T(8,128)(2,1)}), bf16[128,8,1024]{2,1,0:T(8,128)(2,1)}, u32[]{:S(2)}, u32[]{:S(2)}) %all-to-all-start.1) | async-done | bytes 2097184 | tf_op jit(solution)/shard_map/all_to_all | solution.py:312
  87.9 3.6 %fusion.15 = bf16[128,8,512]{2,1,0:T(8,128)(2,1)} fusion(f32[1024]{0:T(1024)S(1)} %iota_convert_fusion, f32[1024]{0:T(1024)S(1)} %multiply_reduce_fusion, bf16[128,8,1024]{2,1,0:T(8,128)(2,1)} %all-to-all-done.1), kind=kOutput, calls=%fused_computation.18 | convolution fusion | flops 1075314688 | bytes 2105344 | tf_op jit(solution)/shard_map/dot_general | solution.py:318
  91.6 2.0 collective-permute-start.2
  96.2 5.8 %all-to-all-start.2 = ((bf16[128,8,512]{2,1,0:T(8,128)(2,1)}), bf16[128,8,512]{2,1,0:T(8,128)(2,1)}, u32[]{:S(2)}, u32[]{:S(2)}) async-start(bf16[128,8,512]{2,1,0:T(8,128)(2,1)} %fusion.15), calls=%async_computation.2 | async-start | bytes 2097152 | tf_op jit(solution)/shard_map/all_to_all | solution.py:312
  101.9 6.7 %project_far.1 = (bf16[1024,1536]{1,0:T(8,128)(2,1)}, bf16[8,1024,128]{2,1,0:T(8,128)(2,1)}) custom-call(bf16[1024,512]{1,0:T(8,128)(2,1)} %bitcast.103, bf16[512,1536]{1,0:T(8,128)(2,1)} %copy.66.w_ref, bf16[1024,512]{1,0:T(8,128)(2,1)} %maximum_bitcast_fusion.wt_ref), custom_call_target="tpu_custom_call" | custom-call | flops 2684354560 | bytes 8388608 | tf_op jit(solution)/shard_map/project_far/pallas_call | solution.py:336
  108.6 9.1 %far_forward.1 = (bf16[8,512,128]{2,1,0:T(8,128)(2,1)}, f32[8,24,128]{2,1,0:T(8,128)}, f32[128,24,128]{2,1,0:T(8,128)}) custom-call(s32[10]{0:T(128)} %pad_add_fusion.1.meta, bf16[2048,1536]{1,0:T(8,128)(2,1)} %get-tuple-element.46.q_ref, bf16[8,512,128]{2,1,0:T(8,128)(2,1)} %fusion.21.cot_t_ref, bf16[8,128,1536]{2,1,0:T(8,128)(2,1)} %bitcast.79, ...), custom_call_target="tpu_custom_call" | custom-call | flops 1073741824 | bytes 6291456 | tf_op jit(solution)/shard_map/far_forward/pallas_call | solution.py:402
  117.7 2.9 %collective-permute-start.1 = (f32[8,24,128]{2,1,0:T(8,128)}, f32[8,24,128]{2,1,0:T(8,128)S(1)}, u32[]{:S(2)}, u32[]{:S(2)}) collective-permute-start(f32[8,24,128]{2,1,0:T(8,128)} %get-tuple-element.60.stats_ref), channel_id=1, source_target_pairs={{0,1},{1,0},{2,3},{3,2},{4,5},{5,4},{6,7},{7,6},{8,9},{9,8},{10,11... | collective-permute-start | bytes 294920 | tf_op jit(solution)/shard_map/ppermute | solution.py:309
  120.5 26.0 %own_backward.1 = (bf16[8,512,128]{2,1,0:T(8,128)(2,1)}, f32[8,128,1024]{2,1,0:T(8,128)}, f32[2,32,8,512]{3,2,1,0:T(8,128)}, f32[2,32,8,512]{3,2,1,0:T(8,128)}) custom-call(s32[16,4]{1,0:T(8,128)} %copy.82.near_ids, s32[10]{0:T(128)} %pad_add_fusion.1.meta, bf16[2048,1536]{1,0:T(8,128)(2,1)} %get-tuple-element.46.q_ref, bf16[1024,512]{1,0:T(8,128)(2,1)} %copy-done.1, ...), custom_call_target="tpu_custom_call" | custom-call | flops 6442450944 | bytes 31457280 | tf_op jit(solution)/shard_map/own_backward/pallas_call | solution.py:419
  146.6 11.3 %all-to-all-start.3 = ((f32[128,24,128]{2,1,0:T(8,128)}), f32[128,24,128]{2,1,0:T(8,128)}, u32[]{:S(2)}, u32[]{:S(2)}) async-start(f32[128,24,128]{2,1,0:T(8,128)} %get-tuple-element.69), calls=%async_computation.3 | async-start | bytes 3145728 | tf_op jit(solution)/shard_map/all_to_all | solution.py:312
  158.1 17.3 %peer_queries.1.acc_ref = f32[8,128,1024]{2,1,0:T(8,128)} custom-call(s32[16,4]{1,0:T(8,128)} %copy.82.near_ids, s32[10]{0:T(128)} %pad_add_fusion.1.meta, bf16[2048,1536]{1,0:T(8,128)(2,1)} %get-tuple-element.46.q_ref, bf16[1024,512]{1,0:T(8,128)(2,1)} %collective-permute-done.2.cot_ref, f32[8,24,128]{2,1,0:T(8,128)} %copy-done.11, ...), custom_call_target="tpu_custom_call" | custom-call | flops 4294967296 | bytes 20971520 | tf_op jit(solution)/shard_map/peer_queries/pallas_call | solution.py:452
  175.4 2.5 %copy.78 = bf16[8,128,512]{2,1,0:T(8,128)(2,1)} copy(bf16[8,128,512]{2,0,1:T(8,128)(2,1)} %bitcast.35) | data formatting | bytes 2097152 | tf_op jit(solution)/shard_map/transpose | solution.py:443
  177.9 3.8 %all-to-all-done.3.stats_ref = f32[128,24,128]{2,1,0:T(8,128)} async-done(((f32[128,24,128]{2,1,0:T(8,128)}), f32[128,24,128]{2,1,0:T(8,128)}, u32[]{:S(2)}, u32[]{:S(2)}) %all-to-all-start.3) | async-done | bytes 1572896 | tf_op jit(solution)/shard_map/all_to_all | solution.py:312
  181.8 12.5 %far_queries.1 = (bf16[1024,1024]{1,0:T(8,128)(2,1)}, f32[2,32,8,512]{3,2,1,0:T(8,128)}, f32[2,32,8,512]{3,2,1,0:T(8,128)}) custom-call(s32[10]{0:T(128)} %pad_add_fusion.1.meta, bf16[1024,1536]{1,0:T(8,128)(2,1)} %get-tuple-element.55.q_ref, bf16[1024,512]{1,0:T(8,128)(2,1)} %bitcast.92, f32[128,24,128]{2,1,0:T(8,128)} %all-to-all-done.3.stats_ref, ...), custom_call_target="tpu_custom_call" | custom-call | flops 2147483648 | bytes 10485760 | tf_op jit(solution)/shard_map/far_queries/pallas_call | solution.py:472
  198.6 8.3 %all-to-all-start.4 = ((bf16[64,16,512]{2,1,0:T(8,128)(2,1)}), bf16[64,16,512]{2,1,0:T(8,128)(2,1)S(1)}, u32[]{:S(2)}, u32[]{:S(2)}) async-start(bf16[64,16,512]{2,1,0:T(8,128)(2,1)} %bitcast.95), calls=%async_computation.4 | async-start | bytes 2097152 | tf_op jit(solution)/shard_map/all_to_all | solution.py:490
  207.0 1.7 convolution_convert_fusion
  210.3 2.2 fusion.4
  212.5 13.6 %all-to-all-done.4 = bf16[64,16,512]{2,1,0:T(8,128)(2,1)S(1)} async-done(((bf16[64,16,512]{2,1,0:T(8,128)(2,1)}), bf16[64,16,512]{2,1,0:T(8,128)(2,1)S(1)}, u32[]{:S(2)}, u32[]{:S(2)}) %all-to-all-start.4) | async-done | bytes 1048608 | tf_op jit(solution)/shard_map/all_to_all | solution.py:490
  (68 shorter events, 21.9 us)
Async XLA Ops:
  0.6 16.7 %copy-start = (bf16[512,512]{1,0:T(8,128)(2,1)S(1)}, bf16[512,512]{1,0:T(8,128)(2,1)}, u32[]{:S(2)}) copy-start(bf16[512,512]{1,0:T(8,128)(2,1)} %param.10) | copy-start | bytes 1572868
  0.6 41.3 %collective-permute-start = (bf16[1024,512]{1,0:T(8,128)(2,1)}, bf16[1024,512]{1,0:T(8,128)(2,1)}, u32[]{:S(2)}, u32[]{:S(2)}) collective-permute-start(bf16[1024,512]{1,0:T(8,128)(2,1)} %x_ref.1), channel_id=1, source_target_pairs={{0,1},{1,0},{2,3},{3,2},{4,5},{5,4},{6,7},{7,6},{8,9},{9,8},{10,11... | collective-permute-start | bytes 3145736 | tf_op jit(solution)/shard_map/ppermute | solution.py:309
  6.9 10.4 %copy-start.7 = (bf16[1024,512]{1,0:T(8,128)(2,1)S(1)}, bf16[1024,512]{1,0:T(8,128)(2,1)}, u32[]{:S(2)}) copy-start(bf16[1024,512]{1,0:T(8,128)(2,1)} %param.14) | copy-start | bytes 3145732
  8.8 34.4 %all-to-all-start = ((bf16[128,8,640]{2,1,0:T(8,128)(2,1)}), bf16[128,8,640]{2,1,0:T(8,128)(2,1)}, u32[]{:S(2)}, u32[]{:S(2)}) async-start(bf16[128,8,640]{2,1,0:T(8,128)(2,1)} %copy.63), calls=%async_computation | async-start | bytes 2621440 | tf_op jit(solution)/shard_map/all_to_all | solution.py:312
  18.1 1.0 copy-start.1
  32.0 6.7 %copy-start.8 = (bf16[1024,512]{1,0:T(8,128)(2,1)S(1)}, bf16[1024,512]{1,0:T(8,128)(2,1)}, u32[]{:S(2)}) copy-start(bf16[1024,512]{1,0:T(8,128)(2,1)} %param.14) | copy-start | bytes 3145732
  38.7 4.6 %copy-start.13 = (f32[128]{0:T(128)S(1)}, f32[128]{0:T(128)}, u32[]{:S(2)}) copy-start(f32[128]{0:T(128)} %constant.107) | copy-start | bytes 1540
  44.5 2.6 %copy-start.4 = (bf16[8,128,512]{2,0,1:T(8,128)(2,1)S(1)}, bf16[8,128,512]{2,0,1:T(8,128)(2,1)}, u32[]{:S(2)}) copy-start(bf16[8,128,512]{2,0,1:T(8,128)(2,1)} %copy.86) | copy-start | bytes 3145732
  48.7 10.1 %copy-start.12 = (s32[16,4]{0,1:T(4,128)S(1)}, s32[16,4]{0,1:T(4,128)}, u32[]{:S(2)}) copy-start(s32[16,4]{0,1:T(4,128)} %param.11) | copy-start | bytes 772
  48.7 39.2 %all-to-all-start.1 = ((bf16[128,8,1024]{2,1,0:T(8,128)(2,1)}), bf16[128,8,1024]{2,1,0:T(8,128)(2,1)}, u32[]{:S(2)}, u32[]{:S(2)}) async-start(bf16[128,8,1024]{2,1,0:T(8,128)(2,1)} %pad_maximum_fusion), calls=%async_computation.1 | async-start | bytes 4194304 | tf_op jit(solution)/shard_map/all_to_all | solution.py:312
  87.9 3.7 %copy-start.2 = (bf16[1024,512]{1,0:T(8,128)(2,1)S(1)}, bf16[1024,512]{1,0:T(8,128)(2,1)}, u32[]{:S(2)}) copy-start(bf16[1024,512]{1,0:T(8,128)(2,1)} %copy-done.1) | copy-start | bytes 3145732
  91.6 55.1 %collective-permute-start.2 = (bf16[1024,512]{1,0:T(8,128)(2,1)S(1)}, bf16[1024,512]{1,0:T(8,128)(2,1)}, u32[]{:S(2)}, u32[]{:S(2)}) collective-permute-start(bf16[1024,512]{1,0:T(8,128)(2,1)S(1)} %copy-done.2), channel_id=1, source_target_pairs={{0,1},{1,0},{2,3},{3,2},{4,5},{5,4},{6,7},{7,6},{8,9},{9,8},{10,11... | collective-permute-start | bytes 3145736 | tf_op jit(solution)/shard_map/ppermute | solution.py:309
  96.2 50.4 %all-to-all-start.2 = ((bf16[128,8,512]{2,1,0:T(8,128)(2,1)}), bf16[128,8,512]{2,1,0:T(8,128)(2,1)}, u32[]{:S(2)}, u32[]{:S(2)}) async-start(bf16[128,8,512]{2,1,0:T(8,128)(2,1)} %fusion.15), calls=%async_computation.2 | async-start | bytes 2097152 | tf_op jit(solution)/shard_map/all_to_all | solution.py:312
  117.7 28.9 %collective-permute-start.1 = (f32[8,24,128]{2,1,0:T(8,128)}, f32[8,24,128]{2,1,0:T(8,128)S(1)}, u32[]{:S(2)}, u32[]{:S(2)}) collective-permute-start(f32[8,24,128]{2,1,0:T(8,128)} %get-tuple-element.60.stats_ref), channel_id=1, source_target_pairs={{0,1},{1,0},{2,3},{3,2},{4,5},{5,4},{6,7},{7,6},{8,9},{9,8},{10,11... | collective-permute-start | bytes 294920 | tf_op jit(solution)/shard_map/ppermute | solution.py:309
  146.6 11.5 %copy-start.11 = (f32[8,24,128]{2,1,0:T(8,128)}, f32[8,24,128]{2,1,0:T(8,128)S(1)}, u32[]{:S(2)}) copy-start(f32[8,24,128]{2,1,0:T(8,128)S(1)} %collective-permute-done.1.stats_ref) | copy-start | bytes 294916
  146.6 35.1 %all-to-all-start.3 = ((f32[128,24,128]{2,1,0:T(8,128)}), f32[128,24,128]{2,1,0:T(8,128)}, u32[]{:S(2)}, u32[]{:S(2)}) async-start(f32[128,24,128]{2,1,0:T(8,128)} %get-tuple-element.69), calls=%async_computation.3 | async-start | bytes 3145728 | tf_op jit(solution)/shard_map/all_to_all | solution.py:312
  158.0 37.8 %collective-permute-start.3 = (f32[2,32,8,512]{3,2,1,0:T(8,128)}, f32[2,32,8,512]{3,2,1,0:T(8,128)S(1)}, u32[]{:S(2)}, u32[]{:S(2)}) collective-permute-start(f32[2,32,8,512]{3,2,1,0:T(8,128)} %get-tuple-element.75), channel_id=1, source_target_pairs={{0,2},{2,0},{4,6},{6,4},{8,10},{10,8},{12,14},{14,12},{16,18},{18,... | collective-permute-start | bytes 3145736 | tf_op jit(solution)/shard_map/ppermute | solution.py:448
  194.3 1.5 copy-start.9
  194.3 3.0 %collective-permute-start.4 = (f32[2,32,8,512]{3,2,1,0:T(8,128)}, f32[2,32,8,512]{3,2,1,0:T(8,128)S(1)}, u32[]{:S(2)}, u32[]{:S(2)}) collective-permute-start(f32[2,32,8,512]{3,2,1,0:T(8,128)} %get-tuple-element.77), channel_id=1, source_target_pairs={{0,2},{2,0},{4,6},{6,4},{8,10},{10,8},{12,14},{14,12},{16,18},{18,... | collective-permute-start | bytes 3145736 | tf_op jit(solution)/shard_map/ppermute | solution.py:448
  195.7 1.5 copy-start.10
  197.5 9.5 %copy-start.3 = (bf16[8,512,128]{2,1,0:T(8,128)(2,1)S(1)}, bf16[8,512,128]{2,1,0:T(8,128)(2,1)}, u32[]{:S(2)}) copy-start(bf16[8,512,128]{2,1,0:T(8,128)(2,1)} %get-tuple-element.59.att_ref) | copy-start | bytes 3145732
  198.6 27.5 %all-to-all-start.4 = ((bf16[64,16,512]{2,1,0:T(8,128)(2,1)}), bf16[64,16,512]{2,1,0:T(8,128)(2,1)S(1)}, u32[]{:S(2)}, u32[]{:S(2)}) async-start(bf16[64,16,512]{2,1,0:T(8,128)(2,1)} %bitcast.95), calls=%async_computation.4 | async-start | bytes 2097152 | tf_op jit(solution)/shard_map/all_to_all | solution.py:490
  206.9 1.7 copy-start.5
  207.0 1.7 copy-start.6
  208.7 1.6 copy-start.14

commit v7 on v6

--- a/solution.py
+++ b/solution.py
@@ -24,6 +24,10 @@
     return lax.dot_general(a, b, (((1,), (1,)), ((), ())), preferred_element_type=F32)
 
 
+def tn(a, b):
+    return lax.dot_general(a, b, (((0,), (0,)), ((), ())), preferred_element_type=F32)
+
+
 def two_heads(pair):
     lane = lax.broadcasted_iota(jnp.int32, pair.shape, 1)
     zero = jnp.zeros_like(pair)
@@ -46,7 +50,7 @@
     return row[:, : row.shape[1] // 2], row[:, row.shape[1] // 2 :]
 
 
-def near_kernel(near_ids, meta, q_ref, tile_ref, k_ref, vt_ref, out_ref, sums_ref, bias_scr):
+def near_kernel(near_ids, meta, q_ref, tile_ref, k_ref, v_ref, out_ref, sums_ref, bias_scr):
     i = pl.program_id(0)
     for j in range(NBR):
         bias_scr[j] = bias_of(tile_ref[0, j])
@@ -56,8 +60,7 @@
     def scores_of(c):
         cols = slice(c * LANES, (c + 1) * LANES)
         qz = two_heads(q_ref[:, cols])
-        keys = jnp.concatenate([k_ref[ids[j], :, cols] for j in range(NBR)], axis=0)
-        return nt(keys, qz) + bias_scr[...].reshape(keys.shape[0], qz.shape[0])
+        return jnp.concatenate([nt(k_ref[ids[j], :, cols], qz) + bias_scr[j] for j in range(NBR)], axis=0)
 
     ready = scores_of(0)
     for c in range(pairs):
@@ -66,49 +69,49 @@
         peak = jnp.max(scores, axis=0, keepdims=True)
         terms = jnp.exp(scores - peak)
         total = jnp.sum(terms, axis=0, keepdims=True)
-        vt = jnp.concatenate([vt_ref[ids[j], cols, :] for j in range(NBR)], axis=1)
-        out_ref[0, cols, :] = own_heads(nn(vt, terms.astype(BF16)))
+        values = jnp.concatenate([v_ref[ids[j], :, cols] for j in range(NBR)], axis=0)
+        out_ref[0, cols, :] = own_heads(tn(values, terms.astype(BF16)))
         store_rows(sums_ref, c, (peak, total))
 
 
-def store_rows(ref, c, rows):
+def store_rows(ref, c, rows, b=0):
     for s, row in enumerate(rows):
         for e, part in enumerate(split_stat(row)):
             at = s * H + 2 * c + e
-            ref[0, at : at + 1, :] = part
-
-
-def merge_kernel(meta, q_ref, cot_t_ref, fk_ref, fvt_ref, out_ref, sums_ref, att_ref, stats_ref, slot_ref):
+            ref[b, at : at + 1, :] = part
+
+
+def merge_kernel(q_ref, cot_t_ref, fk_ref, fv_ref, out_ref, sums_ref, att_ref, stats_ref):
     mid = LANES // 2
-    pairs = q_ref.shape[1] // LANES
-    cols = [slice(c * LANES, (c + 1) * LANES) for c in range(pairs)]
-    scores = [nt(fk_ref[0, :, cols[c]], two_heads(q_ref[:, cols[c]])) for c in range(pairs)]
+    bs = fk_ref.shape[1]
+    units = [(b, c) for b in range(fk_ref.shape[0]) for c in range(q_ref.shape[1] // LANES)]
+    cols = [slice(c * LANES, (c + 1) * LANES) for _, c in units]
+    scores = [
+        nt(fk_ref[b, :, cols[u]], two_heads(q_ref[b * bs : (b + 1) * bs, cols[u]])) for u, (b, c) in enumerate(units)
+    ]
     peaks, kepts, invs, lows = [], [], [], []
-    for c in range(pairs):
-        near_peak, near_total = load_rows(sums_ref, c, 2)
-        peak = jnp.maximum(near_peak, jnp.max(scores[c], axis=0, keepdims=True))
-        terms = jnp.exp(scores[c] - peak)
+    for u, (b, c) in enumerate(units):
+        near_peak, near_total = load_rows(sums_ref, c, 2, b)
+        peak = jnp.maximum(near_peak, jnp.max(scores[u], axis=0, keepdims=True))
+        terms = jnp.exp(scores[u] - peak)
         kept = jnp.exp(near_peak - peak)
         inv = 1.0 / (near_total * kept + jnp.sum(terms, axis=0, keepdims=True))
         lows.append((terms * inv).astype(BF16))
         peaks.append(peak)
         kepts.append(kept)
         invs.append(inv)
-    far_outs = [own_heads(nn(fvt_ref[0, cols[c], :], lows[c])) for c in range(pairs)]
-    atts = []
-    for c in range(pairs):
-        first, second = split_stat(kepts[c] * invs[c])
-        near_out = out_ref[0, cols[c], :]
+    far_outs = [own_heads(tn(fv_ref[b, :, cols[u]], lows[u])) for u, (b, c) in enumerate(units)]
+    for u, (b, c) in enumerate(units):
+        first, second = split_stat(kepts[u] * invs[u])
+        near_out = out_ref[b, cols[u], :]
         near_out = jnp.concatenate([near_out[:mid] * first, near_out[mid:] * second], axis=0)
-        atts.append((far_outs[c] + near_out).astype(BF16).astype(F32))
-    for c in range(pairs):
-        att_ref[0, cols[c], :] = atts[c].astype(BF16)
-        prod = cot_t_ref[0, cols[c], :].astype(F32) * atts[c]
+        att = (far_outs[u] + near_out).astype(BF16)
+        att_ref[b, cols[u], :] = att
+        prod = cot_t_ref[b, cols[u], :].astype(F32) * att.astype(F32)
         delta = jnp.concatenate(
             [jnp.sum(prod[:mid], axis=0, keepdims=True), jnp.sum(prod[mid:], axis=0, keepdims=True)], axis=1
         )
-        store_rows(stats_ref, c, (peaks[c], invs[c], delta))
-        store_rows(slot_ref, c, (peaks[c], invs[c], delta))
+        store_rows(stats_ref, c, (peaks[u], invs[u], delta), b)
 
 
 def deal(dw_scr, kept_ref, given_ref, core):
@@ -120,8 +123,8 @@
             given_ref[g, :, :, t * span : (t + 1) * span] = dw_scr[:, 1 - core, :, at : at + span]
 
 
-def own_kernel(near_ids, meta, q_ref, cot_ref, tile_ref, stats_ref, k_ref, v_ref, kt_ref, fk_ref, fv_ref, fkt_ref,
-               xt_ref, ct_ref, att_ref, dq_ref, acc_ref, kept_ref, given_ref, p_scr, ds_scr, qz_scr, cz_scr, bias_scr,
+def own_kernel(near_ids, meta, q_ref, cot_ref, tile_ref, stats_ref, k_ref, v_ref, fk_ref, fv_ref,
+               xt_ref, ct_ref, att_ref, dq_ref, acc_ref, kept_ref, given_ref, slot_ref, p_scr, ds_scr, qz_scr, cz_scr, bias_scr,
                dw_scr):
     i = pl.program_id(0)
     bs, width = q_ref.shape
@@ -133,6 +136,7 @@
         acc_ref[...] = jnp.zeros_like(acc_ref)
         dw_scr[...] = jnp.zeros_like(dw_scr)
 
+    slot_ref[...] = stats_ref[...]
     for j in range(NBR):
         bias_scr[j] = bias_of(tile_ref[0, j])
     ids = [near_ids[i, j] for j in range(NBR)]
@@ -143,21 +147,22 @@
         qz_scr[c] = qz
         cz_scr[c] = cz
         peak, inv, delta = load_rows(stats_ref, c, 3)
-        keys = jnp.concatenate([k_ref[ids[j], :, cols] for j in range(NBR)] + [fk_ref[0, :, cols]], axis=0)
-        values = jnp.concatenate([v_ref[ids[j], :, cols] for j in range(NBR)] + [fv_ref[0, :, cols]], axis=0)
-        all_scores = nt(keys, qz)
-        all_grads = nt(values, cz)
         parts = []
         for j in range(NBR + 1):
             rows = slice(j * bs, (j + 1) * bs)
-            scores = all_scores[rows] + bias_scr[j] if j < NBR else all_scores[rows]
+            if j < NBR:
+                scores = nt(k_ref[ids[j], :, cols], qz) + bias_scr[j]
+                grad_probs = nt(v_ref[ids[j], :, cols], cz)
+            else:
+                scores = nt(fk_ref[0, :, cols], qz)
+                grad_probs = nt(fv_ref[0, :, cols], cz)
             probs = jnp.exp(scores - peak) * inv
-            parts.append((probs * (all_grads[rows] - delta)).astype(BF16))
+            parts.append((probs * (grad_probs - delta)).astype(BF16))
             if j < NBR:
                 p_scr[c, rows, :] = probs.astype(BF16)
                 ds_scr[c, rows, :] = parts[j]
-        kt = jnp.concatenate([kt_ref[ids[j], cols, :] for j in range(NBR)] + [fkt_ref[0, cols, :]], axis=1)
-        dq_ref[0, cols, :] = (own_heads(nn(kt, jnp.concatenate(parts, axis=0))) * 0.125).astype(BF16)
+        keys = jnp.concatenate([k_ref[ids[j], :, cols] for j in range(NBR)] + [fk_ref[0, :, cols]], axis=0)
+        dq_ref[0, cols, :] = (own_heads(tn(keys, jnp.concatenate(parts, axis=0))) * 0.125).astype(BF16)
     half = dw_scr.shape[:3] + (width,)
     dw_scr[:, :, :, :width] += nt(ct_ref[0], att_ref[0]).reshape(half)
     dw_scr[:, :, :, width:] += nt(xt_ref[0], dq_ref[0]).reshape(half)
@@ -179,10 +184,10 @@
         deal(dw_scr, kept_ref, given_ref, meta[1 + own])
 
 
-def load_rows(ref, c, count):
+def load_rows(ref, c, count, b=0):
     return [
         jnp.concatenate(
-            [ref[0, s * H + 2 * c : s * H + 2 * c + 1, :], ref[0, s * H + 2 * c + 1 : s * H + 2 * c + 2, :]], axis=1
+            [ref[b, s * H + 2 * c : s * H + 2 * c + 1, :], ref[b, s * H + 2 * c + 1 : s * H + 2 * c + 2, :]], axis=1
         )
         for s in range(count)
     ]
@@ -229,43 +234,38 @@
                 acc_ref[n, :, width + c * LANES : width + (c + 1) * LANES] += dvs[c]
 
 
-def far_kernel(meta, q_ref, cot_ref, stats_ref, k_ref, v_ref, acc_ref, xt_ref, dkv_ref, kept_ref, given_ref, dw_scr):
-    width = q_ref.shape[1]
+def far_kernel(meta, q_ref, cot_ref, first_ref, second_ref, k_ref, v_ref, acc_ref, xt_ref, dkv_ref, kept_ref,
+               given_ref, dw_scr):
+    bs, width = k_ref.shape[1:]
     i = pl.program_id(0)
-    own = pl.num_programs(0)
 
     @pl.when(i == 0)
     def _():
         dw_scr[...] = jnp.zeros_like(dw_scr)
 
-    every = range(width // LANES)
-    cols = [slice(c * LANES, (c + 1) * LANES) for c in every]
+    units = [(b, c) for b in range(2) for c in range(width // LANES)]
+    cols = [slice(c * LANES, (c + 1) * LANES) for _, c in units]
+    rows = [slice(b * bs, (b + 1) * bs) for b, _ in units]
+    every = range(len(units))
     dks, dvs = key_terms(
-        [k_ref[0, :, cols[c]] for c in every], [v_ref[0, :, cols[c]] for c in every],
-        [two_heads(q_ref[:, cols[c]]) for c in every], [two_heads(cot_ref[:, cols[c]]) for c in every], None,
-        [load_rows(stats_ref, c, 3) for c in every],
+        [k_ref[units[u][0], :, cols[u]] for u in every], [v_ref[units[u][0], :, cols[u]] for u in every],
+        [two_heads(q_ref[rows[u], cols[u]]) for u in every], [two_heads(cot_ref[rows[u], cols[u]]) for u in every],
+        None, [load_rows((first_ref, second_ref)[b], c, 3) for b, c in units],
     )
-    for c in every:
+    for u, (b, c) in enumerate(units):
         vcols = slice(width + c * LANES, width + (c + 1) * LANES)
-        dkv_ref[:, cols[c]] = (acc_ref[0, :, cols[c]] + dks[c].astype(BF16).astype(F32)).astype(BF16)
-        dkv_ref[:, vcols] = (acc_ref[0, :, vcols] + dvs[c].astype(BF16).astype(F32)).astype(BF16)
-    dw_scr[...] += nn(xt_ref[0], dkv_ref[...]).reshape(dw_scr.shape)
-
-    @pl.when(i == own - 1)
+        dkv_ref[rows[u], cols[u]] = (acc_ref[b, :, cols[u]] + dks[u].astype(BF16).astype(F32)).astype(BF16)
+        dkv_ref[rows[u], vcols] = (acc_ref[b, :, vcols] + dvs[u].astype(BF16).astype(F32)).astype(BF16)
+    xt = jnp.concatenate([xt_ref[0], xt_ref[1]], axis=1)
+    dw_scr[...] += nn(xt, dkv_ref[...]).reshape(dw_scr.shape)
+
+    @pl.when(i == pl.num_programs(0) - 1)
     def _():
-        deal(dw_scr, kept_ref, given_ref, meta[1 + own])
-
-
-def project_kernel(x_ref, w_ref, wt_ref, *rest):
-    qkv_ref, t_ref = rest[-2:]
-    bs = t_ref.shape[2]
-    qkv_ref[...] = nn(x_ref[...], w_ref[...]).astype(BF16)
-
-    @pl.when(pl.program_id(0) < 2)
-    def _():
-        turned = nt(wt_ref[...], x_ref[...]).astype(BF16)
-        for b in range(t_ref.shape[0]):
-            t_ref[b] = turned[:, b * bs : (b + 1) * bs]
+        deal(dw_scr, kept_ref, given_ref, meta[1 + 2 * pl.num_programs(0)])
+
+
+def project_kernel(x_ref, w_ref, *rest):
+    rest[-1][...] = nn(x_ref[...], w_ref[...]).astype(BF16)
 
 
 def call(kernel, scalars, steps, in_specs, out_specs, out_shape, scratch, flops, touched, name, aliases={}):
@@ -329,7 +329,6 @@
     cot_rows = spread(cot)
     cot_t = jnp.einsum("ck,brk->bcr", w_out, layer_cot.reshape(own, bs, width), preferred_element_type=F32).astype(BF16)
 
-    w_turned = w_all[:, width:].T
     hold = pl.BlockSpec(memory_space=pl.ANY)
 
     def project(feats, total, at, carried, name):
@@ -337,20 +336,15 @@
             project_kernel, 0, 3,
             [
                 once((rows, width)),
-                pl.BlockSpec((width, width), lambda i: (0, (i + 1) % 3)),
-                pl.BlockSpec((width, width), lambda i: (jnp.minimum(i, 1), 0)),
+                pl.BlockSpec((width, width), lambda i: (0, i)),
             ]
             + [hold] * len(carried),
             [
-                pl.BlockSpec((rows, width), lambda i: (at, (i + 1) % 3)),
-                pl.BlockSpec((own, width, bs), lambda i: (at, jnp.minimum(i, 1), 0)),
+                pl.BlockSpec((rows, width), lambda i: (at, i)),
             ],
-            [
-                jax.ShapeDtypeStruct((total * bs, 3 * width), BF16),
-                jax.ShapeDtypeStruct((total, 2 * width, bs), BF16),
-            ],
-            [], 2 * rows * width * 5 * width, 8 << 20, name, aliases={3: 0, 4: 1} if carried else {},
-        )(feats, w_all, w_turned, *carried)
+            [jax.ShapeDtypeStruct((total * bs, 3 * width), BF16)],
+            [], 2 * rows * width * 3 * width, 6 << 20, name, aliases={2: 0} if carried else {},
+        )(feats, w_all, *carried)[0]
 
     own_part = project(node_feats, blocks, 0, (), "project_own")
     feats_t = node_feats.reshape(own, bs, width).transpose(0, 2, 1)
@@ -364,7 +358,7 @@
     one_hot = (ids == jnp.arange(ids.shape[0], dtype=jnp.int32)[None, :].astype(F32)).astype(BF16)
     second = jnp.concatenate([gathered(rows_in[:, :, :width]), cot_rows], axis=2)
     second = exchange(second)
-    part_qkv, part_t = project(peer_feats, blocks, 1, own_part, "project_peer")
+    part_qkv = project(peer_feats, blocks, 1, (own_part,), "project_peer")
     part_blk = part_qkv.reshape(blocks, bs, 3 * width)
     pair_flops = 2 * bs * bs * width * 2
     step = lambda i, *s: (i, 0)
@@ -373,59 +367,57 @@
     tile_spec = pl.BlockSpec((1, NBR, bs, bs), lambda i, ids, meta: (meta[0] + i, 0, 0, 0))
     k_spec = pl.BlockSpec((blocks, bs, width), lambda i, *s: (0, 0, 1), pipeline_mode=pl.Buffered(1))
     v_spec = pl.BlockSpec((blocks, bs, width), lambda i, *s: (0, 0, 2), pipeline_mode=pl.Buffered(1))
-    kt_spec = pl.BlockSpec((blocks, width, bs), lambda i, *s: (0, 0, 0), pipeline_mode=pl.Buffered(1))
-    vt_spec = pl.BlockSpec((blocks, width, bs), lambda i, *s: (0, 1, 0), pipeline_mode=pl.Buffered(1))
     stats_spec = pl.BlockSpec((1, STATS, bs), row_step)
     turned_spec = pl.BlockSpec((1, width, bs), row_step)
     near_out, sums = call(
         near_kernel, 2, own,
-        [rows_spec, tile_spec, k_spec, vt_spec],
+        [rows_spec, tile_spec, k_spec, v_spec],
         [pl.BlockSpec((1, width, bs), row_step), pl.BlockSpec((1, 2 * H, bs), row_step)],
         [jax.ShapeDtypeStruct((own, width, bs), F32), jax.ShapeDtypeStruct((own, 2 * H, bs), F32)],
         [pltpu.VMEM((NBR, bs, 2 * bs), F32)],
         own * 16 * pair_flops, 10 << 20, "near_forward",
-    )(near_ids, meta, part_qkv, tiles, part_blk, part_t)
+    )(near_ids, meta, part_qkv, tiles, part_blk, part_blk)
     second, near_out, sums, cot_out = lax.optimization_barrier((second, near_out, sums, cot))
 
     picked = gathered(second[:, :, width:])
     far_feats = second[:, :, :width].transpose(1, 0, 2).reshape(rows, width)
     picked, far_feats = lax.optimization_barrier((picked, far_feats))
     far_cot = exchange(picked)
-    far_qkv, far_t = project(far_feats, own, 0, (), "project_far")
+    far_qkv = jnp.dot(far_feats, w_all, preferred_element_type=F32).astype(BF16)
     far_blk = far_qkv.reshape(own, bs, 3 * width)
     peer_cot = swap(cot_out)
 
     far_k_spec = pl.BlockSpec((1, bs, width), lambda i, *s: (i, 0, 1))
     far_v_spec = pl.BlockSpec((1, bs, width), lambda i, *s: (i, 0, 2))
-    far_kt_spec = pl.BlockSpec((1, width, bs), row_step)
-    far_vt_spec = pl.BlockSpec((1, width, bs), lambda i, *s: (i, 1, 0))
-    att, stats, slots = call(
-        merge_kernel, 1, own,
-        [rows_spec, turned_spec, far_k_spec, far_vt_spec, turned_spec, pl.BlockSpec((1, 2 * H, bs), row_step)],
-        [turned_spec, stats_spec, pl.BlockSpec((1, STATS, bs), lambda i, meta: (meta[1 + i], 0, 0))],
-        [
-            jax.ShapeDtypeStruct((own, width, bs), BF16),
-            jax.ShapeDtypeStruct((own, STATS, bs), F32),
-            jax.ShapeDtypeStruct((devices, STATS, bs), F32),
-        ],
+    pair_rows = pl.BlockSpec((2 * bs, width), step)
+    pair_turned = pl.BlockSpec((2, width, bs), row_step)
+    pair_k = pl.BlockSpec((2, bs, width), lambda i, *s: (i, 0, 1))
+    pair_v = pl.BlockSpec((2, bs, width), lambda i, *s: (i, 0, 2))
+    att, stats = call(
+        merge_kernel, 0, own // 2,
+        [pair_rows, pair_turned, pair_k, pair_v, pair_turned, pl.BlockSpec((2, 2 * H, bs), row_step)],
+        [pair_turned, pl.BlockSpec((2, STATS, bs), row_step)],
+        [jax.ShapeDtypeStruct((own, width, bs), BF16), jax.ShapeDtypeStruct((own, STATS, bs), F32)],
         [], own * 4 * pair_flops, 6 << 20, "far_forward",
-    )(meta, part_qkv, cot_t, far_blk, far_t, near_out, sums)
+    )(part_qkv, cot_t, far_blk, far_blk, near_out, sums)
     peer_stats = swap(stats)
     pairs = width // LANES
     piece = (groups, doms // 2, width // doms, width)
     piece_spec = pl.BlockSpec(piece, lambda i, *s: (0, 0, 0, 0), pipeline_mode=pl.Buffered(1))
     piece_out = jax.ShapeDtypeStruct(piece, F32)
     dw_scratch = pltpu.VMEM((doms // 2, 2, width // doms, 2 * width), F32)
-    dq, acc, kept, given = call(
+    dq, acc, kept, given, slots = call(
         own_kernel, 2, own,
-        [rows_spec, rows_spec, tile_spec, stats_spec, k_spec, v_spec, kt_spec, far_k_spec, far_v_spec, far_kt_spec,
+        [rows_spec, rows_spec, tile_spec, stats_spec, k_spec, v_spec, far_k_spec, far_v_spec,
          turned_spec, turned_spec, turned_spec],
-        [turned_spec, pl.BlockSpec((own, bs, 2 * width), lambda i, *s: (0, 0, 0)), piece_spec, piece_spec],
+        [turned_spec, pl.BlockSpec((own, bs, 2 * width), lambda i, *s: (0, 0, 0)), piece_spec, piece_spec,
+         pl.BlockSpec((1, STATS, bs), lambda i, ids, meta: (meta[1 + i], 0, 0))],
         [
             jax.ShapeDtypeStruct((own, width, bs), BF16),
             jax.ShapeDtypeStruct((own, bs, 2 * width), F32),
             piece_out,
             piece_out,
+            jax.ShapeDtypeStruct((devices, STATS, bs), F32),
         ],
         [
             pltpu.VMEM((pairs, NBR * bs, 2 * bs), BF16),
@@ -436,7 +428,7 @@
             dw_scratch,
         ],
         own * 24 * pair_flops, 30 << 20, "own_backward",
-    )(near_ids, meta, part_qkv, cot, tiles, stats, part_blk, part_blk, part_t, far_blk, far_blk, far_t,
+    )(near_ids, meta, part_qkv, cot, tiles, stats, part_blk, part_blk, far_blk, far_blk,
       feats_t, out_t, att)
     acc, peer_stats, peer_cot, far_cot, slots = lax.optimization_barrier((acc, peer_stats, peer_cot, far_cot, slots))
     far_slots = exchange(slots)
@@ -470,20 +462,21 @@
     )(near_ids, meta, part_qkv, peer_cot, peer_stats, tiles, part_blk, part_blk, acc)
 
     dkv, kept, given = call(
-        far_kernel, 1, own,
+        far_kernel, 1, own // 2,
         [
-            pl.BlockSpec((bs, width), step),
-            pl.BlockSpec((bs, width), step),
-            pl.BlockSpec((1, STATS, bs), lambda i, meta: (meta[1 + i], 0, 0)),
-            pl.BlockSpec((1, bs, width), lambda i, *s: (i, 0, 1)),
-            pl.BlockSpec((1, bs, width), lambda i, *s: (i, 0, 2)),
-            pl.BlockSpec((1, bs, 2 * width), lambda i, *s: (i, 0, 0)),
-            turned_spec,
+            pair_rows,
+            pair_rows,
+            pl.BlockSpec((1, STATS, bs), lambda i, meta: (meta[1 + 2 * i], 0, 0)),
+            pl.BlockSpec((1, STATS, bs), lambda i, meta: (meta[2 + 2 * i], 0, 0)),
+            pair_k,
+            pair_v,
+            pl.BlockSpec((2, bs, 2 * width), row_step),
+            pair_turned,
         ],
-        [pl.BlockSpec((bs, 2 * width), step), piece_spec, piece_spec],
+        [pl.BlockSpec((2 * bs, 2 * width), step), piece_spec, piece_spec],
         [jax.ShapeDtypeStruct((rows, 2 * width), BF16), piece_out, piece_out],
         [dw_scratch], own * 8 * pair_flops, 10 << 20, "far_queries",
-    )(meta, far_qkv, far_cot, far_slots, part_blk, part_blk, acc, feats_t)
+    )(meta, far_qkv, far_cot, far_slots, far_slots, part_blk, part_blk, acc, feats_t)
 
     split = jnp.concatenate([early, paired(kept, given)], axis=2).reshape(devices // 2, 2 * width // doms, width)
     same_core = [[d * groups + g for g in range(groups) for d in range(e, doms, 2)] for e in range(2)]

time: 229 us -> 223 us (0.974)
  Pallas kernels: 98.9 us -> 81 us
  matrix products: 13.4 us -> 19.6 us
  waiting for transfers between devices: 28.6 us -> 31.3 us
    pallas_call x3 -> x2, Pallas kernels: 20.2 us -> 10.6 us  [project(): call(project_kernel, 0, 3, [once((rows, width)), pl.BlockSpec((width, wid...]
    pallas_call x3, Pallas kernels: 35.3 us -> 28.2 us  [the longest x1 12.8 us: body(): call(near_kernel, 2, own, [rows_spec, tile_spec, k_spec, v_spec], [pl.Blo...]
    dot_general x0 -> x1, matrix products: none -> 5.1 us  [body(): far_qkv = jnp.dot(far_feats, w_all, preferred_element_type=F32).astype(BF16)]
    all_to_all x4, waiting for transfers between devices: 12.2 us -> 16.4 us  [exchange(): return lax.all_to_all(x, DEVICES, split_axis=0, concat_axis=0, tiled=True)]
    concatenate x1 -> x0, local copies, waits for them, and re-layouts: 2.6 us -> none  [body(): jnp.concatenate([w_by[0] * jnp.asarray(0.125, BF16), w_by[1], w_by[2]], a...]
  transfers between devices with their start and end apart: 10 -> 10, of which waited for: 6 -> 6; matrix products, arithmetic and copies ran while one was open for 14% -> 17% of each run, Pallas kernels for 43% -> 37%
where the time goes in v7:
time: 223 us; the launch traced here: 221 us
  Pallas kernels  81 us (36%)
  starting transfers between devices  53.6 us (24%)
  waiting for transfers between devices  31.3 us (14%)
  local copies, waits for them, and re-layouts  22.7 us (10%)
  matrix products  19.6 us (9%)
  other arithmetic  11.6 us (5%)
    all_to_all x4, starting transfers between devices, exchange(): return lax.all_to_all(x, DEVICES, split_axis=0, concat_axis=0, tiled=True)  35.7 us
    pallas_call x1, Pallas kernels, body(): call(own_kernel, 2, own, [rows_spec, rows_spec, tile_spec, stats_spec, k_...  26.6 us
    all_to_all x4, waiting for transfers between devices, exchange(): return lax.all_to_all(x, DEVICES, split_axis=0, concat_axis=0, tiled=True)  16.4 us
    pallas_call x1, Pallas kernels, body(): call(peer_kernel, 2, own, [pl.BlockSpec((bs, width), lambda i, *s: (own +...  15.6 us
    all_to_all x1, waiting for transfers between devices, body(): lax.all_to_all(split, DEVICES, split_axis=0, concat_axis=0, axis_index_gr...  13.6 us
    pallas_call x1, Pallas kernels, body(): call(near_kernel, 2, own, [rows_spec, tile_spec, k_spec, v_spec], [pl.Blo...  12.8 us
    pallas_call x2, Pallas kernels, project(): call(project_kernel, 0, 3, [once((rows, width)), pl.BlockSpec((width, wid...  10.6 us
    all_to_all x1, starting transfers between devices, body(): lax.all_to_all(split, DEVICES, split_axis=0, concat_axis=0, axis_index_gr...  9.92 us
  transfers between devices with their start and end apart: 10, of which 6 were waited for; matrix products, arithmetic and copies ran while one was open for 17% of the time, Pallas kernels for 37%

profile of v7, /device:TPU:0, one launch (start us, length us, event | category | flops | bytes accessed | tf_op | source)
XLA Modules:
  0.0 220.7 jit_solution(6145675643972274291)
XLA Ops:
  0.6 4.0 %collective-permute-start = (bf16[1024,512]{1,0:T(8,128)(2,1)}, bf16[1024,512]{1,0:T(8,128)(2,1)}, u32[]{:S(2)}, u32[]{:S(2)}) collective-permute-start(bf16[1024,512]{1,0:T(8,128)(2,1)} %x_ref.1), channel_id=1, source_target_pairs={{0,1},{1,0},{2,3},{3,2},{4,5},{5,4},{6,7},{7,6},{8,9},{9,8},{10,11... | collective-permute-start | bytes 3145736 | tf_op jit(solution)/shard_map/ppermute | solution.py:309
  6.9 1.8 copy.58
  8.8 8.5 %all-to-all-start = ((bf16[128,8,640]{2,1,0:T(8,128)(2,1)}), bf16[128,8,640]{2,1,0:T(8,128)(2,1)}, u32[]{:S(2)}, u32[]{:S(2)}) async-start(bf16[128,8,640]{2,1,0:T(8,128)(2,1)} %copy.58), calls=%async_computation | async-start | bytes 2621440 | tf_op jit(solution)/shard_map/all_to_all | solution.py:312
  17.3 1.7 copy.60
  19.9 2.1 copy.77
  24.1 2.0 convolution_convert_fusion.3.cot_ref
  27.0 1.5 copy.84
  28.5 2.3 %copy.66 = bf16[8,128,512]{1,2,0:T(8,128)(2,1)} copy(bf16[8,128,512]{2,1,0:T(8,128)(2,1)} %bitcast.99) | data formatting | bytes 2097152 | tf_op jit(solution)/shard_map/reshape | solution.py:330
  32.1 2.6 %pad_maximum_fusion.1.w_ref = bf16[512,1536]{1,0:T(8,128)(2,1)} fusion(bf16[512,512]{1,0:T(8,128)(2,1)} %copy.79, bf16[512,512]{1,0:T(8,128)(2,1)} %copy.78, bf16[512,512]{1,0:T(8,128)(2,1)} %copy.77), kind=kLoop, calls=%fused_computation.13 | loop fusion | flops 4718592 | bytes 3145728 | tf_op jit(solution)/shard_map/concatenate | solution.py:306
  34.7 5.4 %project_own.1.rest_0_ = bf16[2048,1536]{1,0:T(8,128)(2,1)} custom-call(bf16[1024,512]{1,0:T(8,128)(2,1)} %x_ref.1, bf16[512,1536]{1,0:T(8,128)(2,1)} %pad_maximum_fusion.1.w_ref), custom_call_target="tpu_custom_call" | custom-call | flops 1610612736 | bytes 6291456 | tf_op jit(solution)/shard_map/project_own/pallas_call | solution.py:335
  40.1 1.7 fusion.21.cot_t_ref
  44.5 2.6 %fusion.18 = bf16[128,8,512]{2,1,0:T(8,128)(2,1)S(1)} fusion(f32[1024]{0:T(1024)S(1)} %iota_convert_fusion, f32[1024]{0:T(1024)S(1)} %multiply_reduce_fusion, bf16[128,8,640]{2,1,0:T(8,128)(2,1)} %all-to-all-done), kind=kOutput, calls=%fused_computation.20 | convolution fusion | flops 1075314688 | bytes 2105344 | tf_op jit(solution)/shard_map/dot_general | solution.py:318
  47.1 1.6 pad_maximum_fusion
  48.7 10.1 %all-to-all-start.1 = ((bf16[128,8,1024]{2,1,0:T(8,128)(2,1)}), bf16[128,8,1024]{2,1,0:T(8,128)(2,1)}, u32[]{:S(2)}, u32[]{:S(2)}) async-start(bf16[128,8,1024]{2,1,0:T(8,128)(2,1)} %pad_maximum_fusion), calls=%async_computation.1 | async-start | bytes 4194304 | tf_op jit(solution)/shard_map/all_to_all | solution.py:312
  60.4 5.3 %project_peer.1.q_ref = bf16[2048,1536]{1,0:T(8,128)(2,1)} custom-call(bf16[1024,512]{1,0:T(8,128)(2,1)} %collective-permute-done.x_ref, bf16[512,1536]{1,0:T(8,128)(2,1)} %pad_maximum_fusion.1.w_ref, bf16[2048,1536]{1,0:T(8,128)(2,1)} %project_own.1.rest_0_), custom_call_target="tpu_custom_call", output_to_operand_aliasing={{}: (2, {})} | custom-call | flops 1610612736 | bytes 6291456 | tf_op jit(solution)/shard_map/project_peer/pallas_call | solution.py:335
  65.6 12.8 %near_forward.1 = (f32[8,512,128]{2,1,0:T(8,128)}, f32[8,16,128]{2,1,0:T(8,128)}) custom-call(s32[16,4]{1,0:T(8,128)} %copy.80.near_ids, s32[10]{0:T(128)} %pad_add_fusion.1.meta, bf16[2048,1536]{1,0:T(8,128)(2,1)} %project_peer.1.q_ref, s32[16,4,128,128]{3,2,1,0:T(8,128)} %tile_ref.5, bf16[16,128,1536]{2,1,0:T(8,128)(2,1)} %bitcast.71, ...), custom_call_target="tpu_custom_call" | custom-call | flops 4294967296 | bytes 10485760 | tf_op jit(solution)/shard_map/near_forward/pallas_call | solution.py:372
  78.4 9.5 %all-to-all-done.1 = bf16[128,8,1024]{2,1,0:T(8,128)(2,1)} async-done(((bf16[128,8,1024]{2,1,0:T(8,128)(2,1)}), bf16[128,8,1024]{2,1,0:T(8,128)(2,1)}, u32[]{:S(2)}, u32[]{:S(2)}) %all-to-all-start.1) | async-done | bytes 2097184 | tf_op jit(solution)/shard_map/all_to_all | solution.py:312
  89.3 3.5 %fusion.15 = bf16[128,8,512]{2,1,0:T(8,128)(2,1)} fusion(f32[1024]{0:T(1024)S(1)} %iota_convert_fusion, f32[1024]{0:T(1024)S(1)} %multiply_reduce_fusion, bf16[128,8,1024]{2,1,0:T(8,128)(2,1)} %all-to-all-done.1), kind=kOutput, calls=%fused_computation.19 | convolution fusion | flops 1075314688 | bytes 2105344 | tf_op jit(solution)/shard_map/dot_general | solution.py:318
  94.1 5.8 %all-to-all-start.2 = ((bf16[128,8,512]{2,1,0:T(8,128)(2,1)}), bf16[128,8,512]{2,1,0:T(8,128)(2,1)}, u32[]{:S(2)}, u32[]{:S(2)}) async-start(bf16[128,8,512]{2,1,0:T(8,128)(2,1)} %fusion.15), calls=%async_computation.2 | async-start | bytes 2097152 | tf_op jit(solution)/shard_map/all_to_all | solution.py:312
  99.9 3.0 %collective-permute-start.2 = (bf16[1024,512]{1,0:T(8,128)(2,1)S(1)}, bf16[1024,512]{1,0:T(8,128)(2,1)}, u32[]{:S(2)}, u32[]{:S(2)}) collective-permute-start(bf16[1024,512]{1,0:T(8,128)(2,1)S(1)} %copy-done.3), channel_id=1, source_target_pairs={{0,1},{1,0},{2,3},{3,2},{4,5},{5,4},{6,7},{7,6},{8,9},{9,8},{10,11... | collective-permute-start | bytes 3145736 | tf_op jit(solution)/shard_map/ppermute | solution.py:309
  102.9 5.1 %convolution_convert_fusion.q_ref = bf16[1024,1536]{1,0:T(8,128)(2,1)} fusion(bf16[1024,512]{1,0:T(8,128)(2,1)} %bitcast.102, bf16[512,512]{1,0:T(8,128)(2,1)} %copy.79, bf16[512,512]{1,0:T(8,128)(2,1)} %copy.78, bf16[512,512]{1,0:T(8,128)(2,1)} %copy.77), kind=kOutput, calls=%fused_computation.4 | convolution fusion | flops 1616904192 | bytes 5767168 | tf_op jit(solution)/shard_map/dot_general | solution.py:386
  108.0 5.9 %far_forward.1 = (bf16[8,512,128]{2,1,0:T(8,128)(2,1)}, f32[8,24,128]{2,1,0:T(8,128)}) custom-call(bf16[2048,1536]{1,0:T(8,128)(2,1)} %project_peer.1.q_ref, bf16[8,512,128]{2,1,0:T(8,128)(2,1)} %fusion.21.cot_t_ref, bf16[8,128,1536]{2,1,0:T(8,128)(2,1)} %bitcast.79, bf16[8,128,1536]{2,1,0:T(8,128)(2,1)} %bitcast.80, ...), custom_call_target="tpu_custom_call" | custom-call | flops 1073741824 | bytes 6291456 | tf_op jit(solution)/shard_map/far_forward/pallas_call | solution.py:396
  114.6 26.6 %own_backward.1 = (bf16[8,512,128]{2,1,0:T(8,128)(2,1)}, f32[8,128,1024]{2,1,0:T(8,128)}, f32[2,32,8,512]{3,2,1,0:T(8,128)}, f32[2,32,8,512]{3,2,1,0:T(8,128)}, f32[128,24,128]{2,1,0:T(8,128)}) custom-call(s32[16,4]{1,0:T(8,128)} %copy.80.near_ids, s32[10]{0:T(128)} %pad_add_fusion.1.meta, bf16[2048,1536]{1,0:T(8,128)(2,1)} %project_peer.1.q_ref, ...), custom_call_target="tpu_custom_call" | custom-call | flops 6442450944 | bytes 31457280 | tf_op jit(solution)/shard_map/own_backward/pallas_call | solution.py:409
  141.3 11.3 %all-to-all-start.3 = ((f32[128,24,128]{2,1,0:T(8,128)}), f32[128,24,128]{2,1,0:T(8,128)}, u32[]{:S(2)}, u32[]{:S(2)}) async-start(f32[128,24,128]{2,1,0:T(8,128)} %get-tuple-element.55), calls=%async_computation.3 | async-start | bytes 3145728 | tf_op jit(solution)/shard_map/all_to_all | solution.py:312
  152.7 15.6 %peer_queries.1.acc_ref = f32[8,128,1024]{2,1,0:T(8,128)} custom-call(s32[16,4]{1,0:T(8,128)} %copy.80.near_ids, s32[10]{0:T(128)} %pad_add_fusion.1.meta, bf16[2048,1536]{1,0:T(8,128)(2,1)} %project_peer.1.q_ref, bf16[1024,512]{1,0:T(8,128)(2,1)} %collective-permute-done.2.cot_ref, f32[8,24,128]{2,1,0:T(8,128)} %copy-done.11, s32[16,4,128,128]{3,2,1,0:T(8,128)} %tile_ref.5, ...), custom_call_target="tpu_custom_call" | custom-call | flops 4294967296 | bytes 20971520 | tf_op jit(solution)/shard_map/peer_queries/pallas_call | solution.py:444
  168.3 2.5 %copy.73 = bf16[8,128,512]{2,1,0:T(8,128)(2,1)} copy(bf16[8,128,512]{2,0,1:T(8,128)(2,1)} %bitcast.34) | data formatting | bytes 2097152 | tf_op jit(solution)/shard_map/transpose | solution.py:435
  170.8 5.5 %all-to-all-done.3.first_ref.second_ref = f32[128,24,128]{2,1,0:T(8,128)} async-done(((f32[128,24,128]{2,1,0:T(8,128)}), f32[128,24,128]{2,1,0:T(8,128)}, u32[]{:S(2)}, u32[]{:S(2)}) %all-to-all-start.3) | async-done | bytes 1572896 | tf_op jit(solution)/shard_map/all_to_all | solution.py:312
  176.4 9.5 %far_queries.1 = (bf16[1024,1024]{1,0:T(8,128)(2,1)}, f32[2,32,8,512]{3,2,1,0:T(8,128)}, f32[2,32,8,512]{3,2,1,0:T(8,128)}) custom-call(s32[10]{0:T(128)} %pad_add_fusion.1.meta, bf16[1024,1536]{1,0:T(8,128)(2,1)} %convolution_convert_fusion.q_ref, bf16[1024,512]{1,0:T(8,128)(2,1)} %bitcast.91, f32[128,24,128]{2,1,0:T(8,128)} %all-to-all-done.3.first_ref.second_ref, ...), custom_call_target="tpu_custom_call" | custom-call | flops 2147483648 | bytes 10485760 | tf_op jit(solution)/shard_map/far_queries/pallas_call | solution.py:464
  190.3 9.9 %all-to-all-start.4 = ((bf16[64,16,512]{2,1,0:T(8,128)(2,1)}), bf16[64,16,512]{2,1,0:T(8,128)(2,1)S(1)}, u32[]{:S(2)}, u32[]{:S(2)}) async-start(bf16[64,16,512]{2,1,0:T(8,128)(2,1)} %bitcast.92), calls=%async_computation.4 | async-start | bytes 2097152 | tf_op jit(solution)/shard_map/all_to_all | solution.py:483
  200.2 1.7 convolution_convert_fusion.1
  203.5 2.2 %fusion.4 = bf16[1024,512]{1,0:T(8,128)(2,1)} fusion(f32[8,128,512]{2,1,0:T(8,128)S(1)} %fusion.27, bf16[1024,1024]{1,0:T(8,128)(2,1)S(1)} %copy-done.14, bf16[512,1536]{0,1:T(8,128)(2,1)S(1)} %bitcast.95), kind=kOutput, calls=%fused_computation.7 | convolution fusion | flops 1074790400 | bytes 6291456 | tf_op jit(solution)/shard_map/dot_general | solution.py:488
  205.7 13.6 %all-to-all-done.4 = bf16[64,16,512]{2,1,0:T(8,128)(2,1)S(1)} async-done(((bf16[64,16,512]{2,1,0:T(8,128)(2,1)}), bf16[64,16,512]{2,1,0:T(8,128)(2,1)S(1)}, u32[]{:S(2)}, u32[]{:S(2)}) %all-to-all-start.4) | async-done | bytes 1048608 | tf_op jit(solution)/shard_map/all_to_all | solution.py:483
  (69 shorter events, 22.3 us)
Async XLA Ops:
  0.6 23.4 %copy-start = (bf16[512,512]{1,0:T(8,128)(2,1)S(1)}, bf16[512,512]{1,0:T(8,128)(2,1)}, u32[]{:S(2)}) copy-start(bf16[512,512]{1,0:T(8,128)(2,1)} %param.10) | copy-start | bytes 1572868
  0.6 41.3 %collective-permute-start = (bf16[1024,512]{1,0:T(8,128)(2,1)}, bf16[1024,512]{1,0:T(8,128)(2,1)}, u32[]{:S(2)}, u32[]{:S(2)}) collective-permute-start(bf16[1024,512]{1,0:T(8,128)(2,1)} %x_ref.1), channel_id=1, source_target_pairs={{0,1},{1,0},{2,3},{3,2},{4,5},{5,4},{6,7},{7,6},{8,9},{9,8},{10,11... | collective-permute-start | bytes 3145736 | tf_op jit(solution)/shard_map/ppermute | solution.py:309
  8.8 34.5 %all-to-all-start = ((bf16[128,8,640]{2,1,0:T(8,128)(2,1)}), bf16[128,8,640]{2,1,0:T(8,128)(2,1)}, u32[]{:S(2)}, u32[]{:S(2)}) async-start(bf16[128,8,640]{2,1,0:T(8,128)(2,1)} %copy.58), calls=%async_computation | async-start | bytes 2621440 | tf_op jit(solution)/shard_map/all_to_all | solution.py:312
  26.0 1.0 copy-start.2
  27.0 3.8 %copy-start.1 = (bf16[1024,512]{1,0:T(8,128)(2,1)S(1)}, bf16[1024,512]{1,0:T(8,128)(2,1)}, u32[]{:S(2)}) copy-start(bf16[1024,512]{1,0:T(8,128)(2,1)} %x_ref.1) | copy-start | bytes 3145732
  34.7 5.4 %copy-start.8 = (bf16[1024,512]{1,0:T(8,128)(2,1)S(1)}, bf16[1024,512]{1,0:T(8,128)(2,1)}, u32[]{:S(2)}) copy-start(bf16[1024,512]{1,0:T(8,128)(2,1)} %param.14) | copy-start | bytes 3145732
  40.1 3.2 %copy-start.13 = (f32[128]{0:T(128)S(1)}, f32[128]{0:T(128)}, u32[]{:S(2)}) copy-start(f32[128]{0:T(128)} %constant.107) | copy-start | bytes 1540
  44.5 2.6 %copy-start.5 = (bf16[8,128,512]{2,0,1:T(8,128)(2,1)S(1)}, bf16[8,128,512]{2,0,1:T(8,128)(2,1)}, u32[]{:S(2)}) copy-start(bf16[8,128,512]{2,0,1:T(8,128)(2,1)} %copy.84) | copy-start | bytes 3145732
  48.7 10.1 %copy-start.12 = (s32[16,4]{0,1:T(4,128)S(1)}, s32[16,4]{0,1:T(4,128)}, u32[]{:S(2)}) copy-start(s32[16,4]{0,1:T(4,128)} %param.11) | copy-start | bytes 772
  48.7 39.2 %all-to-all-start.1 = ((bf16[128,8,1024]{2,1,0:T(8,128)(2,1)}), bf16[128,8,1024]{2,1,0:T(8,128)(2,1)}, u32[]{:S(2)}, u32[]{:S(2)}) async-start(bf16[128,8,1024]{2,1,0:T(8,128)(2,1)} %pad_maximum_fusion), calls=%async_computation.1 | async-start | bytes 4194304 | tf_op jit(solution)/shard_map/all_to_all | solution.py:312
  92.8 7.1 %copy-start.3 = (bf16[1024,512]{1,0:T(8,128)(2,1)S(1)}, bf16[1024,512]{1,0:T(8,128)(2,1)}, u32[]{:S(2)}) copy-start(bf16[1024,512]{1,0:T(8,128)(2,1)} %copy-done.2) | copy-start | bytes 3145732
  94.1 47.2 %all-to-all-start.2 = ((bf16[128,8,512]{2,1,0:T(8,128)(2,1)}), bf16[128,8,512]{2,1,0:T(8,128)(2,1)}, u32[]{:S(2)}, u32[]{:S(2)}) async-start(bf16[128,8,512]{2,1,0:T(8,128)(2,1)} %fusion.15), calls=%async_computation.2 | async-start | bytes 2097152 | tf_op jit(solution)/shard_map/all_to_all | solution.py:312
  99.9 41.4 %collective-permute-start.2 = (bf16[1024,512]{1,0:T(8,128)(2,1)S(1)}, bf16[1024,512]{1,0:T(8,128)(2,1)}, u32[]{:S(2)}, u32[]{:S(2)}) collective-permute-start(bf16[1024,512]{1,0:T(8,128)(2,1)S(1)} %copy-done.3), channel_id=1, source_target_pairs={{0,1},{1,0},{2,3},{3,2},{4,5},{5,4},{6,7},{7,6},{8,9},{9,8},{10,11... | collective-permute-start | bytes 3145736 | tf_op jit(solution)/shard_map/ppermute | solution.py:309
  113.9 27.3 %collective-permute-start.1 = (f32[8,24,128]{2,1,0:T(8,128)}, f32[8,24,128]{2,1,0:T(8,128)S(1)}, u32[]{:S(2)}, u32[]{:S(2)}) collective-permute-start(f32[8,24,128]{2,1,0:T(8,128)} %get-tuple-element.46.stats_ref), channel_id=1, source_target_pairs={{0,1},{1,0},{2,3},{3,2},{4,5},{5,4},{6,7},{7,6},{8,9},{9,8},{10,11... | collective-permute-start | bytes 294920 | tf_op jit(solution)/shard_map/ppermute | solution.py:309
  141.2 11.4 %copy-start.11 = (f32[8,24,128]{2,1,0:T(8,128)}, f32[8,24,128]{2,1,0:T(8,128)S(1)}, u32[]{:S(2)}) copy-start(f32[8,24,128]{2,1,0:T(8,128)S(1)} %collective-permute-done.1.stats_ref) | copy-start | bytes 294916
  141.3 35.1 %all-to-all-start.3 = ((f32[128,24,128]{2,1,0:T(8,128)}), f32[128,24,128]{2,1,0:T(8,128)}, u32[]{:S(2)}, u32[]{:S(2)}) async-start(f32[128,24,128]{2,1,0:T(8,128)} %get-tuple-element.55), calls=%async_computation.3 | async-start | bytes 3145728 | tf_op jit(solution)/shard_map/all_to_all | solution.py:312
  152.6 34.8 %collective-permute-start.3 = (f32[2,32,8,512]{3,2,1,0:T(8,128)}, f32[2,32,8,512]{3,2,1,0:T(8,128)S(1)}, u32[]{:S(2)}, u32[]{:S(2)}) collective-permute-start(f32[2,32,8,512]{3,2,1,0:T(8,128)} %get-tuple-element.61), channel_id=1, source_target_pairs={{0,2},{2,0},{4,6},{6,4},{8,10},{10,8},{12,14},{14,12},{16,18},{18,... | collective-permute-start | bytes 3145736 | tf_op jit(solution)/shard_map/ppermute | solution.py:440
  185.9 1.5 copy-start.9
  185.9 3.0 %collective-permute-start.4 = (f32[2,32,8,512]{3,2,1,0:T(8,128)}, f32[2,32,8,512]{3,2,1,0:T(8,128)S(1)}, u32[]{:S(2)}, u32[]{:S(2)}) collective-permute-start(f32[2,32,8,512]{3,2,1,0:T(8,128)} %get-tuple-element.63), channel_id=1, source_target_pairs={{0,2},{2,0},{4,6},{6,4},{8,10},{10,8},{12,14},{14,12},{16,18},{18,... | collective-permute-start | bytes 3145736 | tf_op jit(solution)/shard_map/ppermute | solution.py:440
  187.4 1.5 copy-start.10
  189.1 11.1 %copy-start.4 = (bf16[8,512,128]{2,1,0:T(8,128)(2,1)S(1)}, bf16[8,512,128]{2,1,0:T(8,128)(2,1)}, u32[]{:S(2)}) copy-start(bf16[8,512,128]{2,1,0:T(8,128)(2,1)} %get-tuple-element.45.att_ref) | copy-start | bytes 3145732
  190.3 29.1 %all-to-all-start.4 = ((bf16[64,16,512]{2,1,0:T(8,128)(2,1)}), bf16[64,16,512]{2,1,0:T(8,128)(2,1)S(1)}, u32[]{:S(2)}, u32[]{:S(2)}) async-start(bf16[64,16,512]{2,1,0:T(8,128)(2,1)} %bitcast.92), calls=%async_computation.4 | async-start | bytes 2097152 | tf_op jit(solution)/shard_map/all_to_all | solution.py:483
  200.2 1.7 copy-start.6
  200.2 1.7 copy-start.7
  201.9 1.6 copy-start.14

commit v8 on v7

--- a/solution.py
+++ b/solution.py
@@ -140,24 +140,27 @@
     for j in range(NBR):
         bias_scr[j] = bias_of(tile_ref[0, j])
     ids = [near_ids[i, j] for j in range(NBR)]
-    for c in range(pairs):
+
+    def products(c):
         cols = slice(c * LANES, (c + 1) * LANES)
         qz = two_heads(q_ref[:, cols])
         cz = two_heads(cot_ref[:, cols])
         qz_scr[c] = qz
         cz_scr[c] = cz
+        scores = [nt(k_ref[ids[j], :, cols], qz) + bias_scr[j] for j in range(NBR)] + [nt(fk_ref[0, :, cols], qz)]
+        grads = [nt(v_ref[ids[j], :, cols], cz) for j in range(NBR)] + [nt(fv_ref[0, :, cols], cz)]
+        return scores, grads
+
+    ready = products(0)
+    for c in range(pairs):
+        cols = slice(c * LANES, (c + 1) * LANES)
+        (scores, grads), ready = ready, products(c + 1) if c + 1 < pairs else None
         peak, inv, delta = load_rows(stats_ref, c, 3)
         parts = []
         for j in range(NBR + 1):
             rows = slice(j * bs, (j + 1) * bs)
-            if j < NBR:
-                scores = nt(k_ref[ids[j], :, cols], qz) + bias_scr[j]
-                grad_probs = nt(v_ref[ids[j], :, cols], cz)
-            else:
-                scores = nt(fk_ref[0, :, cols], qz)
-                grad_probs = nt(fv_ref[0, :, cols], cz)
-            probs = jnp.exp(scores - peak) * inv
-            parts.append((probs * (grad_probs - delta)).astype(BF16))
+            probs = jnp.exp(scores[j] - peak) * inv
+            parts.append((probs * (grads[j] - delta)).astype(BF16))
             if j < NBR:
                 p_scr[c, rows, :] = probs.astype(BF16)
                 ds_scr[c, rows, :] = parts[j]

time: 223 us -> 219 us (0.982)
  starting transfers between devices: 53.6 us -> 49.9 us
  transfers between devices with their start and end apart: 10 -> 10, of which waited for: 6 -> 6; matrix products, arithmetic and copies ran while one was open for 17% -> 17% of each run, Pallas kernels for 37% -> 38%
where the time goes in v8:
time: 219 us; the launch traced here: 216 us
  Pallas kernels  82.1 us (37%)
  starting transfers between devices  49.9 us (23%)
  waiting for transfers between devices  29.2 us (13%)
  local copies, waits for them, and re-layouts  22.7 us (10%)
  matrix products  19.6 us (9%)
  other arithmetic  11.6 us (5%)
    all_to_all x4, starting transfers between devices, exchange(): return lax.all_to_all(x, DEVICES, split_axis=0, concat_axis=0, tiled=True)  34 us
    pallas_call x1, Pallas kernels, body(): call(own_kernel, 2, own, [rows_spec, rows_spec, tile_spec, stats_spec, k_...  25.5 us
    pallas_call x1, Pallas kernels, body(): call(peer_kernel, 2, own, [pl.BlockSpec((bs, width), lambda i, *s: (own +...  17.8 us
    all_to_all x4, waiting for transfers between devices, exchange(): return lax.all_to_all(x, DEVICES, split_axis=0, concat_axis=0, tiled=True)  14.2 us
    all_to_all x1, waiting for transfers between devices, body(): lax.all_to_all(split, DEVICES, split_axis=0, concat_axis=0, axis_index_gr...  13.6 us
    pallas_call x1, Pallas kernels, body(): call(near_kernel, 2, own, [rows_spec, tile_spec, k_spec, v_spec], [pl.Blo...  12.8 us
    pallas_call x2, Pallas kernels, project(): call(project_kernel, 0, 3, [once((rows, width)), pl.BlockSpec((width, wid...  10.6 us
    pallas_call x1, Pallas kernels, body(): call(far_kernel, 1, own // 2, [pair_rows, pair_rows, pl.BlockSpec((1, STA...  9.52 us
  transfers between devices with their start and end apart: 10, of which 6 were waited for; matrix products, arithmetic and copies ran while one was open for 17% of the time, Pallas kernels for 38%

profile of v8, /device:TPU:0, one launch (start us, length us, event | category | flops | bytes accessed | tf_op | source)
XLA Modules:
  0.0 215.9 jit_solution(1588651150920366487)
XLA Ops:
  0.6 4.0 %collective-permute-start = (bf16[1024,512]{1,0:T(8,128)(2,1)}, bf16[1024,512]{1,0:T(8,128)(2,1)}, u32[]{:S(2)}, u32[]{:S(2)}) collective-permute-start(bf16[1024,512]{1,0:T(8,128)(2,1)} %x_ref.1), channel_id=1, source_target_pairs={{0,1},{1,0},{2,3},{3,2},{4,5},{5,4},{6,7},{7,6},{8,9},{9,8},{10,11... | collective-permute-start | bytes 3145736 | tf_op jit(solution)/shard_map/ppermute | solution.py:312
  6.9 1.8 copy.58
  8.8 8.5 %all-to-all-start = ((bf16[128,8,640]{2,1,0:T(8,128)(2,1)}), bf16[128,8,640]{2,1,0:T(8,128)(2,1)}, u32[]{:S(2)}, u32[]{:S(2)}) async-start(bf16[128,8,640]{2,1,0:T(8,128)(2,1)} %copy.58), calls=%async_computation | async-start | bytes 2621440 | tf_op jit(solution)/shard_map/all_to_all | solution.py:315
  17.3 1.7 copy.60
  19.9 2.1 copy.77
  24.1 2.0 convolution_convert_fusion.3.cot_ref
  27.0 1.5 copy.84
  28.5 2.3 %copy.66 = bf16[8,128,512]{1,2,0:T(8,128)(2,1)} copy(bf16[8,128,512]{2,1,0:T(8,128)(2,1)} %bitcast.99) | data formatting | bytes 2097152 | tf_op jit(solution)/shard_map/reshape | solution.py:333
  32.1 2.6 %pad_maximum_fusion.1.w_ref = bf16[512,1536]{1,0:T(8,128)(2,1)} fusion(bf16[512,512]{1,0:T(8,128)(2,1)} %copy.79, bf16[512,512]{1,0:T(8,128)(2,1)} %copy.78, bf16[512,512]{1,0:T(8,128)(2,1)} %copy.77), kind=kLoop, calls=%fused_computation.13 | loop fusion | flops 4718592 | bytes 3145728 | tf_op jit(solution)/shard_map/concatenate | solution.py:309
  34.7 5.4 %project_own.1.rest_0_ = bf16[2048,1536]{1,0:T(8,128)(2,1)} custom-call(bf16[1024,512]{1,0:T(8,128)(2,1)} %x_ref.1, bf16[512,1536]{1,0:T(8,128)(2,1)} %pad_maximum_fusion.1.w_ref), custom_call_target="tpu_custom_call" | custom-call | flops 1610612736 | bytes 6291456 | tf_op jit(solution)/shard_map/project_own/pallas_call | solution.py:338
  40.1 1.7 fusion.21.cot_t_ref
  44.5 2.6 %fusion.18 = bf16[128,8,512]{2,1,0:T(8,128)(2,1)S(1)} fusion(f32[1024]{0:T(1024)S(1)} %iota_convert_fusion, f32[1024]{0:T(1024)S(1)} %multiply_reduce_fusion, bf16[128,8,640]{2,1,0:T(8,128)(2,1)} %all-to-all-done), kind=kOutput, calls=%fused_computation.20 | convolution fusion | flops 1075314688 | bytes 2105344 | tf_op jit(solution)/shard_map/dot_general | solution.py:321
  47.1 1.6 pad_maximum_fusion
  48.7 10.1 %all-to-all-start.1 = ((bf16[128,8,1024]{2,1,0:T(8,128)(2,1)}), bf16[128,8,1024]{2,1,0:T(8,128)(2,1)}, u32[]{:S(2)}, u32[]{:S(2)}) async-start(bf16[128,8,1024]{2,1,0:T(8,128)(2,1)} %pad_maximum_fusion), calls=%async_computation.1 | async-start | bytes 4194304 | tf_op jit(solution)/shard_map/all_to_all | solution.py:315
  60.4 5.3 %project_peer.1.q_ref = bf16[2048,1536]{1,0:T(8,128)(2,1)} custom-call(bf16[1024,512]{1,0:T(8,128)(2,1)} %collective-permute-done.x_ref, bf16[512,1536]{1,0:T(8,128)(2,1)} %pad_maximum_fusion.1.w_ref, bf16[2048,1536]{1,0:T(8,128)(2,1)} %project_own.1.rest_0_), custom_call_target="tpu_custom_call", output_to_operand_aliasing={{}: (2, {})} | custom-call | flops 1610612736 | bytes 6291456 | tf_op jit(solution)/shard_map/project_peer/pallas_call | solution.py:338
  65.6 12.8 %near_forward.1 = (f32[8,512,128]{2,1,0:T(8,128)}, f32[8,16,128]{2,1,0:T(8,128)}) custom-call(s32[16,4]{1,0:T(8,128)} %copy.80.near_ids, s32[10]{0:T(128)} %pad_add_fusion.1.meta, bf16[2048,1536]{1,0:T(8,128)(2,1)} %project_peer.1.q_ref, s32[16,4,128,128]{3,2,1,0:T(8,128)} %tile_ref.5, bf16[16,128,1536]{2,1,0:T(8,128)(2,1)} %bitcast.71, ...), custom_call_target="tpu_custom_call" | custom-call | flops 4294967296 | bytes 10485760 | tf_op jit(solution)/shard_map/near_forward/pallas_call | solution.py:375
  78.4 9.5 %all-to-all-done.1 = bf16[128,8,1024]{2,1,0:T(8,128)(2,1)} async-done(((bf16[128,8,1024]{2,1,0:T(8,128)(2,1)}), bf16[128,8,1024]{2,1,0:T(8,128)(2,1)}, u32[]{:S(2)}, u32[]{:S(2)}) %all-to-all-start.1) | async-done | bytes 2097184 | tf_op jit(solution)/shard_map/all_to_all | solution.py:315
  89.3 3.5 %fusion.15 = bf16[128,8,512]{2,1,0:T(8,128)(2,1)} fusion(f32[1024]{0:T(1024)S(1)} %iota_convert_fusion, f32[1024]{0:T(1024)S(1)} %multiply_reduce_fusion, bf16[128,8,1024]{2,1,0:T(8,128)(2,1)} %all-to-all-done.1), kind=kOutput, calls=%fused_computation.19 | convolution fusion | flops 1075314688 | bytes 2105344 | tf_op jit(solution)/shard_map/dot_general | solution.py:321
  94.1 5.8 %all-to-all-start.2 = ((bf16[128,8,512]{2,1,0:T(8,128)(2,1)}), bf16[128,8,512]{2,1,0:T(8,128)(2,1)}, u32[]{:S(2)}, u32[]{:S(2)}) async-start(bf16[128,8,512]{2,1,0:T(8,128)(2,1)} %fusion.15), calls=%async_computation.2 | async-start | bytes 2097152 | tf_op jit(solution)/shard_map/all_to_all | solution.py:315
  99.9 3.0 %collective-permute-start.2 = (bf16[1024,512]{1,0:T(8,128)(2,1)S(1)}, bf16[1024,512]{1,0:T(8,128)(2,1)}, u32[]{:S(2)}, u32[]{:S(2)}) collective-permute-start(bf16[1024,512]{1,0:T(8,128)(2,1)S(1)} %copy-done.3), channel_id=1, source_target_pairs={{0,1},{1,0},{2,3},{3,2},{4,5},{5,4},{6,7},{7,6},{8,9},{9,8},{10,11... | collective-permute-start | bytes 3145736 | tf_op jit(solution)/shard_map/ppermute | solution.py:312
  102.9 5.1 %convolution_convert_fusion.q_ref = bf16[1024,1536]{1,0:T(8,128)(2,1)} fusion(bf16[1024,512]{1,0:T(8,128)(2,1)} %bitcast.102, bf16[512,512]{1,0:T(8,128)(2,1)} %copy.79, bf16[512,512]{1,0:T(8,128)(2,1)} %copy.78, bf16[512,512]{1,0:T(8,128)(2,1)} %copy.77), kind=kOutput, calls=%fused_computation.4 | convolution fusion | flops 1616904192 | bytes 5767168 | tf_op jit(solution)/shard_map/dot_general | solution.py:389
  108.0 5.9 %far_forward.1 = (bf16[8,512,128]{2,1,0:T(8,128)(2,1)}, f32[8,24,128]{2,1,0:T(8,128)}) custom-call(bf16[2048,1536]{1,0:T(8,128)(2,1)} %project_peer.1.q_ref, bf16[8,512,128]{2,1,0:T(8,128)(2,1)} %fusion.21.cot_t_ref, bf16[8,128,1536]{2,1,0:T(8,128)(2,1)} %bitcast.79, bf16[8,128,1536]{2,1,0:T(8,128)(2,1)} %bitcast.80, ...), custom_call_target="tpu_custom_call" | custom-call | flops 1073741824 | bytes 6291456 | tf_op jit(solution)/shard_map/far_forward/pallas_call | solution.py:399
  114.6 25.5 %own_backward.1 = (bf16[8,512,128]{2,1,0:T(8,128)(2,1)}, f32[8,128,1024]{2,1,0:T(8,128)}, f32[2,32,8,512]{3,2,1,0:T(8,128)}, f32[2,32,8,512]{3,2,1,0:T(8,128)}, f32[128,24,128]{2,1,0:T(8,128)}) custom-call(s32[16,4]{1,0:T(8,128)} %copy.80.near_ids, s32[10]{0:T(128)} %pad_add_fusion.1.meta, bf16[2048,1536]{1,0:T(8,128)(2,1)} %project_peer.1.q_ref, ...), custom_call_target="tpu_custom_call" | custom-call | flops 6442450944 | bytes 31457280 | tf_op jit(solution)/shard_map/own_backward/pallas_call | solution.py:412
  140.2 9.7 %all-to-all-start.3 = ((f32[128,24,128]{2,1,0:T(8,128)}), f32[128,24,128]{2,1,0:T(8,128)}, u32[]{:S(2)}, u32[]{:S(2)}) async-start(f32[128,24,128]{2,1,0:T(8,128)} %get-tuple-element.55), calls=%async_computation.3 | async-start | bytes 3145728 | tf_op jit(solution)/shard_map/all_to_all | solution.py:315
  149.9 17.8 %peer_queries.1.acc_ref = f32[8,128,1024]{2,1,0:T(8,128)} custom-call(s32[16,4]{1,0:T(8,128)} %copy.80.near_ids, s32[10]{0:T(128)} %pad_add_fusion.1.meta, bf16[2048,1536]{1,0:T(8,128)(2,1)} %project_peer.1.q_ref, bf16[1024,512]{1,0:T(8,128)(2,1)} %collective-permute-done.2.cot_ref, f32[8,24,128]{2,1,0:T(8,128)} %copy-done.11, s32[16,4,128,128]{3,2,1,0:T(8,128)} %tile_ref.5, ...), custom_call_target="tpu_custom_call" | custom-call | flops 4294967296 | bytes 20971520 | tf_op jit(solution)/shard_map/peer_queries/pallas_call | solution.py:447
  167.7 2.5 %copy.73 = bf16[8,128,512]{2,1,0:T(8,128)(2,1)} copy(bf16[8,128,512]{2,0,1:T(8,128)(2,1)} %bitcast.34) | data formatting | bytes 2097152 | tf_op jit(solution)/shard_map/transpose | solution.py:438
  170.2 3.4 %all-to-all-done.3.first_ref.second_ref = f32[128,24,128]{2,1,0:T(8,128)} async-done(((f32[128,24,128]{2,1,0:T(8,128)}), f32[128,24,128]{2,1,0:T(8,128)}, u32[]{:S(2)}, u32[]{:S(2)}) %all-to-all-start.3) | async-done | bytes 1572896 | tf_op jit(solution)/shard_map/all_to_all | solution.py:315
  173.6 9.5 %far_queries.1 = (bf16[1024,1024]{1,0:T(8,128)(2,1)}, f32[2,32,8,512]{3,2,1,0:T(8,128)}, f32[2,32,8,512]{3,2,1,0:T(8,128)}) custom-call(s32[10]{0:T(128)} %pad_add_fusion.1.meta, bf16[1024,1536]{1,0:T(8,128)(2,1)} %convolution_convert_fusion.q_ref, bf16[1024,512]{1,0:T(8,128)(2,1)} %bitcast.91, f32[128,24,128]{2,1,0:T(8,128)} %all-to-all-done.3.first_ref.second_ref, ...), custom_call_target="tpu_custom_call" | custom-call | flops 2147483648 | bytes 10485760 | tf_op jit(solution)/shard_map/far_queries/pallas_call | solution.py:467
  187.5 7.9 %all-to-all-start.4 = ((bf16[64,16,512]{2,1,0:T(8,128)(2,1)}), bf16[64,16,512]{2,1,0:T(8,128)(2,1)S(1)}, u32[]{:S(2)}, u32[]{:S(2)}) async-start(bf16[64,16,512]{2,1,0:T(8,128)(2,1)} %bitcast.92), calls=%async_computation.4 | async-start | bytes 2097152 | tf_op jit(solution)/shard_map/all_to_all | solution.py:486
  195.4 1.7 convolution_convert_fusion.1
  198.7 2.2 %fusion.4 = bf16[1024,512]{1,0:T(8,128)(2,1)} fusion(f32[8,128,512]{2,1,0:T(8,128)S(1)} %fusion.27, bf16[1024,1024]{1,0:T(8,128)(2,1)S(1)} %copy-done.14, bf16[512,1536]{0,1:T(8,128)(2,1)S(1)} %bitcast.95), kind=kOutput, calls=%fused_computation.7 | convolution fusion | flops 1074790400 | bytes 6291456 | tf_op jit(solution)/shard_map/dot_general | solution.py:491
  200.9 13.6 %all-to-all-done.4 = bf16[64,16,512]{2,1,0:T(8,128)(2,1)S(1)} async-done(((bf16[64,16,512]{2,1,0:T(8,128)(2,1)}), bf16[64,16,512]{2,1,0:T(8,128)(2,1)S(1)}, u32[]{:S(2)}, u32[]{:S(2)}) %all-to-all-start.4) | async-done | bytes 1048608 | tf_op jit(solution)/shard_map/all_to_all | solution.py:486
  (69 shorter events, 22.3 us)
Async XLA Ops:
  0.6 23.4 %copy-start = (bf16[512,512]{1,0:T(8,128)(2,1)S(1)}, bf16[512,512]{1,0:T(8,128)(2,1)}, u32[]{:S(2)}) copy-start(bf16[512,512]{1,0:T(8,128)(2,1)} %param.10) | copy-start | bytes 1572868
  0.6 41.3 %collective-permute-start = (bf16[1024,512]{1,0:T(8,128)(2,1)}, bf16[1024,512]{1,0:T(8,128)(2,1)}, u32[]{:S(2)}, u32[]{:S(2)}) collective-permute-start(bf16[1024,512]{1,0:T(8,128)(2,1)} %x_ref.1), channel_id=1, source_target_pairs={{0,1},{1,0},{2,3},{3,2},{4,5},{5,4},{6,7},{7,6},{8,9},{9,8},{10,11... | collective-permute-start | bytes 3145736 | tf_op jit(solution)/shard_map/ppermute | solution.py:312
  8.8 34.5 %all-to-all-start = ((bf16[128,8,640]{2,1,0:T(8,128)(2,1)}), bf16[128,8,640]{2,1,0:T(8,128)(2,1)}, u32[]{:S(2)}, u32[]{:S(2)}) async-start(bf16[128,8,640]{2,1,0:T(8,128)(2,1)} %copy.58), calls=%async_computation | async-start | bytes 2621440 | tf_op jit(solution)/shard_map/all_to_all | solution.py:315
  26.0 1.0 copy-start.2
  27.0 3.8 %copy-start.1 = (bf16[1024,512]{1,0:T(8,128)(2,1)S(1)}, bf16[1024,512]{1,0:T(8,128)(2,1)}, u32[]{:S(2)}) copy-start(bf16[1024,512]{1,0:T(8,128)(2,1)} %x_ref.1) | copy-start | bytes 3145732
  34.7 5.4 %copy-start.8 = (bf16[1024,512]{1,0:T(8,128)(2,1)S(1)}, bf16[1024,512]{1,0:T(8,128)(2,1)}, u32[]{:S(2)}) copy-start(bf16[1024,512]{1,0:T(8,128)(2,1)} %param.14) | copy-start | bytes 3145732
  40.1 3.2 %copy-start.13 = (f32[128]{0:T(128)S(1)}, f32[128]{0:T(128)}, u32[]{:S(2)}) copy-start(f32[128]{0:T(128)} %constant.107) | copy-start | bytes 1540
  44.5 2.6 %copy-start.5 = (bf16[8,128,512]{2,0,1:T(8,128)(2,1)S(1)}, bf16[8,128,512]{2,0,1:T(8,128)(2,1)}, u32[]{:S(2)}) copy-start(bf16[8,128,512]{2,0,1:T(8,128)(2,1)} %copy.84) | copy-start | bytes 3145732
  48.7 10.1 %copy-start.12 = (s32[16,4]{0,1:T(4,128)S(1)}, s32[16,4]{0,1:T(4,128)}, u32[]{:S(2)}) copy-start(s32[16,4]{0,1:T(4,128)} %param.11) | copy-start | bytes 772
  48.7 39.2 %all-to-all-start.1 = ((bf16[128,8,1024]{2,1,0:T(8,128)(2,1)}), bf16[128,8,1024]{2,1,0:T(8,128)(2,1)}, u32[]{:S(2)}, u32[]{:S(2)}) async-start(bf16[128,8,1024]{2,1,0:T(8,128)(2,1)} %pad_maximum_fusion), calls=%async_computation.1 | async-start | bytes 4194304 | tf_op jit(solution)/shard_map/all_to_all | solution.py:315
  92.8 7.1 %copy-start.3 = (bf16[1024,512]{1,0:T(8,128)(2,1)S(1)}, bf16[1024,512]{1,0:T(8,128)(2,1)}, u32[]{:S(2)}) copy-start(bf16[1024,512]{1,0:T(8,128)(2,1)} %copy-done.2) | copy-start | bytes 3145732
  94.1 46.1 %all-to-all-start.2 = ((bf16[128,8,512]{2,1,0:T(8,128)(2,1)}), bf16[128,8,512]{2,1,0:T(8,128)(2,1)}, u32[]{:S(2)}, u32[]{:S(2)}) async-start(bf16[128,8,512]{2,1,0:T(8,128)(2,1)} %fusion.15), calls=%async_computation.2 | async-start | bytes 2097152 | tf_op jit(solution)/shard_map/all_to_all | solution.py:315
  99.9 40.3 %collective-permute-start.2 = (bf16[1024,512]{1,0:T(8,128)(2,1)S(1)}, bf16[1024,512]{1,0:T(8,128)(2,1)}, u32[]{:S(2)}, u32[]{:S(2)}) collective-permute-start(bf16[1024,512]{1,0:T(8,128)(2,1)S(1)} %copy-done.3), channel_id=1, source_target_pairs={{0,1},{1,0},{2,3},{3,2},{4,5},{5,4},{6,7},{7,6},{8,9},{9,8},{10,11... | collective-permute-start | bytes 3145736 | tf_op jit(solution)/shard_map/ppermute | solution.py:312
  113.9 26.2 %collective-permute-start.1 = (f32[8,24,128]{2,1,0:T(8,128)}, f32[8,24,128]{2,1,0:T(8,128)S(1)}, u32[]{:S(2)}, u32[]{:S(2)}) collective-permute-start(f32[8,24,128]{2,1,0:T(8,128)} %get-tuple-element.46.stats_ref), channel_id=1, source_target_pairs={{0,1},{1,0},{2,3},{3,2},{4,5},{5,4},{6,7},{7,6},{8,9},{9,8},{10,11... | collective-permute-start | bytes 294920 | tf_op jit(solution)/shard_map/ppermute | solution.py:312
  140.1 9.8 %copy-start.11 = (f32[8,24,128]{2,1,0:T(8,128)}, f32[8,24,128]{2,1,0:T(8,128)S(1)}, u32[]{:S(2)}) copy-start(f32[8,24,128]{2,1,0:T(8,128)S(1)} %collective-permute-done.1.stats_ref) | copy-start | bytes 294916
  140.2 33.5 %all-to-all-start.3 = ((f32[128,24,128]{2,1,0:T(8,128)}), f32[128,24,128]{2,1,0:T(8,128)}, u32[]{:S(2)}, u32[]{:S(2)}) async-start(f32[128,24,128]{2,1,0:T(8,128)} %get-tuple-element.55), calls=%async_computation.3 | async-start | bytes 3145728 | tf_op jit(solution)/shard_map/all_to_all | solution.py:315
  149.8 34.8 %collective-permute-start.3 = (f32[2,32,8,512]{3,2,1,0:T(8,128)}, f32[2,32,8,512]{3,2,1,0:T(8,128)S(1)}, u32[]{:S(2)}, u32[]{:S(2)}) collective-permute-start(f32[2,32,8,512]{3,2,1,0:T(8,128)} %get-tuple-element.61), channel_id=1, source_target_pairs={{0,2},{2,0},{4,6},{6,4},{8,10},{10,8},{12,14},{14,12},{16,18},{18,... | collective-permute-start | bytes 3145736 | tf_op jit(solution)/shard_map/ppermute | solution.py:443
  183.1 1.5 copy-start.9
  183.1 3.0 %collective-permute-start.4 = (f32[2,32,8,512]{3,2,1,0:T(8,128)}, f32[2,32,8,512]{3,2,1,0:T(8,128)S(1)}, u32[]{:S(2)}, u32[]{:S(2)}) collective-permute-start(f32[2,32,8,512]{3,2,1,0:T(8,128)} %get-tuple-element.63), channel_id=1, source_target_pairs={{0,2},{2,0},{4,6},{6,4},{8,10},{10,8},{12,14},{14,12},{16,18},{18,... | collective-permute-start | bytes 3145736 | tf_op jit(solution)/shard_map/ppermute | solution.py:443
  184.6 1.5 copy-start.10
  186.4 9.0 %copy-start.4 = (bf16[8,512,128]{2,1,0:T(8,128)(2,1)S(1)}, bf16[8,512,128]{2,1,0:T(8,128)(2,1)}, u32[]{:S(2)}) copy-start(bf16[8,512,128]{2,1,0:T(8,128)(2,1)} %get-tuple-element.45.att_ref) | copy-start | bytes 3145732
  187.5 27.0 %all-to-all-start.4 = ((bf16[64,16,512]{2,1,0:T(8,128)(2,1)}), bf16[64,16,512]{2,1,0:T(8,128)(2,1)S(1)}, u32[]{:S(2)}, u32[]{:S(2)}) async-start(bf16[64,16,512]{2,1,0:T(8,128)(2,1)} %bitcast.92), calls=%async_computation.4 | async-start | bytes 2097152 | tf_op jit(solution)/shard_map/all_to_all | solution.py:486
  195.4 1.7 copy-start.6
  195.4 1.7 copy-start.7
  197.1 1.6 copy-start.14

commit v9 on v8

--- a/solution.py
+++ b/solution.py
@@ -196,12 +196,12 @@
     ]
 
 
-def key_terms(ks, vs, qzs, czs, bias, stats):
+def key_terms(ks, vs, qzs, czs, biases, stats):
     scores = [nt(k, qz) for k, qz in zip(ks, qzs)]
     grads = [nt(v, cz) for v, cz in zip(vs, czs)]
-    probs = [
-        jnp.exp((s if bias is None else s + bias) - peak) * inv for s, (peak, inv, _) in zip(scores, stats)
-    ]
+    if biases is not None:
+        scores = [s + bias for s, bias in zip(scores, biases)]
+    probs = [jnp.exp(s - peak) * inv for s, (peak, inv, _) in zip(scores, stats)]
     ds = [(p * (g - delta)).astype(BF16) for p, g, (_, _, delta) in zip(probs, grads, stats)]
     return [nn(d, qz) for d, qz in zip(ds, qzs)], [nn(p.astype(BF16), cz) for p, cz in zip(probs, czs)]
 
@@ -220,21 +220,36 @@
         cols = slice(c * LANES, (c + 1) * LANES)
         qz_scr[c] = two_heads(q_ref[:, cols])
         cz_scr[c] = two_heads(cot_ref[:, cols])
-    for j in range(NBR):
-        n = near_ids[own + i, j]
-
-        @pl.when(n < own)
-        def _(j=j, n=n):
-            every = range(pairs)
-            cols = [slice(c * LANES, (c + 1) * LANES) for c in every]
+    ids = [near_ids[own + i, j] for j in range(NBR)]
+    taken = [jnp.where(n < own, 1, 0) for n in ids]
+    before = [sum(taken[:j], 0) for j in range(NBR)]
+    count = sum(taken)
+    order = [sum(jnp.where((before[j] == k) & (ids[j] < own), j, 0) for j in range(NBR)) for k in range(NBR)]
+    every = range(pairs)
+    cols = [slice(c * LANES, (c + 1) * LANES) for c in every]
+    for k in range(0, NBR, 2):
+
+        @pl.when(count > k)
+        def _(k=k):
+            both = count > k + 1
+            slots = (order[k], jnp.where(both, order[k + 1], order[k]))
+            weights = (None, jnp.where(both, 1.0, 0.0).astype(F32))
+            blocks = [near_ids[own + i, j] for j in slots]
+            ks, vs, biases, stats = [], [], [], []
+            for n, j, weight in zip(blocks, slots, weights):
+                ks += [k_ref[n, :, cols[c]] for c in every]
+                vs += [v_ref[n, :, cols[c]] for c in every]
+                biases += [bias_of(tile_ref[0, j])] * pairs
+                for c in every:
+                    peak, inv, delta = load_rows(stats_ref, c, 3)
+                    stats.append((peak, inv if weight is None else inv * weight, delta))
             dks, dvs = key_terms(
-                [k_ref[n, :, cols[c]] for c in every], [v_ref[n, :, cols[c]] for c in every],
-                [qz_scr[c] for c in every], [cz_scr[c] for c in every], bias_of(tile_ref[0, j]),
-                [load_rows(stats_ref, c, 3) for c in every],
+                ks, vs, [qz_scr[c] for c in every] * 2, [cz_scr[c] for c in every] * 2, biases, stats
             )
-            for c in every:
-                acc_ref[n, :, cols[c]] += dks[c]
-                acc_ref[n, :, width + c * LANES : width + (c + 1) * LANES] += dvs[c]
+            for b, n in enumerate(blocks):
+                for c in every:
+                    acc_ref[n, :, cols[c]] += dks[b * pairs + c]
+                    acc_ref[n, :, width + c * LANES : width + (c + 1) * LANES] += dvs[b * pairs + c]
 
 
 def far_kernel(meta, q_ref, cot_ref, first_ref, second_ref, k_ref, v_ref, acc_ref, xt_ref, dkv_ref, kept_ref,

time: 219 us -> 218 us (level)
  no operation moved by 1% of the time
where the time goes in v9:
time: 218 us; the launch traced here: 216 us
  Pallas kernels  81.9 us (38%)
  starting transfers between devices  49.7 us (23%)
  waiting for transfers between devices  29.7 us (14%)
  local copies, waits for them, and re-layouts  22.7 us (10%)
  matrix products  19.6 us (9%)
  other arithmetic  11.6 us (5%)
    all_to_all x4, starting transfers between devices, exchange(): return lax.all_to_all(x, DEVICES, split_axis=0, concat_axis=0, tiled=True)  34.5 us
    pallas_call x1, Pallas kernels, body(): call(own_kernel, 2, own, [rows_spec, rows_spec, tile_spec, stats_spec, k_...  25.8 us
    pallas_call x1, Pallas kernels, body(): call(peer_kernel, 2, own, [pl.BlockSpec((bs, width), lambda i, *s: (own +...  17.3 us
    all_to_all x4, waiting for transfers between devices, exchange(): return lax.all_to_all(x, DEVICES, split_axis=0, concat_axis=0, tiled=True)  14.7 us
    all_to_all x1, waiting for transfers between devices, body(): lax.all_to_all(split, DEVICES, split_axis=0, concat_axis=0, axis_index_gr...  13.6 us
    pallas_call x1, Pallas kernels, body(): call(near_kernel, 2, own, [rows_spec, tile_spec, k_spec, v_spec], [pl.Blo...  12.8 us
    pallas_call x2, Pallas kernels, project(): call(project_kernel, 0, 3, [once((rows, width)), pl.BlockSpec((width, wid...  10.6 us
    pallas_call x1, Pallas kernels, body(): call(far_kernel, 1, own // 2, [pair_rows, pair_rows, pl.BlockSpec((1, STA...  9.52 us
  transfers between devices with their start and end apart: 10, of which 6 were waited for; matrix products, arithmetic and copies ran while one was open for 17% of the time, Pallas kernels for 38%

profile of v9, /device:TPU:0, one launch (start us, length us, event | category | flops | bytes accessed | tf_op | source)
XLA Modules:
  0.0 216.0 jit_solution(7892707661242281824)
XLA Ops:
  0.6 4.0 %collective-permute-start = (bf16[1024,512]{1,0:T(8,128)(2,1)}, bf16[1024,512]{1,0:T(8,128)(2,1)}, u32[]{:S(2)}, u32[]{:S(2)}) collective-permute-start(bf16[1024,512]{1,0:T(8,128)(2,1)} %x_ref.1), channel_id=1, source_target_pairs={{0,1},{1,0},{2,3},{3,2},{4,5},{5,4},{6,7},{7,6},{8,9},{9,8},{10,11... | collective-permute-start | bytes 3145736 | tf_op jit(solution)/shard_map/ppermute | solution.py:327
  6.9 1.8 copy.58
  8.8 8.5 %all-to-all-start = ((bf16[128,8,640]{2,1,0:T(8,128)(2,1)}), bf16[128,8,640]{2,1,0:T(8,128)(2,1)}, u32[]{:S(2)}, u32[]{:S(2)}) async-start(bf16[128,8,640]{2,1,0:T(8,128)(2,1)} %copy.58), calls=%async_computation | async-start | bytes 2621440 | tf_op jit(solution)/shard_map/all_to_all | solution.py:330
  17.3 1.7 copy.60
  19.9 2.1 copy.77
  24.1 2.0 convolution_convert_fusion.3.cot_ref
  27.0 1.5 copy.84
  28.5 2.3 %copy.66 = bf16[8,128,512]{1,2,0:T(8,128)(2,1)} copy(bf16[8,128,512]{2,1,0:T(8,128)(2,1)} %bitcast.99) | data formatting | bytes 2097152 | tf_op jit(solution)/shard_map/reshape | solution.py:348
  32.1 2.6 %pad_maximum_fusion.1.w_ref = bf16[512,1536]{1,0:T(8,128)(2,1)} fusion(bf16[512,512]{1,0:T(8,128)(2,1)} %copy.79, bf16[512,512]{1,0:T(8,128)(2,1)} %copy.78, bf16[512,512]{1,0:T(8,128)(2,1)} %copy.77), kind=kLoop, calls=%fused_computation.13 | loop fusion | flops 4718592 | bytes 3145728 | tf_op jit(solution)/shard_map/concatenate | solution.py:324
  34.7 5.4 %project_own.1.rest_0_ = bf16[2048,1536]{1,0:T(8,128)(2,1)} custom-call(bf16[1024,512]{1,0:T(8,128)(2,1)} %x_ref.1, bf16[512,1536]{1,0:T(8,128)(2,1)} %pad_maximum_fusion.1.w_ref), custom_call_target="tpu_custom_call" | custom-call | flops 1610612736 | bytes 6291456 | tf_op jit(solution)/shard_map/project_own/pallas_call | solution.py:353
  40.1 1.7 fusion.21.cot_t_ref
  44.5 2.6 %fusion.18 = bf16[128,8,512]{2,1,0:T(8,128)(2,1)S(1)} fusion(f32[1024]{0:T(1024)S(1)} %iota_convert_fusion, f32[1024]{0:T(1024)S(1)} %multiply_reduce_fusion, bf16[128,8,640]{2,1,0:T(8,128)(2,1)} %all-to-all-done), kind=kOutput, calls=%fused_computation.20 | convolution fusion | flops 1075314688 | bytes 2105344 | tf_op jit(solution)/shard_map/dot_general | solution.py:336
  47.1 1.6 pad_maximum_fusion
  48.7 10.1 %all-to-all-start.1 = ((bf16[128,8,1024]{2,1,0:T(8,128)(2,1)}), bf16[128,8,1024]{2,1,0:T(8,128)(2,1)}, u32[]{:S(2)}, u32[]{:S(2)}) async-start(bf16[128,8,1024]{2,1,0:T(8,128)(2,1)} %pad_maximum_fusion), calls=%async_computation.1 | async-start | bytes 4194304 | tf_op jit(solution)/shard_map/all_to_all | solution.py:330
  60.4 5.3 %project_peer.1.q_ref = bf16[2048,1536]{1,0:T(8,128)(2,1)} custom-call(bf16[1024,512]{1,0:T(8,128)(2,1)} %collective-permute-done.x_ref, bf16[512,1536]{1,0:T(8,128)(2,1)} %pad_maximum_fusion.1.w_ref, bf16[2048,1536]{1,0:T(8,128)(2,1)} %project_own.1.rest_0_), custom_call_target="tpu_custom_call", output_to_operand_aliasing={{}: (2, {})} | custom-call | flops 1610612736 | bytes 6291456 | tf_op jit(solution)/shard_map/project_peer/pallas_call | solution.py:353
  65.6 12.8 %near_forward.1 = (f32[8,512,128]{2,1,0:T(8,128)}, f32[8,16,128]{2,1,0:T(8,128)}) custom-call(s32[16,4]{1,0:T(8,128)} %copy.80.near_ids, s32[10]{0:T(128)} %pad_add_fusion.1.meta, bf16[2048,1536]{1,0:T(8,128)(2,1)} %project_peer.1.q_ref, s32[16,4,128,128]{3,2,1,0:T(8,128)} %tile_ref.5, bf16[16,128,1536]{2,1,0:T(8,128)(2,1)} %bitcast.71, ...), custom_call_target="tpu_custom_call" | custom-call | flops 4294967296 | bytes 10485760 | tf_op jit(solution)/shard_map/near_forward/pallas_call | solution.py:390
  78.4 9.5 %all-to-all-done.1 = bf16[128,8,1024]{2,1,0:T(8,128)(2,1)} async-done(((bf16[128,8,1024]{2,1,0:T(8,128)(2,1)}), bf16[128,8,1024]{2,1,0:T(8,128)(2,1)}, u32[]{:S(2)}, u32[]{:S(2)}) %all-to-all-start.1) | async-done | bytes 2097184 | tf_op jit(solution)/shard_map/all_to_all | solution.py:330
  89.3 3.5 %fusion.15 = bf16[128,8,512]{2,1,0:T(8,128)(2,1)} fusion(f32[1024]{0:T(1024)S(1)} %iota_convert_fusion, f32[1024]{0:T(1024)S(1)} %multiply_reduce_fusion, bf16[128,8,1024]{2,1,0:T(8,128)(2,1)} %all-to-all-done.1), kind=kOutput, calls=%fused_computation.19 | convolution fusion | flops 1075314688 | bytes 2105344 | tf_op jit(solution)/shard_map/dot_general | solution.py:336
  94.1 5.8 %all-to-all-start.2 = ((bf16[128,8,512]{2,1,0:T(8,128)(2,1)}), bf16[128,8,512]{2,1,0:T(8,128)(2,1)}, u32[]{:S(2)}, u32[]{:S(2)}) async-start(bf16[128,8,512]{2,1,0:T(8,128)(2,1)} %fusion.15), calls=%async_computation.2 | async-start | bytes 2097152 | tf_op jit(solution)/shard_map/all_to_all | solution.py:330
  99.9 3.0 %collective-permute-start.2 = (bf16[1024,512]{1,0:T(8,128)(2,1)S(1)}, bf16[1024,512]{1,0:T(8,128)(2,1)}, u32[]{:S(2)}, u32[]{:S(2)}) collective-permute-start(bf16[1024,512]{1,0:T(8,128)(2,1)S(1)} %copy-done.3), channel_id=1, source_target_pairs={{0,1},{1,0},{2,3},{3,2},{4,5},{5,4},{6,7},{7,6},{8,9},{9,8},{10,11... | collective-permute-start | bytes 3145736 | tf_op jit(solution)/shard_map/ppermute | solution.py:327
  102.9 5.1 %convolution_convert_fusion.q_ref = bf16[1024,1536]{1,0:T(8,128)(2,1)} fusion(bf16[1024,512]{1,0:T(8,128)(2,1)} %bitcast.102, bf16[512,512]{1,0:T(8,128)(2,1)} %copy.79, bf16[512,512]{1,0:T(8,128)(2,1)} %copy.78, bf16[512,512]{1,0:T(8,128)(2,1)} %copy.77), kind=kOutput, calls=%fused_computation.4 | convolution fusion | flops 1616904192 | bytes 5767168 | tf_op jit(solution)/shard_map/dot_general | solution.py:404
  108.0 5.9 %far_forward.1 = (bf16[8,512,128]{2,1,0:T(8,128)(2,1)}, f32[8,24,128]{2,1,0:T(8,128)}) custom-call(bf16[2048,1536]{1,0:T(8,128)(2,1)} %project_peer.1.q_ref, bf16[8,512,128]{2,1,0:T(8,128)(2,1)} %fusion.21.cot_t_ref, bf16[8,128,1536]{2,1,0:T(8,128)(2,1)} %bitcast.79, bf16[8,128,1536]{2,1,0:T(8,128)(2,1)} %bitcast.80, ...), custom_call_target="tpu_custom_call" | custom-call | flops 1073741824 | bytes 6291456 | tf_op jit(solution)/shard_map/far_forward/pallas_call | solution.py:414
  114.6 25.8 %own_backward.1 = (bf16[8,512,128]{2,1,0:T(8,128)(2,1)}, f32[8,128,1024]{2,1,0:T(8,128)}, f32[2,32,8,512]{3,2,1,0:T(8,128)}, f32[2,32,8,512]{3,2,1,0:T(8,128)}, f32[128,24,128]{2,1,0:T(8,128)}) custom-call(s32[16,4]{1,0:T(8,128)} %copy.80.near_ids, s32[10]{0:T(128)} %pad_add_fusion.1.meta, bf16[2048,1536]{1,0:T(8,128)(2,1)} %project_peer.1.q_ref, ...), custom_call_target="tpu_custom_call" | custom-call | flops 6442450944 | bytes 31457280 | tf_op jit(solution)/shard_map/own_backward/pallas_call | solution.py:427
  140.4 10.1 %all-to-all-start.3 = ((f32[128,24,128]{2,1,0:T(8,128)}), f32[128,24,128]{2,1,0:T(8,128)}, u32[]{:S(2)}, u32[]{:S(2)}) async-start(f32[128,24,128]{2,1,0:T(8,128)} %get-tuple-element.55), calls=%async_computation.3 | async-start | bytes 3145728 | tf_op jit(solution)/shard_map/all_to_all | solution.py:330
  150.7 17.3 %peer_queries.1.acc_ref = f32[8,128,1024]{2,1,0:T(8,128)} custom-call(s32[16,4]{1,0:T(8,128)} %copy.80.near_ids, s32[10]{0:T(128)} %pad_add_fusion.1.meta, bf16[2048,1536]{1,0:T(8,128)(2,1)} %project_peer.1.q_ref, bf16[1024,512]{1,0:T(8,128)(2,1)} %collective-permute-done.2.cot_ref, f32[8,24,128]{2,1,0:T(8,128)} %copy-done.11, s32[16,4,128,128]{3,2,1,0:T(8,128)} %tile_ref.5, ...), custom_call_target="tpu_custom_call" | custom-call | flops 4294967296 | bytes 20971520 | tf_op jit(solution)/shard_map/peer_queries/pallas_call | solution.py:462
  168.0 2.5 %copy.73 = bf16[8,128,512]{2,1,0:T(8,128)(2,1)} copy(bf16[8,128,512]{2,0,1:T(8,128)(2,1)} %bitcast.34) | data formatting | bytes 2097152 | tf_op jit(solution)/shard_map/transpose | solution.py:453
  170.5 3.9 %all-to-all-done.3.first_ref.second_ref = f32[128,24,128]{2,1,0:T(8,128)} async-done(((f32[128,24,128]{2,1,0:T(8,128)}), f32[128,24,128]{2,1,0:T(8,128)}, u32[]{:S(2)}, u32[]{:S(2)}) %all-to-all-start.3) | async-done | bytes 1572896 | tf_op jit(solution)/shard_map/all_to_all | solution.py:330
  174.4 9.5 %far_queries.1 = (bf16[1024,1024]{1,0:T(8,128)(2,1)}, f32[2,32,8,512]{3,2,1,0:T(8,128)}, f32[2,32,8,512]{3,2,1,0:T(8,128)}) custom-call(s32[10]{0:T(128)} %pad_add_fusion.1.meta, bf16[1024,1536]{1,0:T(8,128)(2,1)} %convolution_convert_fusion.q_ref, bf16[1024,512]{1,0:T(8,128)(2,1)} %bitcast.91, f32[128,24,128]{2,1,0:T(8,128)} %all-to-all-done.3.first_ref.second_ref, ...), custom_call_target="tpu_custom_call" | custom-call | flops 2147483648 | bytes 10485760 | tf_op jit(solution)/shard_map/far_queries/pallas_call | solution.py:482
  188.3 7.2 %all-to-all-start.4 = ((bf16[64,16,512]{2,1,0:T(8,128)(2,1)}), bf16[64,16,512]{2,1,0:T(8,128)(2,1)S(1)}, u32[]{:S(2)}, u32[]{:S(2)}) async-start(bf16[64,16,512]{2,1,0:T(8,128)(2,1)} %bitcast.92), calls=%async_computation.4 | async-start | bytes 2097152 | tf_op jit(solution)/shard_map/all_to_all | solution.py:501
  195.5 1.7 convolution_convert_fusion.1
  198.8 2.2 %fusion.4 = bf16[1024,512]{1,0:T(8,128)(2,1)} fusion(f32[8,128,512]{2,1,0:T(8,128)S(1)} %fusion.27, bf16[1024,1024]{1,0:T(8,128)(2,1)S(1)} %copy-done.14, bf16[512,1536]{0,1:T(8,128)(2,1)S(1)} %bitcast.95), kind=kOutput, calls=%fused_computation.7 | convolution fusion | flops 1074790400 | bytes 6291456 | tf_op jit(solution)/shard_map/dot_general | solution.py:506
  201.0 13.6 %all-to-all-done.4 = bf16[64,16,512]{2,1,0:T(8,128)(2,1)S(1)} async-done(((bf16[64,16,512]{2,1,0:T(8,128)(2,1)}), bf16[64,16,512]{2,1,0:T(8,128)(2,1)S(1)}, u32[]{:S(2)}, u32[]{:S(2)}) %all-to-all-start.4) | async-done | bytes 1048608 | tf_op jit(solution)/shard_map/all_to_all | solution.py:501
  (69 shorter events, 22.3 us)
Async XLA Ops:
  0.6 23.4 %copy-start = (bf16[512,512]{1,0:T(8,128)(2,1)S(1)}, bf16[512,512]{1,0:T(8,128)(2,1)}, u32[]{:S(2)}) copy-start(bf16[512,512]{1,0:T(8,128)(2,1)} %param.10) | copy-start | bytes 1572868
  0.6 41.3 %collective-permute-start = (bf16[1024,512]{1,0:T(8,128)(2,1)}, bf16[1024,512]{1,0:T(8,128)(2,1)}, u32[]{:S(2)}, u32[]{:S(2)}) collective-permute-start(bf16[1024,512]{1,0:T(8,128)(2,1)} %x_ref.1), channel_id=1, source_target_pairs={{0,1},{1,0},{2,3},{3,2},{4,5},{5,4},{6,7},{7,6},{8,9},{9,8},{10,11... | collective-permute-start | bytes 3145736 | tf_op jit(solution)/shard_map/ppermute | solution.py:327
  8.8 34.5 %all-to-all-start = ((bf16[128,8,640]{2,1,0:T(8,128)(2,1)}), bf16[128,8,640]{2,1,0:T(8,128)(2,1)}, u32[]{:S(2)}, u32[]{:S(2)}) async-start(bf16[128,8,640]{2,1,0:T(8,128)(2,1)} %copy.58), calls=%async_computation | async-start | bytes 2621440 | tf_op jit(solution)/shard_map/all_to_all | solution.py:330
  26.0 1.0 copy-start.2
  27.0 3.8 %copy-start.1 = (bf16[1024,512]{1,0:T(8,128)(2,1)S(1)}, bf16[1024,512]{1,0:T(8,128)(2,1)}, u32[]{:S(2)}) copy-start(bf16[1024,512]{1,0:T(8,128)(2,1)} %x_ref.1) | copy-start | bytes 3145732
  34.7 5.4 %copy-start.8 = (bf16[1024,512]{1,0:T(8,128)(2,1)S(1)}, bf16[1024,512]{1,0:T(8,128)(2,1)}, u32[]{:S(2)}) copy-start(bf16[1024,512]{1,0:T(8,128)(2,1)} %param.14) | copy-start | bytes 3145732
  40.1 3.2 %copy-start.13 = (f32[128]{0:T(128)S(1)}, f32[128]{0:T(128)}, u32[]{:S(2)}) copy-start(f32[128]{0:T(128)} %constant.107) | copy-start | bytes 1540
  44.5 2.6 %copy-start.5 = (bf16[8,128,512]{2,0,1:T(8,128)(2,1)S(1)}, bf16[8,128,512]{2,0,1:T(8,128)(2,1)}, u32[]{:S(2)}) copy-start(bf16[8,128,512]{2,0,1:T(8,128)(2,1)} %copy.84) | copy-start | bytes 3145732
  48.7 10.1 %copy-start.12 = (s32[16,4]{0,1:T(4,128)S(1)}, s32[16,4]{0,1:T(4,128)}, u32[]{:S(2)}) copy-start(s32[16,4]{0,1:T(4,128)} %param.11) | copy-start | bytes 772
  48.7 39.2 %all-to-all-start.1 = ((bf16[128,8,1024]{2,1,0:T(8,128)(2,1)}), bf16[128,8,1024]{2,1,0:T(8,128)(2,1)}, u32[]{:S(2)}, u32[]{:S(2)}) async-start(bf16[128,8,1024]{2,1,0:T(8,128)(2,1)} %pad_maximum_fusion), calls=%async_computation.1 | async-start | bytes 4194304 | tf_op jit(solution)/shard_map/all_to_all | solution.py:330
  92.8 7.1 %copy-start.3 = (bf16[1024,512]{1,0:T(8,128)(2,1)S(1)}, bf16[1024,512]{1,0:T(8,128)(2,1)}, u32[]{:S(2)}) copy-start(bf16[1024,512]{1,0:T(8,128)(2,1)} %copy-done.2) | copy-start | bytes 3145732
  94.1 46.4 %all-to-all-start.2 = ((bf16[128,8,512]{2,1,0:T(8,128)(2,1)}), bf16[128,8,512]{2,1,0:T(8,128)(2,1)}, u32[]{:S(2)}, u32[]{:S(2)}) async-start(bf16[128,8,512]{2,1,0:T(8,128)(2,1)} %fusion.15), calls=%async_computation.2 | async-start | bytes 2097152 | tf_op jit(solution)/shard_map/all_to_all | solution.py:330
  99.9 40.6 %collective-permute-start.2 = (bf16[1024,512]{1,0:T(8,128)(2,1)S(1)}, bf16[1024,512]{1,0:T(8,128)(2,1)}, u32[]{:S(2)}, u32[]{:S(2)}) collective-permute-start(bf16[1024,512]{1,0:T(8,128)(2,1)S(1)} %copy-done.3), channel_id=1, source_target_pairs={{0,1},{1,0},{2,3},{3,2},{4,5},{5,4},{6,7},{7,6},{8,9},{9,8},{10,11... | collective-permute-start | bytes 3145736 | tf_op jit(solution)/shard_map/ppermute | solution.py:327
  113.9 26.5 %collective-permute-start.1 = (f32[8,24,128]{2,1,0:T(8,128)}, f32[8,24,128]{2,1,0:T(8,128)S(1)}, u32[]{:S(2)}, u32[]{:S(2)}) collective-permute-start(f32[8,24,128]{2,1,0:T(8,128)} %get-tuple-element.46.stats_ref), channel_id=1, source_target_pairs={{0,1},{1,0},{2,3},{3,2},{4,5},{5,4},{6,7},{7,6},{8,9},{9,8},{10,11... | collective-permute-start | bytes 294920 | tf_op jit(solution)/shard_map/ppermute | solution.py:327
  140.4 10.3 %copy-start.11 = (f32[8,24,128]{2,1,0:T(8,128)}, f32[8,24,128]{2,1,0:T(8,128)S(1)}, u32[]{:S(2)}) copy-start(f32[8,24,128]{2,1,0:T(8,128)S(1)} %collective-permute-done.1.stats_ref) | copy-start | bytes 294916
  140.4 33.9 %all-to-all-start.3 = ((f32[128,24,128]{2,1,0:T(8,128)}), f32[128,24,128]{2,1,0:T(8,128)}, u32[]{:S(2)}, u32[]{:S(2)}) async-start(f32[128,24,128]{2,1,0:T(8,128)} %get-tuple-element.55), calls=%async_computation.3 | async-start | bytes 3145728 | tf_op jit(solution)/shard_map/all_to_all | solution.py:330
  150.6 34.8 %collective-permute-start.3 = (f32[2,32,8,512]{3,2,1,0:T(8,128)}, f32[2,32,8,512]{3,2,1,0:T(8,128)S(1)}, u32[]{:S(2)}, u32[]{:S(2)}) collective-permute-start(f32[2,32,8,512]{3,2,1,0:T(8,128)} %get-tuple-element.61), channel_id=1, source_target_pairs={{0,2},{2,0},{4,6},{6,4},{8,10},{10,8},{12,14},{14,12},{16,18},{18,... | collective-permute-start | bytes 3145736 | tf_op jit(solution)/shard_map/ppermute | solution.py:458
  183.9 1.5 copy-start.9
  183.9 3.0 %collective-permute-start.4 = (f32[2,32,8,512]{3,2,1,0:T(8,128)}, f32[2,32,8,512]{3,2,1,0:T(8,128)S(1)}, u32[]{:S(2)}, u32[]{:S(2)}) collective-permute-start(f32[2,32,8,512]{3,2,1,0:T(8,128)} %get-tuple-element.63), channel_id=1, source_target_pairs={{0,2},{2,0},{4,6},{6,4},{8,10},{10,8},{12,14},{14,12},{16,18},{18,... | collective-permute-start | bytes 3145736 | tf_op jit(solution)/shard_map/ppermute | solution.py:458
  185.4 1.5 copy-start.10
  187.1 8.3 %copy-start.4 = (bf16[8,512,128]{2,1,0:T(8,128)(2,1)S(1)}, bf16[8,512,128]{2,1,0:T(8,128)(2,1)}, u32[]{:S(2)}) copy-start(bf16[8,512,128]{2,1,0:T(8,128)(2,1)} %get-tuple-element.45.att_ref) | copy-start | bytes 3145732
  188.3 26.3 %all-to-all-start.4 = ((bf16[64,16,512]{2,1,0:T(8,128)(2,1)}), bf16[64,16,512]{2,1,0:T(8,128)(2,1)S(1)}, u32[]{:S(2)}, u32[]{:S(2)}) async-start(bf16[64,16,512]{2,1,0:T(8,128)(2,1)} %bitcast.92), calls=%async_computation.4 | async-start | bytes 2097152 | tf_op jit(solution)/shard_map/all_to_all | solution.py:501
  195.5 1.7 copy-start.6
  195.5 1.7 copy-start.7
  197.2 1.6 copy-start.14

commit v10 on v9

--- a/solution.py
+++ b/solution.py
@@ -399,7 +399,6 @@
 
     picked = gathered(second[:, :, width:])
     far_feats = second[:, :, :width].transpose(1, 0, 2).reshape(rows, width)
-    picked, far_feats = lax.optimization_barrier((picked, far_feats))
     far_cot = exchange(picked)
     far_qkv = jnp.dot(far_feats, w_all, preferred_element_type=F32).astype(BF16)
     far_blk = far_qkv.reshape(own, bs, 3 * width)

time: 218 us -> 220 us (level)
  starting transfers between devices: 49.7 us -> 53.2 us
    optimization_barrier x0 -> x1, local copies, waits for them, and re-layouts: none -> 2.74 us  [body(): lax.optimization_barrier((second, near_out, sums, cot))]
    all_to_all x1, starting transfers between devices: 7.17 us -> 9.74 us  [body(): lax.all_to_all(split, DEVICES, split_axis=0, concat_axis=0, axis_index_gr...]
    transpose x2 -> x0, local copies, waits for them, and re-layouts: 2.57 us -> none  [body(): far_feats = second[:, :, :width].transpose(1, 0, 2).reshape(rows, width)]
    pallas_call x1, Pallas kernels: 25.8 us -> 23.5 us  [body(): call(own_kernel, 2, own, [rows_spec, rows_spec, tile_spec, stats_spec, k_...]
  transfers between devices with their start and end apart: 10 -> 10, of which waited for: 6 -> 7; matrix products, arithmetic and copies ran while one was open for 17% -> 17% of each run, Pallas kernels for 38% -> 37%
where the time goes in v10:
time: 220 us
  Pallas kernels  81.5 us (37%)
  starting transfers between devices  53.2 us (24%)
  waiting for transfers between devices  29.6 us (13%)
  local copies, waits for them, and re-layouts  22.8 us (10%)
  matrix products  20 us (9%)
  other arithmetic  11.5 us (5%)
    all_to_all x4, starting transfers between devices, exchange(): return lax.all_to_all(x, DEVICES, split_axis=0, concat_axis=0, tiled=True)  35.7 us
    pallas_call x1, Pallas kernels, body(): call(own_kernel, 2, own, [rows_spec, rows_spec, tile_spec, stats_spec, k_...  23.5 us
    pallas_call x1, Pallas kernels, body(): call(peer_kernel, 2, own, [pl.BlockSpec((bs, width), lambda i, *s: (own +...  19.1 us
    all_to_all x1, waiting for transfers between devices, body(): lax.all_to_all(split, DEVICES, split_axis=0, concat_axis=0, axis_index_gr...  13.6 us
    all_to_all x4, waiting for transfers between devices, exchange(): return lax.all_to_all(x, DEVICES, split_axis=0, concat_axis=0, tiled=True)  12.9 us
    pallas_call x1, Pallas kernels, body(): call(near_kernel, 2, own, [rows_spec, tile_spec, k_spec, v_spec], [pl.Blo...  12.8 us
    pallas_call x2, Pallas kernels, project(): call(project_kernel, 0, 3, [once((rows, width)), pl.BlockSpec((width, wid...  10.8 us
    all_to_all x1, starting transfers between devices, body(): lax.all_to_all(split, DEVICES, split_axis=0, concat_axis=0, axis_index_gr...  9.74 us
  transfers between devices with their start and end apart: 10, of which 7 were waited for; matrix products, arithmetic and copies ran while one was open for 17% of the time, Pallas kernels for 37%

profile of v10, /device:TPU:0, one launch (start us, length us, event | category | flops | bytes accessed | tf_op | source)
XLA Modules:
  0.0 219.6 jit_solution(2354387372738720745)
XLA Ops:
  0.6 4.0 %collective-permute-start = (bf16[1024,512]{1,0:T(8,128)(2,1)}, bf16[1024,512]{1,0:T(8,128)(2,1)}, u32[]{:S(2)}, u32[]{:S(2)}) collective-permute-start(bf16[1024,512]{1,0:T(8,128)(2,1)} %x_ref.1), channel_id=1, source_target_pairs={{0,1},{1,0},{2,3},{3,2},{4,5},{5,4},{6,7},{7,6},{8,9},{9,8},{10,11... | collective-permute-start | bytes 3145736 | tf_op jit(solution)/shard_map/ppermute | solution.py:327
  6.9 1.8 copy.58
  8.8 8.5 %all-to-all-start = ((bf16[128,8,640]{2,1,0:T(8,128)(2,1)}), bf16[128,8,640]{2,1,0:T(8,128)(2,1)}, u32[]{:S(2)}, u32[]{:S(2)}) async-start(bf16[128,8,640]{2,1,0:T(8,128)(2,1)} %copy.58), calls=%async_computation | async-start | bytes 2621440 | tf_op jit(solution)/shard_map/all_to_all | solution.py:330
  17.3 1.7 copy.60
  19.9 2.1 copy.77
  24.0 2.0 convolution_convert_fusion.3.cot_ref
  28.5 2.3 %copy.66 = bf16[8,128,512]{1,2,0:T(8,128)(2,1)} copy(bf16[8,128,512]{2,1,0:T(8,128)(2,1)} %bitcast.100) | data formatting | bytes 2097152 | tf_op jit(solution)/shard_map/reshape | solution.py:348
  32.1 2.6 %pad_maximum_fusion.1.w_ref = bf16[512,1536]{1,0:T(8,128)(2,1)} fusion(bf16[512,512]{1,0:T(8,128)(2,1)} %copy.79, bf16[512,512]{1,0:T(8,128)(2,1)} %copy.78, bf16[512,512]{1,0:T(8,128)(2,1)} %copy.77), kind=kLoop, calls=%fused_computation.13 | loop fusion | flops 4718592 | bytes 3145728 | tf_op jit(solution)/shard_map/concatenate | solution.py:324
  34.7 5.4 %project_own.1.rest_0_ = bf16[2048,1536]{1,0:T(8,128)(2,1)} custom-call(bf16[1024,512]{1,0:T(8,128)(2,1)} %x_ref.1, bf16[512,1536]{1,0:T(8,128)(2,1)} %pad_maximum_fusion.1.w_ref), custom_call_target="tpu_custom_call" | custom-call | flops 1610612736 | bytes 6291456 | tf_op jit(solution)/shard_map/project_own/pallas_call | solution.py:353
  40.1 1.7 fusion.21.cot_t_ref
  44.5 2.6 %fusion.18 = bf16[128,8,512]{2,1,0:T(8,128)(2,1)S(1)} fusion(f32[1024]{0:T(1024)S(1)} %iota_convert_fusion, f32[1024]{0:T(1024)S(1)} %multiply_reduce_fusion, bf16[128,8,640]{2,1,0:T(8,128)(2,1)} %all-to-all-done), kind=kOutput, calls=%fused_computation.20 | convolution fusion | flops 1075314688 | bytes 2105344 | tf_op jit(solution)/shard_map/dot_general | solution.py:336
  48.7 10.1 %all-to-all-start.1 = ((bf16[128,8,1024]{2,1,0:T(8,128)(2,1)}), bf16[128,8,1024]{2,1,0:T(8,128)(2,1)}, u32[]{:S(2)}, u32[]{:S(2)}) async-start(bf16[128,8,1024]{2,1,0:T(8,128)(2,1)} %pad_maximum_fusion), calls=%async_computation.1 | async-start | bytes 4194304 | tf_op jit(solution)/shard_map/all_to_all | solution.py:330
  60.3 5.4 %project_peer.1.q_ref = bf16[2048,1536]{1,0:T(8,128)(2,1)} custom-call(bf16[1024,512]{1,0:T(8,128)(2,1)} %collective-permute-done.x_ref, bf16[512,1536]{1,0:T(8,128)(2,1)} %pad_maximum_fusion.1.w_ref, bf16[2048,1536]{1,0:T(8,128)(2,1)} %project_own.1.rest_0_), custom_call_target="tpu_custom_call", output_to_operand_aliasing={{}: (2, {})} | custom-call | flops 1610612736 | bytes 6291456 | tf_op jit(solution)/shard_map/project_peer/pallas_call | solution.py:353
  65.7 12.8 %near_forward.1 = (f32[8,512,128]{2,1,0:T(8,128)}, f32[8,16,128]{2,1,0:T(8,128)}) custom-call(s32[16,4]{1,0:T(8,128)} %copy.80.near_ids, s32[10]{0:T(128)} %pad_add_fusion.1.meta, bf16[2048,1536]{1,0:T(8,128)(2,1)} %project_peer.1.q_ref, s32[16,4,128,128]{3,2,1,0:T(8,128)} %tile_ref.5, bf16[16,128,1536]{2,1,0:T(8,128)(2,1)} %bitcast.71, ...), custom_call_target="tpu_custom_call" | custom-call | flops 4294967296 | bytes 10485760 | tf_op jit(solution)/shard_map/near_forward/pallas_call | solution.py:390
  78.5 9.4 %all-to-all-done.1 = bf16[128,8,1024]{2,1,0:T(8,128)(2,1)} async-done(((bf16[128,8,1024]{2,1,0:T(8,128)(2,1)}), bf16[128,8,1024]{2,1,0:T(8,128)(2,1)}, u32[]{:S(2)}, u32[]{:S(2)}) %all-to-all-start.1) | async-done | bytes 2097184 | tf_op jit(solution)/shard_map/all_to_all | solution.py:330
  88.0 2.7 %copy.68 = bf16[128,8,1024]{2,0,1:T(8,128)(2,1)S(1)} copy(bf16[128,8,1024]{2,1,0:T(8,128)(2,1)} %all-to-all-done.1) | data formatting | bytes 4194304 | tf_op jit(solution)/shard_map/optimization_barrier | solution.py:398
  90.7 4.3 %fusion.15 = bf16[128,8,512]{2,1,0:T(8,128)(2,1)} fusion(f32[1024]{0:T(1024)S(1)} %iota_convert_fusion, f32[1024]{0:T(1024)S(1)} %multiply_reduce_fusion, bf16[128,8,1024]{2,1,0:T(8,128)(2,1)} %all-to-all-done.1), kind=kOutput, calls=%fused_computation.19 | convolution fusion | flops 1075314688 | bytes 2105344 | tf_op jit(solution)/shard_map/dot_general | solution.py:336
  95.0 6.1 %all-to-all-start.2 = ((bf16[128,8,512]{2,1,0:T(8,128)(2,1)}), bf16[128,8,512]{2,1,0:T(8,128)(2,1)}, u32[]{:S(2)}, u32[]{:S(2)}) async-start(bf16[128,8,512]{2,1,0:T(8,128)(2,1)} %fusion.15), calls=%async_computation.2 | async-start | bytes 2097152 | tf_op jit(solution)/shard_map/all_to_all | solution.py:330
  101.1 2.9 %collective-permute-start.2 = (bf16[1024,512]{1,0:T(8,128)(2,1)}, bf16[1024,512]{1,0:T(8,128)(2,1)}, u32[]{:S(2)}, u32[]{:S(2)}) collective-permute-start(bf16[1024,512]{1,0:T(8,128)(2,1)} %copy-done.3), channel_id=1, source_target_pairs={{0,1},{1,0},{2,3},{3,2},{4,5},{5,4},{6,7},{7,6},{8,9},{9,8},{10,11... | collective-permute-start | bytes 3145736 | tf_op jit(solution)/shard_map/ppermute | solution.py:327
  103.9 4.8 %convolution_convert_fusion.q_ref = bf16[1024,1536]{1,0:T(8,128)(2,1)} fusion(bf16[1024,512]{1,0:T(8,128)(2,1)S(1)} %bitcast.89, bf16[512,512]{1,0:T(8,128)(2,1)} %copy.79, bf16[512,512]{1,0:T(8,128)(2,1)} %copy.78, bf16[512,512]{1,0:T(8,128)(2,1)} %copy.77), kind=kOutput, calls=%fused_computation.4 | convolution fusion | flops 1616904192 | bytes 5767168 | tf_op jit(solution)/shard_map/dot_general | solution.py:403
  108.7 5.9 %far_forward.1 = (bf16[8,512,128]{2,1,0:T(8,128)(2,1)}, f32[8,24,128]{2,1,0:T(8,128)}) custom-call(bf16[2048,1536]{1,0:T(8,128)(2,1)} %project_peer.1.q_ref, bf16[8,512,128]{2,1,0:T(8,128)(2,1)} %fusion.21.cot_t_ref, bf16[8,128,1536]{2,1,0:T(8,128)(2,1)} %bitcast.79, bf16[8,128,1536]{2,1,0:T(8,128)(2,1)} %bitcast.80, ...), custom_call_target="tpu_custom_call" | custom-call | flops 1073741824 | bytes 6291456 | tf_op jit(solution)/shard_map/far_forward/pallas_call | solution.py:413
  115.3 23.5 %own_backward.1 = (bf16[8,512,128]{2,1,0:T(8,128)(2,1)}, f32[8,128,1024]{2,1,0:T(8,128)}, f32[2,32,8,512]{3,2,1,0:T(8,128)}, f32[2,32,8,512]{3,2,1,0:T(8,128)}, f32[128,24,128]{2,1,0:T(8,128)}) custom-call(s32[16,4]{1,0:T(8,128)} %copy.80.near_ids, s32[10]{0:T(128)} %pad_add_fusion.1.meta, bf16[2048,1536]{1,0:T(8,128)(2,1)} %project_peer.1.q_ref, ...), custom_call_target="tpu_custom_call" | custom-call | flops 6442450944 | bytes 31457280 | tf_op jit(solution)/shard_map/own_backward/pallas_call | solution.py:426
  138.8 1.8 collective-permute-done.1.stats_ref
  140.7 11.0 %all-to-all-start.3 = ((f32[128,24,128]{2,1,0:T(8,128)}), f32[128,24,128]{2,1,0:T(8,128)}, u32[]{:S(2)}, u32[]{:S(2)}) async-start(f32[128,24,128]{2,1,0:T(8,128)} %get-tuple-element.51), calls=%async_computation.3 | async-start | bytes 3145728 | tf_op jit(solution)/shard_map/all_to_all | solution.py:330
  151.8 19.1 %peer_queries.1.acc_ref = f32[8,128,1024]{2,1,0:T(8,128)} custom-call(s32[16,4]{1,0:T(8,128)} %copy.80.near_ids, s32[10]{0:T(128)} %pad_add_fusion.1.meta, bf16[2048,1536]{1,0:T(8,128)(2,1)} %project_peer.1.q_ref, bf16[1024,512]{1,0:T(8,128)(2,1)} %collective-permute-done.2.cot_ref, f32[8,24,128]{2,1,0:T(8,128)} %copy-done.11, s32[16,4,128,128]{3,2,1,0:T(8,128)} %tile_ref.5, ...), custom_call_target="tpu_custom_call" | custom-call | flops 4294967296 | bytes 20971520 | tf_op jit(solution)/shard_map/peer_queries/pallas_call | solution.py:461
  170.8 2.5 %copy.73 = bf16[8,128,512]{2,1,0:T(8,128)(2,1)} copy(bf16[8,128,512]{2,0,1:T(8,128)(2,1)} %bitcast.34) | data formatting | bytes 2097152 | tf_op jit(solution)/shard_map/transpose | solution.py:452
  173.3 2.1 all-to-all-done.3.first_ref.second_ref
  175.5 9.5 %far_queries.1 = (bf16[1024,1024]{1,0:T(8,128)(2,1)}, f32[2,32,8,512]{3,2,1,0:T(8,128)}, f32[2,32,8,512]{3,2,1,0:T(8,128)}) custom-call(s32[10]{0:T(128)} %pad_add_fusion.1.meta, bf16[1024,1536]{1,0:T(8,128)(2,1)} %convolution_convert_fusion.q_ref, bf16[1024,512]{1,0:T(8,128)(2,1)} %bitcast.92, f32[128,24,128]{2,1,0:T(8,128)} %all-to-all-done.3.first_ref.second_ref, ...), custom_call_target="tpu_custom_call" | custom-call | flops 2147483648 | bytes 10485760 | tf_op jit(solution)/shard_map/far_queries/pallas_call | solution.py:481
  189.4 9.7 %all-to-all-start.4 = ((bf16[64,16,512]{2,1,0:T(8,128)(2,1)}), bf16[64,16,512]{2,1,0:T(8,128)(2,1)S(1)}, u32[]{:S(2)}, u32[]{:S(2)}) async-start(bf16[64,16,512]{2,1,0:T(8,128)(2,1)} %bitcast.93), calls=%async_computation.4 | async-start | bytes 2097152 | tf_op jit(solution)/shard_map/all_to_all | solution.py:500
  199.2 1.7 convolution_convert_fusion.1
  202.5 2.2 %fusion.4 = bf16[1024,512]{1,0:T(8,128)(2,1)} fusion(f32[8,128,512]{2,1,0:T(8,128)S(1)} %fusion.27, bf16[1024,1024]{1,0:T(8,128)(2,1)S(1)} %copy-done.14, bf16[512,1536]{0,1:T(8,128)(2,1)S(1)} %bitcast.96), kind=kOutput, calls=%fused_computation.7 | convolution fusion | flops 1074790400 | bytes 6291456 | tf_op jit(solution)/shard_map/dot_general | solution.py:505
  204.7 13.6 %all-to-all-done.4 = bf16[64,16,512]{2,1,0:T(8,128)(2,1)S(1)} async-done(((bf16[64,16,512]{2,1,0:T(8,128)(2,1)}), bf16[64,16,512]{2,1,0:T(8,128)(2,1)S(1)}, u32[]{:S(2)}, u32[]{:S(2)}) %all-to-all-start.4) | async-done | bytes 1048608 | tf_op jit(solution)/shard_map/all_to_all | solution.py:500
  (70 shorter events, 22.9 us)
Async XLA Ops:
  0.6 23.4 %copy-start = (bf16[512,512]{1,0:T(8,128)(2,1)S(1)}, bf16[512,512]{1,0:T(8,128)(2,1)}, u32[]{:S(2)}) copy-start(bf16[512,512]{1,0:T(8,128)(2,1)} %param.10) | copy-start | bytes 1572868
  0.6 41.3 %collective-permute-start = (bf16[1024,512]{1,0:T(8,128)(2,1)}, bf16[1024,512]{1,0:T(8,128)(2,1)}, u32[]{:S(2)}, u32[]{:S(2)}) collective-permute-start(bf16[1024,512]{1,0:T(8,128)(2,1)} %x_ref.1), channel_id=1, source_target_pairs={{0,1},{1,0},{2,3},{3,2},{4,5},{5,4},{6,7},{7,6},{8,9},{9,8},{10,11... | collective-permute-start | bytes 3145736 | tf_op jit(solution)/shard_map/ppermute | solution.py:327
  8.8 34.5 %all-to-all-start = ((bf16[128,8,640]{2,1,0:T(8,128)(2,1)}), bf16[128,8,640]{2,1,0:T(8,128)(2,1)}, u32[]{:S(2)}, u32[]{:S(2)}) async-start(bf16[128,8,640]{2,1,0:T(8,128)(2,1)} %copy.58), calls=%async_computation | async-start | bytes 2621440 | tf_op jit(solution)/shard_map/all_to_all | solution.py:330
  26.0 1.0 copy-start.3
  27.0 3.8 %copy-start.1 = (bf16[1024,512]{1,0:T(8,128)(2,1)S(1)}, bf16[1024,512]{1,0:T(8,128)(2,1)}, u32[]{:S(2)}) copy-start(bf16[1024,512]{1,0:T(8,128)(2,1)} %x_ref.1) | copy-start | bytes 3145732
  34.7 5.4 %copy-start.8 = (bf16[1024,512]{1,0:T(8,128)(2,1)S(1)}, bf16[1024,512]{1,0:T(8,128)(2,1)}, u32[]{:S(2)}) copy-start(bf16[1024,512]{1,0:T(8,128)(2,1)} %param.14) | copy-start | bytes 3145732
  40.1 3.2 %copy-start.13 = (f32[128]{0:T(128)S(1)}, f32[128]{0:T(128)}, u32[]{:S(2)}) copy-start(f32[128]{0:T(128)} %constant.107) | copy-start | bytes 1540
  44.5 2.6 %copy-start.5 = (bf16[8,128,512]{2,0,1:T(8,128)(2,1)S(1)}, bf16[8,128,512]{2,0,1:T(8,128)(2,1)}, u32[]{:S(2)}) copy-start(bf16[8,128,512]{2,0,1:T(8,128)(2,1)} %copy.84) | copy-start | bytes 3145732
  48.7 10.1 %copy-start.12 = (s32[16,4]{0,1:T(4,128)S(1)}, s32[16,4]{0,1:T(4,128)}, u32[]{:S(2)}) copy-start(s32[16,4]{0,1:T(4,128)} %param.11) | copy-start | bytes 772
  48.7 39.2 %all-to-all-start.1 = ((bf16[128,8,1024]{2,1,0:T(8,128)(2,1)}), bf16[128,8,1024]{2,1,0:T(8,128)(2,1)}, u32[]{:S(2)}, u32[]{:S(2)}) async-start(bf16[128,8,1024]{2,1,0:T(8,128)(2,1)} %pad_maximum_fusion), calls=%async_computation.1 | async-start | bytes 4194304 | tf_op jit(solution)/shard_map/all_to_all | solution.py:330
  90.7 4.3 %copy-start.2 = (bf16[128,8,1024]{2,0,1:T(8,128)(2,1)}, bf16[128,8,1024]{2,0,1:T(8,128)(2,1)S(1)}, u32[]{:S(2)}) copy-start(bf16[128,8,1024]{2,0,1:T(8,128)(2,1)S(1)} %copy.68) | copy-start | bytes 6291460
  95.0 8.9 %slice-start = ((bf16[128,8,1024]{2,0,1:T(8,128)(2,1)}), bf16[128,8,512]{2,0,1:T(8,128)(2,1)S(1)}, s32[]{:S(2)}) async-start(bf16[128,8,1024]{2,0,1:T(8,128)(2,1)} %copy-done.2), calls=%async_computation.5 | async-start | bytes 2097152 | tf_op jit(solution)/shard_map/slice | solution.py:401
  95.0 45.7 %all-to-all-start.2 = ((bf16[128,8,512]{2,1,0:T(8,128)(2,1)}), bf16[128,8,512]{2,1,0:T(8,128)(2,1)}, u32[]{:S(2)}, u32[]{:S(2)}) async-start(bf16[128,8,512]{2,1,0:T(8,128)(2,1)} %fusion.15), calls=%async_computation.2 | async-start | bytes 2097152 | tf_op jit(solution)/shard_map/all_to_all | solution.py:330
  101.1 39.6 %collective-permute-start.2 = (bf16[1024,512]{1,0:T(8,128)(2,1)}, bf16[1024,512]{1,0:T(8,128)(2,1)}, u32[]{:S(2)}, u32[]{:S(2)}) collective-permute-start(bf16[1024,512]{1,0:T(8,128)(2,1)} %copy-done.3), channel_id=1, source_target_pairs={{0,1},{1,0},{2,3},{3,2},{4,5},{5,4},{6,7},{7,6},{8,9},{9,8},{10,11... | collective-permute-start | bytes 3145736 | tf_op jit(solution)/shard_map/ppermute | solution.py:327
  114.6 26.1 %collective-permute-start.1 = (f32[8,24,128]{2,1,0:T(8,128)}, f32[8,24,128]{2,1,0:T(8,128)S(1)}, u32[]{:S(2)}, u32[]{:S(2)}) collective-permute-start(f32[8,24,128]{2,1,0:T(8,128)} %get-tuple-element.43.stats_ref), channel_id=1, source_target_pairs={{0,1},{1,0},{2,3},{3,2},{4,5},{5,4},{6,7},{7,6},{8,9},{9,8},{10,11... | collective-permute-start | bytes 294920 | tf_op jit(solution)/shard_map/ppermute | solution.py:327
  140.7 11.1 %copy-start.11 = (f32[8,24,128]{2,1,0:T(8,128)}, f32[8,24,128]{2,1,0:T(8,128)S(1)}, u32[]{:S(2)}) copy-start(f32[8,24,128]{2,1,0:T(8,128)S(1)} %collective-permute-done.1.stats_ref) | copy-start | bytes 294916
  140.7 34.8 %all-to-all-start.3 = ((f32[128,24,128]{2,1,0:T(8,128)}), f32[128,24,128]{2,1,0:T(8,128)}, u32[]{:S(2)}, u32[]{:S(2)}) async-start(f32[128,24,128]{2,1,0:T(8,128)} %get-tuple-element.51), calls=%async_computation.3 | async-start | bytes 3145728 | tf_op jit(solution)/shard_map/all_to_all | solution.py:330
  151.7 34.8 %collective-permute-start.3 = (f32[2,32,8,512]{3,2,1,0:T(8,128)}, f32[2,32,8,512]{3,2,1,0:T(8,128)S(1)}, u32[]{:S(2)}, u32[]{:S(2)}) collective-permute-start(f32[2,32,8,512]{3,2,1,0:T(8,128)} %get-tuple-element.57), channel_id=1, source_target_pairs={{0,2},{2,0},{4,6},{6,4},{8,10},{10,8},{12,14},{14,12},{16,18},{18,... | collective-permute-start | bytes 3145736 | tf_op jit(solution)/shard_map/ppermute | solution.py:457
  185.0 1.5 copy-start.9
  185.0 3.0 %collective-permute-start.4 = (f32[2,32,8,512]{3,2,1,0:T(8,128)}, f32[2,32,8,512]{3,2,1,0:T(8,128)S(1)}, u32[]{:S(2)}, u32[]{:S(2)}) collective-permute-start(f32[2,32,8,512]{3,2,1,0:T(8,128)} %get-tuple-element.59), channel_id=1, source_target_pairs={{0,2},{2,0},{4,6},{6,4},{8,10},{10,8},{12,14},{14,12},{16,18},{18,... | collective-permute-start | bytes 3145736 | tf_op jit(solution)/shard_map/ppermute | solution.py:457
  186.5 1.5 copy-start.10
  188.2 10.9 %copy-start.4 = (bf16[8,512,128]{2,1,0:T(8,128)(2,1)S(1)}, bf16[8,512,128]{2,1,0:T(8,128)(2,1)}, u32[]{:S(2)}) copy-start(bf16[8,512,128]{2,1,0:T(8,128)(2,1)} %get-tuple-element.42.att_ref) | copy-start | bytes 3145732
  189.4 28.9 %all-to-all-start.4 = ((bf16[64,16,512]{2,1,0:T(8,128)(2,1)}), bf16[64,16,512]{2,1,0:T(8,128)(2,1)S(1)}, u32[]{:S(2)}, u32[]{:S(2)}) async-start(bf16[64,16,512]{2,1,0:T(8,128)(2,1)} %bitcast.93), calls=%async_computation.4 | async-start | bytes 2097152 | tf_op jit(solution)/shard_map/all_to_all | solution.py:500
  199.1 1.7 copy-start.6
  199.2 1.7 copy-start.7
  200.9 1.6 copy-start.14
